TPU v7x, 32 devices: a whole 2x2x4 slice. The times are simulated.
32 devices in a mesh: groups: 2 (over x), hid: 16 (over z, y, core).
Axes of the slice: x: 2, y: 2, z: 4, core: 2. Of those that a mesh axis runs over, the one named last changes fastest.
Arguments:
- tokens: bfloat16 [512, 6144], P('groups', 'hid'), parts along dimension 0, may hold values from -6 to 6
- upstream: bfloat16 [512, 6144], P('groups', 'hid'), parts along dimension 0, may hold values from -6 to 6
- loss_mask: int32 [512], P('groups'), parts along dimension 0, may hold values from 0 to 1, as said below
- gate_weight: bfloat16 [6144, 23552], P(None, 'hid'), may hold values from -0.109375 to 0.109375
- up_weight: bfloat16 [6144, 23552], P(None, 'hid'), may hold values from -0.109375 to 0.109375
- down_weight: bfloat16 [23552, 6144], P('hid'), may hold values from -0.0546875 to 0.0546875
Outputs:
- ffn_output: bfloat16 [512, 6144], P('groups', 'hid'), parts along dimension 0
- token_grad: bfloat16 [512, 6144], P('groups', 'hid'), parts along dimension 0
- gate_grad: bfloat16 [12288, 23552], P('groups', 'hid'), parts along dimension 0
- up_grad: bfloat16 [12288, 23552], P('groups', 'hid'), parts along dimension 0
- down_grad: bfloat16 [23552, 12288], P('hid', 'groups'), parts along dimension 1
There are 2 independent parts, one for each index of `groups`. A program takes and returns all parts, laid end to end along the dimension named above; an argument that names none is the same for every part. Nothing has to cross between parts.
Inputs may be any that keep to these rules, and one draw needn't show every extreme that they name: `loss_mask`: exactly 128 of the 256 tokens have mask 1.
All inputs are finite; a program needn't handle non-finite values.
Results may differ from a plain program's by a relative error of at most 0.005.
Values may be sent and summed in bfloat16 or wider, within the bound.
No kernel may reach another device: no remote copies, remote signals or barrier semaphores. Data moves between devices by JAX's collectives and lax.ppermute only.
A program may use at most 256 MiB of HBM per device.

v0:
```python
import jax
import jax.numpy as jnp
from jax import lax
from jax.sharding import PartitionSpec as P


def body(tokens, upstream, loss_mask, gate_weight, up_weight, down_weight):
    masked = upstream * loss_mask[:, None].astype(upstream.dtype)
    whole_tokens, whole_grad = (
        lax.all_gather(tokens, "hid", axis=1, tiled=True),
        lax.all_gather(masked, "hid", axis=1, tiled=True),
    )
    gate_lin = jnp.dot(whole_tokens, gate_weight, preferred_element_type=jnp.float32)
    up_lin = jnp.dot(whole_tokens, up_weight, preferred_element_type=jnp.float32)
    sigmoid_gate = jax.nn.sigmoid(gate_lin)
    activated = gate_lin * sigmoid_gate
    hidden = (activated * up_lin).astype(jnp.bfloat16)
    summed_out = lax.psum_scatter(
        lax.dot_general(
            down_weight, hidden, (((0,), (1,)), ((), ())), preferred_element_type=jnp.float32
        ),
        "hid",
        scatter_dimension=0,
        tiled=True,
    )
    ffn_output = summed_out.T.astype(jnp.bfloat16)
    d_hidden = lax.dot_general(
        whole_grad, down_weight, (((1,), (1,)), ((), ())), preferred_element_type=jnp.float32
    )
    d_up = (d_hidden * activated).astype(jnp.bfloat16)
    d_gate = (d_hidden * up_lin * sigmoid_gate * (1.0 + gate_lin * (1.0 - sigmoid_gate))).astype(
        jnp.bfloat16
    )
    down_grad = lax.dot_general(
        hidden, whole_grad, (((0,), (0,)), ((), ())), preferred_element_type=jnp.float32
    ).astype(jnp.bfloat16)
    gate_grad = lax.dot_general(
        whole_tokens, d_gate, (((0,), (0,)), ((), ())), preferred_element_type=jnp.float32
    ).astype(jnp.bfloat16)
    up_grad = lax.dot_general(
        whole_tokens, d_up, (((0,), (0,)), ((), ())), preferred_element_type=jnp.float32
    ).astype(jnp.bfloat16)
    first = lax.dot_general(
        gate_weight, d_gate, (((1,), (1,)), ((), ())), preferred_element_type=jnp.float32
    )
    second = lax.dot_general(
        up_weight, d_up, (((1,), (1,)), ((), ())), preferred_element_type=jnp.float32
    )
    summed_grad = lax.psum_scatter(first + second, "hid", scatter_dimension=0, tiled=True)
    grad_rows = summed_grad.T.astype(jnp.bfloat16)
    return (ffn_output, grad_rows, gate_grad, up_grad, down_grad)


def solution(mesh):
    in_specs = (
        P("groups", "hid"),
        P("groups", "hid"),
        P("groups"),
        P(None, "hid"),
        P(None, "hid"),
        P("hid", None),
    )
    out_specs = (
        P("groups", "hid"),
        P("groups", "hid"),
        P("groups", "hid"),
        P("groups", "hid"),
        P("hid", "groups"),
    )
    return jax.shard_map(body, mesh=mesh, in_specs=in_specs, out_specs=out_specs, check_vma=False)
```

profile of v0, /device:TPU:0, one launch (start us, length us, event | category | flops | bytes accessed | tf_op | source)
XLA Modules:
  0.0 326.8 jit_solution(13062746339680967557)
XLA Ops:
  7.2 0.0 all-gather.3.cloned.1.call-start
  7.2 0.7 all-gather.3.cloned.1.call-update
  7.9 0.0 all-gather.5.cloned.1.call-start
  7.9 0.7 convert_element_type.43
  8.6 1.7 broadcast_multiply_fusion
  10.3 0.0 all-gather.5.cloned.1.call-update
  10.4 0.0 reduce-scatter.5.cloned.1.call-start
  10.4 49.7 %all-gather.3.cloned.1.call-done = bf16[256,6144]{1,0:T(8,128)(2,1)} async-done(((bf16[256,384]{1,0:T(8,128)(2,1)}), bf16[256,6144]{1,0:T(8,128)(2,1)}) %all-gather.3.cloned.1.call-update) | async-done | bytes 3145744 | tf_op jit(solution)/shard_map/all_gather | solution.py:10
  60.1 13.4 %fusion.5 = f32[256,1472]{0,1:T(8,128)} fusion(bf16[256,6144]{1,0:T(8,128)(2,1)} %all-gather.3.cloned.1.call-done, bf16[6144,1472]{0,1:T(8,128)(2,1)} %param.10), kind=kOutput, calls=%fused_computation.17 | convolution fusion | flops 4630511616 | bytes 22740992 | tf_op jit(solution)/shard_map/dot_general | solution.py:14
  73.5 9.9 %fusion.4 = f32[256,1472]{0,1:T(8,128)} fusion(bf16[256,6144]{1,0:T(8,128)(2,1)S(1)} %copy-done, bf16[6144,1472]{0,1:T(8,128)(2,1)} %param.9), kind=kOutput, calls=%fused_computation.16 | convolution fusion | flops 4630511616 | bytes 22740992 | tf_op jit(solution)/shard_map/dot_general | solution.py:13
  83.4 24.9 %all-gather.5.cloned.1.call-done = bf16[256,6144]{1,0:T(8,128)(2,1)} async-done(((bf16[256,384]{1,0:T(8,128)(2,1)}), bf16[256,6144]{1,0:T(8,128)(2,1)}) %all-gather.5.cloned.1.call-update) | async-done | bytes 3145744 | tf_op jit(solution)/shard_map/all_gather | solution.py:11
  108.3 14.4 %multiply_convert_fusion = (bf16[256,1472]{0,1:T(8,128)(2,1)S(1)}, bf16[256,1472]{0,1:T(8,128)(2,1)S(1)}, bf16[256,1472]{0,1:T(8,128)(2,1)}) fusion(f32[256,1472]{0,1:T(8,128)} %fusion.4, f32[256,1472]{0,1:T(8,128)} %fusion.5, bf16[256,6144]{1,0:T(8,128)(2,1)} %all-gather.5.cloned.1.call-done, bf16[1472,6144]{1,0:T(8,128)(2,1)} %param.11), kind=kOutput, calls=%fused_computation.8 | convolution fusion | flops 4636164096 | bytes 26509312 | tf_op jit(solution)/shard_map/dot_general | solution.py:27
  122.7 9.7 %fusion.6 = f32[256,6144]{1,0:T(8,128)S(1)} fusion(bf16[256,1472]{0,1:T(8,128)(2,1)S(1)} %get-tuple-element.6, bf16[6144,1472]{0,1:T(8,128)(2,1)} %param.9), kind=kOutput, calls=%fused_computation.18 | convolution fusion | flops 4630511616 | bytes 25133056 | tf_op jit(solution)/shard_map/dot_general | solution.py:43
  132.4 13.8 %fusion.2 = f32[6144,256]{0,1:T(8,128)} fusion(f32[256,6144]{1,0:T(8,128)S(1)} %fusion.6, bf16[256,1472]{0,1:T(8,128)(2,1)S(1)} %get-tuple-element.5, bf16[6144,1472]{0,1:T(8,128)(2,1)} %param.10), kind=kOutput, calls=%fused_computation.7 | convolution fusion | flops 4632084480 | bytes 31424512 | tf_op jit(solution)/shard_map/dot_general | solution.py:46
  146.2 0.0 reduce-scatter.5.cloned.1.call-update
  146.3 0.0 reduce-scatter.3.cloned.1.call-start
  146.3 11.4 %convolution_bitcast_fusion = f32[6144,256]{0,1:T(8,128)} fusion(bf16[256,1472]{0,1:T(8,128)(2,1)} %get-tuple-element.7, bf16[1472,6144]{1,0:T(8,128)(2,1)} %param.11), kind=kOutput, calls=%fused_computation.6 | convolution fusion | flops 4630511616 | bytes 25133056 | tf_op jit(solution)/shard_map/dot_general | solution.py:19
  157.8 13.9 %convolution_convert_fusion = bf16[1472,6144]{1,0:T(8,128)(2,1)} fusion(bf16[256,1472]{0,1:T(8,128)(2,1)} %get-tuple-element.7, bf16[256,6144]{1,0:T(8,128)(2,1)} %all-gather.5.cloned.1.call-done), kind=kOutput, calls=%fused_computation | convolution fusion | flops 4639555584 | bytes 21987328 | tf_op jit(solution)/shard_map/dot_general | solution.py:34
  171.6 10.2 %fusion.1 = bf16[6144,1472]{0,1:T(8,128)(2,1)} fusion(bf16[256,1472]{0,1:T(8,128)(2,1)} %copy-done.2, bf16[256,6144]{1,0:T(8,128)(2,1)S(1)} %copy-done), kind=kOutput, calls=%fused_computation.4 | convolution fusion | flops 4639555584 | bytes 21987328 | tf_op jit(solution)/shard_map/dot_general | solution.py:40
  181.9 10.2 %fusion = bf16[6144,1472]{0,1:T(8,128)(2,1)} fusion(bf16[256,1472]{0,1:T(8,128)(2,1)} %copy-done.1, bf16[256,6144]{1,0:T(8,128)(2,1)S(1)} %copy-done), kind=kOutput, calls=%fused_computation.3 | convolution fusion | flops 4639555584 | bytes 21987328 | tf_op jit(solution)/shard_map/dot_general | solution.py:37
  192.1 37.7 %reduce-scatter.5.cloned.1.call-done = f32[384,256]{0,1:T(8,128)} async-done(((f32[6144,256]{0,1:T(8,128)}), f32[384,256]{0,1:T(8,128)}) %reduce-scatter.5.cloned.1.call-update) | async-done | bytes 393232 | tf_op jit(solution)/shard_map/reduce_scatter | solution.py:49
  229.8 1.7 convert_bitcast_fusion
  231.5 87.0 %reduce-scatter.3.cloned.1.call-done = f32[384,256]{0,1:T(8,128)} async-done(((f32[6144,256]{0,1:T(8,128)}), f32[384,256]{0,1:T(8,128)}) %reduce-scatter.3.cloned.1.call-update) | async-done | bytes 393232 | tf_op jit(solution)/shard_map/reduce_scatter | solution.py:18
  318.6 1.7 convert_bitcast_fusion.1
  (7 shorter events, 0.0 us)
Async XLA Ops:
  7.2 52.9 %all-gather.3.cloned.1.call-start = ((), (), s32[]{:S(2)}) async-start(), calls=%async_computation.2 | async-start | bytes 3342336 | tf_op jit(solution)/shard_map/all_gather | solution.py:10
  7.9 100.4 %all-gather.5.cloned.1.call-start = ((), (), s32[]{:S(2)}) async-start(), calls=%async_computation.4 | async-start | bytes 3342336 | tf_op jit(solution)/shard_map/all_gather | solution.py:11
  10.4 219.5 %reduce-scatter.5.cloned.1.call-start = ((), (), s32[]{:S(2)}) async-start(), calls=%async_computation.5 | async-start | bytes 6684672 | tf_op jit(solution)/shard_map/reduce_scatter | solution.py:49
  60.1 13.4 %copy-start = (bf16[256,6144]{1,0:T(8,128)(2,1)S(1)}, bf16[256,6144]{1,0:T(8,128)(2,1)}, u32[]{:S(2)}) copy-start(bf16[256,6144]{1,0:T(8,128)(2,1)} %all-gather.3.cloned.1.call-done) | copy-start | bytes 9437188
  122.7 9.7 %copy-start.1 = (bf16[256,1472]{0,1:T(8,128)(2,1)}, bf16[256,1472]{0,1:T(8,128)(2,1)S(1)}, u32[]{:S(2)}) copy-start(bf16[256,1472]{0,1:T(8,128)(2,1)S(1)} %get-tuple-element.6) | copy-start | bytes 2260996
  122.7 9.7 %copy-start.2 = (bf16[256,1472]{0,1:T(8,128)(2,1)}, bf16[256,1472]{0,1:T(8,128)(2,1)S(1)}, u32[]{:S(2)}) copy-start(bf16[256,1472]{0,1:T(8,128)(2,1)S(1)} %get-tuple-element.5) | copy-start | bytes 2260996
  146.3 172.3 %reduce-scatter.3.cloned.1.call-start = ((), (), s32[]{:S(2)}) async-start(), calls=%async_computation.3 | async-start | bytes 6684672 | tf_op jit(solution)/shard_map/reduce_scatter | solution.py:18
Sparse Core Ops, SparseCore 0:
  10.2 49.9 all-gather.2
  62.9 45.3 all-gather.4
  146.4 83.4 reduce-scatter.4
  234.2 84.3 reduce-scatter.2
where the time goes:
time: 327 us
  waiting for transfers between devices  200 us (61%)
  matrix products  107 us (33%)
  between operations  13.8 us (4%)
  other arithmetic  5.78 us (2%)
    reduce_scatter x1, waiting for transfers between devices, body(): lax.psum_scatter(lax.dot_general(down_weight, hidden, (((0,), (1,)), ((),...  87 us
    all_gather x1, waiting for transfers between devices, body(): lax.all_gather(tokens, 'hid', axis=1, tiled=True)  49.7 us
    reduce_scatter x1, waiting for transfers between devices, body(): lax.psum_scatter(first + second, 'hid', scatter_dimension=0, tiled=True)  37.7 us
    all_gather x1, waiting for transfers between devices, body(): lax.all_gather(masked, 'hid', axis=1, tiled=True)  24.9 us
    dot_general x1, matrix products, body(): lax.dot_general(whole_grad, down_weight, (((1,), (1,)), ((), ())), prefer...  14.4 us
    dot_general x1, matrix products, body(): lax.dot_general(hidden, whole_grad, (((0,), (0,)), ((), ())), preferred_e...  13.9 us
    dot_general x1, matrix products, body(): lax.dot_general(up_weight, d_up, (((1,), (1,)), ((), ())), preferred_elem...  13.8 us
    dot_general x1, matrix products, body(): jnp.dot(whole_tokens, up_weight, preferred_element_type=jnp.float32)  13.4 us
  transfers between devices with their start and end apart: 4, of which 4 were waited for; matrix products, arithmetic and copies ran while one was open for 22% of the time, Pallas kernels for 0%

commit v1 on v0

v1 whole, which is shorter than its diff:
```python
import functools

import jax
import jax.numpy as jnp
from jax import lax
from jax.experimental import pallas as pl
from jax.experimental.pallas import tpu as pltpu
from jax.sharding import PartitionSpec as P

F32 = jnp.float32
BF16 = jnp.bfloat16
VMEM_BYTES = 48 * 1024 * 1024


def dot(a, b, ca, cb):
    return lax.dot_general(a, b, (((ca,), (cb,)), ((), ())), preferred_element_type=F32)


def params():
    return pltpu.CompilerParams(vmem_limit_bytes=VMEM_BYTES)


def order_kernel(mask_ref, tokens_ref, upstream_ref, one_hot_ref, tokens_out, grad_out):
    tok = tokens_ref.shape[0]
    live = grad_out.shape[1]
    mask = mask_ref[...].astype(F32)
    before = lax.broadcasted_iota(jnp.int32, (tok, tok), 0) < lax.broadcasted_iota(jnp.int32, (tok, tok), 1)
    rank = dot(jnp.broadcast_to(mask, (8, tok)).astype(BF16), before.astype(F32).astype(BF16), 1, 0)[:1]
    column = lax.broadcasted_iota(jnp.int32, (1, tok), 1).astype(F32)
    place = jnp.where(mask > 0, rank, live + column - rank)
    row = lax.broadcasted_iota(jnp.int32, (tok, tok), 0).astype(F32)
    one_hot = (row == place).astype(F32).astype(BF16)
    one_hot_ref[...] = one_hot
    tokens_out[...] = dot(tokens_ref[...], one_hot, 0, 1).astype(BF16)
    grad_out[...] = dot(upstream_ref[...], one_hot[:live], 0, 1).astype(BF16)


def order_tokens(tokens, upstream, loss_mask, live):
    tok, width = tokens.shape

    def whole(*shape):
        return pl.BlockSpec(shape, lambda i: (0, 0))

    return pl.pallas_call(
        order_kernel,
        grid=(1,),
        in_specs=[whole(1, tok), whole(tok, width), whole(tok, width)],
        out_specs=[whole(tok, tok), whole(width, tok), whole(width, live)],
        out_shape=(
            jax.ShapeDtypeStruct((tok, tok), BF16),
            jax.ShapeDtypeStruct((width, tok), BF16),
            jax.ShapeDtypeStruct((width, live), BF16),
        ),
        compiler_params=params(),
        name="order_tokens",
    )(loss_mask.reshape(1, tok), tokens, upstream)


def pair_of(mine, other, core):
    return jnp.concatenate([jnp.where(core == 0, mine, other), jnp.where(core == 0, other, mine)], axis=0)


def forward_first_kernel(where_ref, mine, other, gate_w, up_w, gate_acc, up_acc):
    x = pair_of(mine[0], other[0], where_ref[0])

    @pl.when(pl.program_id(0) == 0)
    def _():
        gate_acc[...] = dot(gate_w[...], x, 1, 0)
        up_acc[...] = dot(up_w[...], x, 1, 0)

    @pl.when(pl.program_id(0) > 0)
    def _():
        gate_acc[...] += dot(gate_w[...], x, 1, 0)
        up_acc[...] += dot(up_w[...], x, 1, 0)


def forward_rest_kernel(
    live, where_ref, mine, other, gate_w, up_w, gate_in, up_in, hidden_ref, hidden_t_ref, act_ref, slope_ref, gate_acc, up_acc
):
    x = pair_of(mine[0], other[0], where_ref[0])

    @pl.when(pl.program_id(0) == 0)
    def _():
        gate_acc[...] = gate_in[...] + dot(gate_w[...], x, 1, 0)
        up_acc[...] = up_in[...] + dot(up_w[...], x, 1, 0)

    @pl.when(pl.program_id(0) > 0)
    def _():
        gate_acc[...] += dot(gate_w[...], x, 1, 0)
        up_acc[...] += dot(up_w[...], x, 1, 0)

    @pl.when(pl.program_id(0) == pl.num_programs(0) - 1)
    def _():
        gate_lin = gate_acc[...]
        up_lin = up_acc[...]
        sig = jax.nn.sigmoid(gate_lin)
        act = gate_lin * sig
        hidden = (act * up_lin).astype(BF16)
        hidden_ref[...] = hidden.T
        hidden_t_ref[...] = hidden[:, :live]
        act_ref[...] = act[:, :live]
        slope_ref[...] = (up_lin * sig * (1.0 + gate_lin * (1.0 - sig)))[:, :live]


def whole(*shape):
    return pl.BlockSpec(shape, lambda j, s: (0, 0))


def stacked(*shape):
    return pl.BlockSpec((1, *shape), lambda j, s: (j, 0, 0))


def columns(ff, width):
    return pl.BlockSpec((ff, 2 * width), lambda j, s: (0, s[1 + j]))


def call(kernel, name, where, operands, in_specs, outs, out_specs, flops, nbytes, scratch=()):
    return pl.pallas_call(
        kernel,
        grid_spec=pltpu.PrefetchScalarGridSpec(
            num_scalar_prefetch=1,
            grid=(where.shape[0] - 1,),
            in_specs=in_specs,
            out_specs=out_specs,
            scratch_shapes=scratch,
        ),
        out_shape=[jax.ShapeDtypeStruct(shape, kind) for shape, kind in outs],
        compiler_params=params(),
        cost_estimate=pl.CostEstimate(flops=flops, bytes_accessed=nbytes, transcendentals=0),
        name=name,
    )(where, *operands)


def forward_first(where, mine, other, gate_w, up_w):
    steps, width, tok = mine.shape
    ff = gate_w.shape[0]
    return call(
        forward_first_kernel,
        "forward_first",
        where,
        (mine, other, gate_w, up_w),
        [stacked(width, tok), stacked(width, tok), columns(ff, width), columns(ff, width)],
        [((ff, tok), F32), ((ff, tok), F32)],
        [whole(ff, tok), whole(ff, tok)],
        8 * steps * width * ff * tok,
        8 * steps * width * ff,
    )


def forward_rest(where, mine, other, gate_w, up_w, gate_acc, up_acc, live):
    steps, width, tok = mine.shape
    ff = gate_w.shape[0]
    return call(
        functools.partial(forward_rest_kernel, live),
        "forward_rest",
        where,
        (mine, other, gate_w, up_w, gate_acc, up_acc),
        [
            stacked(width, tok),
            stacked(width, tok),
            columns(ff, width),
            columns(ff, width),
            whole(ff, tok),
            whole(ff, tok),
        ],
        [((tok, ff), BF16), ((ff, live), BF16), ((ff, live), F32), ((ff, live), F32)],
        [whole(tok, ff), whole(ff, live), whole(ff, live), whole(ff, live)],
        8 * steps * width * ff * tok,
        8 * steps * width * ff,
        [pltpu.VMEM((ff, tok), F32), pltpu.VMEM((ff, tok), F32)],
    )


def down_kernel(
    where_ref, hidden, act, slope, mine, other, down_w, keep_ref, send_ref, d_gate_ref, d_up_ref, d_gate_t_ref, d_up_t_ref, d_hidden
):
    core = where_ref[0]
    w = down_w[...]
    width = mine.shape[1]
    out = dot(hidden[...], w, 1, 0)
    low, high = out[:, :width], out[:, width:]
    keep_ref[0] = jnp.where(core == 0, low, high)
    send_ref[0] = jnp.where(core == 0, high, low).astype(BF16)
    part = dot(w, pair_of(mine[0], other[0], core), 1, 0)

    @pl.when(pl.program_id(0) == 0)
    def _():
        d_hidden[...] = part

    @pl.when(pl.program_id(0) > 0)
    def _():
        d_hidden[...] += part

    @pl.when(pl.program_id(0) == pl.num_programs(0) - 1)
    def _():
        d_up = (d_hidden[...] * act[...]).astype(BF16)
        d_gate = (d_hidden[...] * slope[...]).astype(BF16)
        d_up_t_ref[...] = d_up
        d_gate_t_ref[...] = d_gate
        d_up_ref[...] = d_up.T
        d_gate_ref[...] = d_gate.T


def down(where, hidden, act, slope, mine, other, down_w):
    steps, width, live = mine.shape
    tok, ff = hidden.shape
    return call(
        down_kernel,
        "down",
        where,
        (hidden, act, slope, mine, other, down_w),
        [whole(tok, ff), whole(ff, live), whole(ff, live), stacked(width, live), stacked(width, live), columns(ff, width)],
        [((steps, tok, width), F32), ((steps, tok, width), BF16)] + 2 * [((live, ff), BF16)] + 2 * [((ff, live), BF16)],
        [stacked(tok, width), stacked(tok, width), whole(live, ff), whole(live, ff), whole(ff, live), whole(ff, live)],
        2 * (tok + live) * down_w.size,
        2 * down_w.size,
        [pltpu.VMEM((ff, live), F32)],
    )


def token_grad_kernel(where_ref, d_gate, d_up, gate_w, up_w, keep_ref, send_ref):
    core = where_ref[0]
    width = keep_ref.shape[2]
    out = dot(d_gate[...], gate_w[...], 1, 0) + dot(d_up[...], up_w[...], 1, 0)
    low, high = out[:, :width], out[:, width:]
    keep_ref[0] = jnp.where(core == 0, low, high)
    send_ref[0] = jnp.where(core == 0, high, low).astype(BF16)


def token_grad_parts(where, d_gate, d_up, gate_w, up_w, width):
    live, ff = d_gate.shape
    steps = where.shape[0] - 1
    return call(
        token_grad_kernel,
        "token_grad_parts",
        where,
        (d_gate, d_up, gate_w, up_w),
        [whole(live, ff), whole(live, ff), columns(ff, width), columns(ff, width)],
        [((steps, live, width), F32), ((steps, live, width), BF16)],
        [stacked(live, width), stacked(live, width)],
        8 * live * steps * ff * width,
        8 * steps * ff * width,
    )


def weight_grad_kernel(where_ref, hid, mine, other, out_ref):
    x = pair_of(mine[0], other[0], where_ref[0])
    out_ref[...] = dot(hid[...], x, 1, 1).astype(BF16)


def weight_grad(where, hid, mine, other, name):
    steps, width, _ = mine.shape
    ff, live = hid.shape
    return call(
        weight_grad_kernel,
        name,
        where,
        (hid, mine, other),
        [whole(ff, live), stacked(width, live), stacked(width, live)],
        [((ff, 2 * steps * width), BF16)],
        [columns(ff, width)],
        4 * live * ff * steps * width,
        4 * ff * steps * width,
    )[0]


def last_kernel(one_hot, *refs):
    total = refs[0][...].astype(F32)
    for part in refs[1:-1]:
        total = total + part[...].astype(F32)
    refs[-1][...] = dot(one_hot[...], total.astype(BF16), 0, 0).astype(BF16)


def last_sum(one_hot, parts, name):
    rows, tok = one_hot.shape
    return pl.pallas_call(
        last_kernel,
        out_shape=jax.ShapeDtypeStruct((tok, parts[0].shape[1]), BF16),
        compiler_params=params(),
        name=name,
    )(one_hot, *parts)


def flip(x, bits):
    return lax.ppermute(x, "hid", [(i, i ^ bits) for i in range(16)])


def gather(x):
    z2 = flip(x, 8)
    z1 = flip(x, 4)
    y = flip(x, 2)
    z3 = flip(z2, 4)
    first = jnp.stack([x, y, z1, flip(z1, 2)])
    rest = jnp.stack([z2, flip(z2, 2), z3, flip(z3, 2)])
    return first, flip(first, 1), rest, flip(rest, 1)


def scatter_sum(keep, send):
    recv = flip(send, 1)
    pair = keep + recv.astype(F32)
    row = [None] * 4
    for k in (3, 2, 1, 0):
        row[k] = pair[2 * k] + flip(pair[2 * k + 1].astype(BF16), 2).astype(F32)
    two = row[2] + flip(row[3].astype(BF16), 4).astype(F32)
    return row[0], flip(two.astype(BF16), 8), flip(row[1].astype(BF16), 4)


def body16(tokens, upstream, loss_mask, gate_weight, up_weight, down_weight):
    live = tokens.shape[0] // 2
    width = tokens.shape[1]
    me = lax.axis_index("hid")
    chips = (me // 2) ^ jnp.arange(8)
    where = jnp.concatenate([(me % 2)[None], chips]).astype(jnp.int32)
    where_first, where_rest = where[:5], jnp.concatenate([where[:1], where[5:]])
    gate_w, up_w = gate_weight.T, up_weight.T
    one_hot, tokens, grad = order_tokens(tokens, upstream, loss_mask, live)
    x_first, x_first_other, x_rest, x_rest_other = gather(tokens)
    g_first, g_first_other, g_rest, g_rest_other = gather(grad)
    acc = forward_first(where_first, x_first, x_first_other, gate_w, up_w)
    hidden, hidden_t, act, slope = forward_rest(where_rest, x_rest, x_rest_other, gate_w, up_w, *acc, live)
    x_mine, x_other = jnp.concatenate([x_first, x_rest]), jnp.concatenate([x_first_other, x_rest_other])
    g_mine, g_other = jnp.concatenate([g_first, g_rest]), jnp.concatenate([g_first_other, g_rest_other])
    out_keep, out_send, d_gate, d_up, d_gate_t, d_up_t = down(where, hidden, act, slope, g_mine, g_other, down_weight)
    out_parts = scatter_sum(out_keep, out_send)
    tg_keep, tg_send = token_grad_parts(where, d_gate, d_up, gate_w, up_w, width)
    tg_parts = scatter_sum(tg_keep, tg_send)
    down_grad = weight_grad(where, hidden_t, g_mine, g_other, "down_grad")
    gate_grad = weight_grad(where, d_gate_t, x_mine, x_other, "gate_grad").T
    up_grad = weight_grad(where, d_up_t, x_mine, x_other, "up_grad").T
    ffn_output = last_sum(one_hot, out_parts, "ffn_output")
    token_grad = last_sum(one_hot[:live], tg_parts, "token_grad")
    return ffn_output, token_grad, gate_grad, up_grad, down_grad


def body_any(tokens, upstream, loss_mask, gate_weight, up_weight, down_weight):
    masked = upstream * loss_mask[:, None].astype(upstream.dtype)
    tokens = lax.all_gather(tokens, "hid", axis=1, tiled=True)
    grad = lax.all_gather(masked, "hid", axis=1, tiled=True)
    gate_lin = dot(tokens, gate_weight, 1, 0)
    up_lin = dot(tokens, up_weight, 1, 0)
    sig = jax.nn.sigmoid(gate_lin)
    act = gate_lin * sig
    hidden = (act * up_lin).astype(BF16)
    out = lax.psum_scatter(dot(down_weight, hidden, 0, 1), "hid", scatter_dimension=0, tiled=True)
    d_hidden = dot(grad, down_weight, 1, 1)
    d_up = (d_hidden * act).astype(BF16)
    d_gate = (d_hidden * up_lin * sig * (1.0 + gate_lin * (1.0 - sig))).astype(BF16)
    down_grad = dot(hidden, grad, 0, 0).astype(BF16)
    gate_grad = dot(tokens, d_gate, 0, 0).astype(BF16)
    up_grad = dot(tokens, d_up, 0, 0).astype(BF16)
    back = dot(gate_weight, d_gate, 1, 1) + dot(up_weight, d_up, 1, 1)
    back = lax.psum_scatter(back, "hid", scatter_dimension=0, tiled=True)
    return out.T.astype(BF16), back.T.astype(BF16), gate_grad, up_grad, down_grad


def solution(mesh):
    spec = P("groups", "hid")
    in_specs = (spec, spec, P("groups"), P(None, "hid"), P(None, "hid"), P("hid", None))
    out_specs = (spec, spec, spec, spec, P("hid", "groups"))
    body = body16 if mesh.shape["hid"] == 16 else body_any
    return jax.shard_map(body, mesh=mesh, in_specs=in_specs, out_specs=out_specs, check_vma=False)
```

time: 327 us -> 172 us (0.53)
  waiting for transfers between devices: 200 us -> 45.1 us
  matrix products: 107 us -> 0 us
  Pallas kernels: 0 us -> 84.5 us
  starting transfers between devices: 0.16 us -> 33.8 us
  between operations: 13.8 us -> 1.02 us
  local copies, waits for them, and re-layouts: 0.01 us -> 5.17 us
  other arithmetic: 5.78 us -> 2.43 us
    reduce_scatter x2 -> x0, waiting for transfers between devices: 125 us -> none  [the longest x1 87 us: body(): lax.psum_scatter(lax.dot_general(down_weight, hidden, (((0,), (1,)), ((),...]
    dot_general x9 -> x0, matrix products: 107 us -> none  [the longest x1 14.4 us: body(): lax.dot_general(whole_grad, down_weight, (((1,), (1,)), ((), ())), prefer...]
    pallas_call x0 -> x10, Pallas kernels: none -> 84.5 us  [the longest x7 82.2 us: call(): pl.pallas_call(kernel, grid_spec=pltpu.PrefetchScalarGridSpec(num_scalar_...]
    all_gather x2 -> x0, waiting for transfers between devices: 74.6 us -> none  [the longest x1 49.7 us: body(): lax.all_gather(tokens, 'hid', axis=1, tiled=True)]
    ppermute x0 -> x34, waiting for transfers between devices: none -> 45.1 us  [flip(): return lax.ppermute(x, 'hid', [(i, i ^ bits) for i in range(16)])]
    ppermute x0 -> x34, starting transfers between devices: none -> 33.8 us  [flip(): return lax.ppermute(x, 'hid', [(i, i ^ bits) for i in range(16)])]
    unnamed x6 -> x26, local copies, waits for them, and re-layouts: 0.01 us -> 4.83 us
    convert_element_type x3 -> x4, other arithmetic: 4.07 us -> 0.3 us  [scatter_sum(): return (row[0], flip(two.astype(BF16), 8), flip(row[1].astype(BF16), 4))]
  transfers between devices with their start and end apart: 4 -> 34, of which waited for: 4 -> 11; matrix products, arithmetic and copies ran while one was open for 22% -> 2% of each run, Pallas kernels for 0% -> 33%
where the time goes in v1:
time: 172 us
  Pallas kernels  84.5 us (49%)
  waiting for transfers between devices  45.1 us (26%)
  starting transfers between devices  33.8 us (20%)
  local copies, waits for them, and re-layouts  5.17 us (3%)
  other arithmetic  2.43 us (1%)
    pallas_call x7, Pallas kernels, call(): pl.pallas_call(kernel, grid_spec=pltpu.PrefetchScalarGridSpec(num_scalar_...  82.2 us
    ppermute x34, waiting for transfers between devices, flip(): return lax.ppermute(x, 'hid', [(i, i ^ bits) for i in range(16)])  45.1 us
    ppermute x34, starting transfers between devices, flip(): return lax.ppermute(x, 'hid', [(i, i ^ bits) for i in range(16)])  33.8 us
    unnamed x26, local copies, waits for them, and re-layouts  4.83 us
  transfers between devices with their start and end apart: 34, of which 11 were waited for; matrix products, arithmetic and copies ran while one was open for 2% of the time, Pallas kernels for 33%

profile of v1, /device:TPU:0, one launch (start us, length us, event | category | flops | bytes accessed | tf_op | source)
XLA Modules:
  0.0 172.0 jit_solution(2066186633179158383)
XLA Ops:
  3.6 4.1 %collective-permute-start = (bf16[384,256]{1,0:T(8,128)(2,1)S(1)}, bf16[384,256]{1,0:T(8,128)(2,1)S(1)}, u32[]{:S(2)}, u32[]{:S(2)}) collective-permute-start(bf16[384,256]{1,0:T(8,128)(2,1)S(1)} %get-tuple-element.23), channel_id=1, source_target_pairs={{0,8},{1,9},{2,10},{3,11},{4,12},{5,13},{6,14},{7,15},{8,0},{9,1},... | collective-permute-start | bytes 589832 | tf_op jit(solution)/shard_map/ppermute | solution.py:285
  7.7 1.6 collective-permute-start.6
  9.3 1.5 collective-permute-start.5
  12.1 5.4 %collective-permute-done.9 = bf16[384,128]{1,0:T(8,128)(2,1)S(1)} collective-permute-done((bf16[384,128]{1,0:T(8,128)(2,1)S(1)}, bf16[384,128]{1,0:T(8,128)(2,1)S(1)}, u32[]{:S(2)}, u32[]{:S(2)}) %collective-permute-start.9) | collective-permute-done | bytes 98336 | tf_op jit(solution)/shard_map/ppermute | solution.py:285
  17.8 1.5 collective-permute-done.10
  19.3 1.6 collective-permute-start.11
  21.8 2.1 %collective-permute-done.12 = bf16[384,128]{1,0:T(8,128)(2,1)S(1)} collective-permute-done((bf16[384,128]{1,0:T(8,128)(2,1)S(1)}, bf16[384,128]{1,0:T(8,128)(2,1)S(1)}, u32[]{:S(2)}, u32[]{:S(2)}) %collective-permute-start.12) | collective-permute-done | bytes 98336 | tf_op jit(solution)/shard_map/ppermute | solution.py:285
  23.9 1.5 collective-permute-start.13
  29.5 1.3 collective-permute-start.7
  31.7 10.3 %collective-permute-done.15 = bf16[384,128]{1,0:T(8,128)(2,1)S(1)} collective-permute-done((bf16[384,128]{1,0:T(8,128)(2,1)S(1)}, bf16[384,128]{1,0:T(8,128)(2,1)S(1)}, u32[]{:S(2)}, u32[]{:S(2)}) %collective-permute-start.15) | collective-permute-done | bytes 98336 | tf_op jit(solution)/shard_map/ppermute | solution.py:285
  43.9 5.8 %collective-permute-done.3 = bf16[384,256]{1,0:T(8,128)(2,1)S(1)} collective-permute-done((bf16[384,256]{1,0:T(8,128)(2,1)S(1)}, bf16[384,256]{1,0:T(8,128)(2,1)S(1)}, u32[]{:S(2)}, u32[]{:S(2)}) %collective-permute-start.3) | collective-permute-done | bytes 196640 | tf_op jit(solution)/shard_map/ppermute | solution.py:285
  50.1 10.0 %forward_first.1 = (f32[1472,256]{1,0:T(8,128)S(1)}, f32[1472,256]{1,0:T(8,128)S(1)}) custom-call(s32[5]{0:T(128)S(1)} %bitcast.105, bf16[4,384,256]{2,1,0:T(8,128)(2,1)S(1)} %pad_maximum_fusion.1.mine, bf16[4,384,256]{2,1,0:T(8,128)(2,1)S(1)} %collective-permute-done.8.other, bf16[1472,6144]{1,0:T(8,128)(2,1)} %bitcast.107, bf16[1472,6144]{1,0:T(8,128)(2,1)} %bitcast.110), custom_call_target="tpu_custom_call" | custom-call | flops 4630511616 | bytes 18087936 | tf_op jit(solution)/shard_map/forward_first/pallas_call | solution.py:118
  61.2 10.7 %forward_rest.1 = (bf16[256,1472]{1,0:T(8,128)(2,1)S(1)}, bf16[1472,128]{1,0:T(8,128)(2,1)S(1)}, f32[1472,128]{1,0:T(8,128)S(1)}, f32[1472,128]{1,0:T(8,128)S(1)}) custom-call(s32[5]{0:T(128)S(1)} %pad_add_fusion.1.where_ref, bf16[4,384,256]{2,1,0:T(8,128)(2,1)S(1)} %pad_maximum_fusion.mine, bf16[4,384,256]{2,1,0:T(8,128)(2,1)S(1)} %collective-permute-done.4.other, ...), custom_call_target="tpu_custom_call" | custom-call | flops 4630511616 | bytes 18087936 | tf_op jit(solution)/shard_map/forward_rest/pallas_call | solution.py:118
  71.9 16.4 %down.1 = (f32[8,256,384]{2,1,0:T(8,128)}, bf16[8,256,384]{2,1,0:T(8,128)(2,1)}, bf16[128,1472]{1,0:T(8,128)(2,1)S(1)}, bf16[128,1472]{1,0:T(8,128)(2,1)S(1)}, b...) custom-call(s32[9]{0:T(128)S(1)} %pad_add_fusion.where_ref, bf16[256,1472]{1,0:T(8,128)(2,1)S(1)} %get-tuple-element.26.hidden, ...), custom_call_target="tpu_custom_call" | custom-call | flops 6945767424 | bytes 18087936 | tf_op jit(solution)/shard_map/down/pallas_call | solution.py:118
  88.8 15.0 %token_grad_parts.1 = (f32[8,128,384]{2,1,0:T(8,128)S(1)}, bf16[8,128,384]{2,1,0:T(8,128)(2,1)S(1)}) custom-call(s32[9]{0:T(128)S(1)} %pad_add_fusion.where_ref, bf16[128,1472]{1,0:T(8,128)(2,1)S(1)} %get-tuple-element.32.d_gate, bf16[128,1472]{1,0:T(8,128)(2,1)S(1)} %get-tuple-element.33.d_up, bf16[1472,6144]{1,0:T(8,128)(2,1)} %bitcast.109, ...), custom_call_target="tpu_custom_call" | custom-call | flops 4630511616 | bytes 36175872 | tf_op jit(solution)/shard_map/token_grad_parts/pallas_call | solution.py:118
  104.1 10.1 %gate_grad.1 = bf16[1472,6144]{1,0:T(8,128)(2,1)} custom-call(s32[9]{0:T(128)S(1)} %pad_add_fusion.where_ref, bf16[1472,128]{1,0:T(8,128)(2,1)S(1)} %get-tuple-element.36.hid, bf16[8,384,256]{2,1,0:T(8,128)(2,1)S(1)} %constant_dynamic-update-slice_fusion.10.mine, bf16[8,384,256]{2,1,0:T(8,128)(2,1)S(1)} %constant_dynamic-update-slice_fusion.18.other), custom_call_target="tpu_custom_call" | custom-call | flops 2315255808 | bytes 18087936 | tf_op jit(solution)/shard_map/gate_grad/pallas_call | solution.py:118
  114.2 10.1 %up_grad.1 = bf16[1472,6144]{1,0:T(8,128)(2,1)} custom-call(s32[9]{0:T(128)S(1)} %pad_add_fusion.where_ref, bf16[1472,128]{1,0:T(8,128)(2,1)S(1)} %get-tuple-element.37.hid, bf16[8,384,256]{2,1,0:T(8,128)(2,1)S(1)} %constant_dynamic-update-slice_fusion.10.mine, bf16[8,384,256]{2,1,0:T(8,128)(2,1)S(1)} %constant_dynamic-update-slice_fusion.18.other), custom_call_target="tpu_custom_call" | custom-call | flops 2315255808 | bytes 18087936 | tf_op jit(solution)/shard_map/up_grad/pallas_call | solution.py:118
  134.5 1.3 collective-permute-start.30
  135.8 4.9 %collective-permute-done.24 = bf16[256,384]{1,0:T(8,128)(2,1)S(1)} collective-permute-done((bf16[256,384]{1,0:T(8,128)(2,1)S(1)}, bf16[256,384]{1,0:T(8,128)(2,1)S(1)}, u32[]{:S(2)}, u32[]{:S(2)}) %collective-permute-start.24) | collective-permute-done | bytes 196640 | tf_op jit(solution)/shard_map/ppermute | solution.py:285
  142.0 3.0 %collective-permute-done.21 = bf16[256,384]{1,0:T(8,128)(2,1)S(1)} collective-permute-done((bf16[256,384]{1,0:T(8,128)(2,1)S(1)}, bf16[256,384]{1,0:T(8,128)(2,1)S(1)}, u32[]{:S(2)}, u32[]{:S(2)}) %collective-permute-start.21) | collective-permute-done | bytes 196640 | tf_op jit(solution)/shard_map/ppermute | solution.py:285
  146.0 3.2 %collective-permute-done.19 = bf16[256,384]{1,0:T(8,128)(2,1)S(1)} collective-permute-done((bf16[256,384]{1,0:T(8,128)(2,1)S(1)}, bf16[256,384]{1,0:T(8,128)(2,1)S(1)}, u32[]{:S(2)}, u32[]{:S(2)}) %collective-permute-start.19) | collective-permute-done | bytes 196640 | tf_op jit(solution)/shard_map/ppermute | solution.py:285
  150.6 2.3 %collective-permute-start.31 = (bf16[128,384]{1,0:T(8,128)(2,1)S(1)}, bf16[128,384]{1,0:T(8,128)(2,1)S(1)}, u32[]{:S(2)}, u32[]{:S(2)}) collective-permute-start(bf16[128,384]{1,0:T(8,128)(2,1)S(1)} %fusion.14), channel_id=1, source_target_pairs={{0,8},{1,9},{2,10},{3,11},{4,12},{5,13},{6,14},{7,15},{8,0},{9,1},... | collective-permute-start | bytes 294920 | tf_op jit(solution)/shard_map/ppermute | solution.py:285
  153.2 6.8 %collective-permute-done.22 = bf16[256,384]{1,0:T(8,128)(2,1)S(1)} collective-permute-done((bf16[256,384]{1,0:T(8,128)(2,1)S(1)}, bf16[256,384]{1,0:T(8,128)(2,1)S(1)}, u32[]{:S(2)}, u32[]{:S(2)}) %collective-permute-start.22) | collective-permute-done | bytes 196640 | tf_op jit(solution)/shard_map/ppermute | solution.py:285
  160.2 9.9 %down_grad.1 = bf16[1472,6144]{1,0:T(8,128)(2,1)} custom-call(s32[9]{0:T(128)S(1)} %pad_add_fusion.where_ref, bf16[1472,128]{1,0:T(8,128)(2,1)S(1)} %get-tuple-element.38.hid, bf16[8,384,128]{2,1,0:T(8,128)(2,1)S(1)} %constant_dynamic-update-slice_fusion.mine, bf16[8,384,128]{2,1,0:T(8,128)(2,1)S(1)} %constant_dynamic-update-slice_fusion.8.other), custom_call_target="tpu_custom_call" | custom-call | flops 2315255808 | bytes 18087936 | tf_op jit(solution)/shard_map/down_grad/pallas_call | solution.py:118
  (101 shorter events, 30.5 us)
Async XLA Ops:
  3.6 24.0 %collective-permute-start = (bf16[384,256]{1,0:T(8,128)(2,1)S(1)}, bf16[384,256]{1,0:T(8,128)(2,1)S(1)}, u32[]{:S(2)}, u32[]{:S(2)}) collective-permute-start(bf16[384,256]{1,0:T(8,128)(2,1)S(1)} %get-tuple-element.23), channel_id=1, source_target_pairs={{0,8},{1,9},{2,10},{3,11},{4,12},{5,13},{6,14},{7,15},{8,0},{9,1},... | collective-permute-start | bytes 589832 | tf_op jit(solution)/shard_map/ppermute | solution.py:285
  7.7 20.9 %collective-permute-start.6 = (bf16[384,256]{1,0:T(8,128)(2,1)S(1)}, bf16[384,256]{1,0:T(8,128)(2,1)S(1)}, u32[]{:S(2)}, u32[]{:S(2)}) collective-permute-start(bf16[384,256]{1,0:T(8,128)(2,1)S(1)} %get-tuple-element.23), channel_id=1, source_target_pairs={{0,4},{1,5},{2,6},{3,7},{4,0},{5,1},{6,2},{7,3},{8,12},{9,13},{10,... | collective-permute-start | bytes 589832 | tf_op jit(solution)/shard_map/ppermute | solution.py:285
  9.3 18.5 %collective-permute-start.5 = (bf16[384,256]{1,0:T(8,128)(2,1)S(1)}, bf16[384,256]{1,0:T(8,128)(2,1)S(1)}, u32[]{:S(2)}, u32[]{:S(2)}) collective-permute-start(bf16[384,256]{1,0:T(8,128)(2,1)S(1)} %get-tuple-element.23), channel_id=1, source_target_pairs={{0,2},{1,3},{2,0},{3,1},{4,6},{5,7},{6,4},{7,5},{8,10},{9,11},{10,... | collective-permute-start | bytes 589832 | tf_op jit(solution)/shard_map/ppermute | solution.py:285
  11.3 8.0 %collective-permute-start.10 = (bf16[384,128]{1,0:T(8,128)(2,1)S(1)}, bf16[384,128]{1,0:T(8,128)(2,1)}, u32[]{:S(2)}, u32[]{:S(2)}) collective-permute-start(bf16[384,128]{1,0:T(8,128)(2,1)S(1)} %get-tuple-element.29), channel_id=1, source_target_pairs={{0,4},{1,5},{2,6},{3,7},{4,0},{5,1},{6,2},{7,3},{8,12},{9,13},{10,... | collective-permute-start | bytes 294920 | tf_op jit(solution)/shard_map/ppermute | solution.py:285
  27.7 22.3 %collective-permute-start.16 = (bf16[4,384,128]{2,1,0:T(8,128)(2,1)S(1)}, bf16[4,384,128]{2,1,0:T(8,128)(2,1)S(1)}, u32[]{:S(2)}, u32[]{:S(2)}) collective-permute-start(bf16[4,384,128]{2,1,0:T(8,128)(2,1)S(1)} %pad_maximum_fusion.2), channel_id=1, source_target_pairs={{0,1},{1,0},{2,3},{3,2},{4,5},{5,4},{6,7},{7,6},{8,9},{9,8},{10,11... | collective-permute-start | bytes 1179656 | tf_op jit(solution)/shard_map/ppermute | solution.py:285
  27.8 15.1 %collective-permute-start.2 = (bf16[384,256]{1,0:T(8,128)(2,1)S(1)}, bf16[384,256]{1,0:T(8,128)(2,1)S(1)}, u32[]{:S(2)}, u32[]{:S(2)}) collective-permute-start(bf16[384,256]{1,0:T(8,128)(2,1)S(1)} %collective-permute-done), channel_id=1, source_target_pairs={{0,4},{1,5},{2,6},{3,7},{4,0},{5,1},{6,2},{7,3},{8,12},{9,13},{10,... | collective-permute-start | bytes 589832 | tf_op jit(solution)/shard_map/ppermute | solution.py:285
  28.6 15.3 %collective-permute-start.1 = (bf16[384,256]{1,0:T(8,128)(2,1)S(1)}, bf16[384,256]{1,0:T(8,128)(2,1)S(1)}, u32[]{:S(2)}, u32[]{:S(2)}) collective-permute-start(bf16[384,256]{1,0:T(8,128)(2,1)S(1)} %collective-permute-done), channel_id=1, source_target_pairs={{0,2},{1,3},{2,0},{3,1},{4,6},{5,7},{6,4},{7,5},{8,10},{9,11},{10,... | collective-permute-start | bytes 589832 | tf_op jit(solution)/shard_map/ppermute | solution.py:285
  29.5 12.6 %collective-permute-start.7 = (bf16[384,256]{1,0:T(8,128)(2,1)S(1)}, bf16[384,256]{1,0:T(8,128)(2,1)S(1)}, u32[]{:S(2)}, u32[]{:S(2)}) collective-permute-start(bf16[384,256]{1,0:T(8,128)(2,1)S(1)} %collective-permute-done.6), channel_id=1, source_target_pairs={{0,2},{1,3},{2,0},{3,1},{4,6},{5,7},{6,4},{7,5},{8,10},{9,11},{10,... | collective-permute-start | bytes 589832 | tf_op jit(solution)/shard_map/ppermute | solution.py:285
  30.9 11.1 %collective-permute-start.15 = (bf16[384,128]{1,0:T(8,128)(2,1)S(1)}, bf16[384,128]{1,0:T(8,128)(2,1)S(1)}, u32[]{:S(2)}, u32[]{:S(2)}) collective-permute-start(bf16[384,128]{1,0:T(8,128)(2,1)S(1)} %collective-permute-done.14), channel_id=1, source_target_pairs={{0,2},{1,3},{2,0},{3,1},{4,6},{5,7},{6,4},{7,5},{8,10},{9,11},{10,... | collective-permute-start | bytes 294920 | tf_op jit(solution)/shard_map/ppermute | solution.py:285
  42.1 7.9 %collective-permute-start.17 = (bf16[4,384,128]{2,1,0:T(8,128)(2,1)S(1)}, bf16[4,384,128]{2,1,0:T(8,128)(2,1)S(1)}, u32[]{:S(2)}, u32[]{:S(2)}) collective-permute-start(bf16[4,384,128]{2,1,0:T(8,128)(2,1)S(1)} %pad_maximum_fusion.3), channel_id=1, source_target_pairs={{0,1},{1,0},{2,3},{3,2},{4,5},{5,4},{6,7},{7,6},{8,9},{9,8},{10,11... | collective-permute-start | bytes 1179656 | tf_op jit(solution)/shard_map/ppermute | solution.py:285
  49.8 11.4 %collective-permute-start.4 = (bf16[4,384,256]{2,1,0:T(8,128)(2,1)S(1)}, bf16[4,384,256]{2,1,0:T(8,128)(2,1)S(1)}, u32[]{:S(2)}, u32[]{:S(2)}) collective-permute-start(bf16[4,384,256]{2,1,0:T(8,128)(2,1)S(1)} %pad_maximum_fusion.mine), channel_id=1, source_target_pairs={{0,1},{1,0},{2,3},{3,2},{4,5},{5,4},{6,7},{7,6},{8,9},{9,8},{10,11... | collective-permute-start | bytes 2359304 | tf_op jit(solution)/shard_map/ppermute | solution.py:285
  88.3 40.3 %collective-permute-start.18 = (bf16[8,256,384]{2,1,0:T(8,128)(2,1)}, bf16[8,256,384]{2,1,0:T(8,128)(2,1)S(1)}, u32[]{:S(2)}, u32[]{:S(2)}) collective-permute-start(bf16[8,256,384]{2,1,0:T(8,128)(2,1)} %get-tuple-element.31), channel_id=1, source_target_pairs={{0,1},{1,0},{2,3},{3,2},{4,5},{5,4},{6,7},{7,6},{8,9},{9,8},{10,11... | collective-permute-start | bytes 4718600 | tf_op jit(solution)/shard_map/ppermute | solution.py:285
  103.9 20.4 %collective-permute-start.26 = (bf16[8,128,384]{2,1,0:T(8,128)(2,1)S(1)}, bf16[8,128,384]{2,1,0:T(8,128)(2,1)S(1)}, u32[]{:S(2)}, u32[]{:S(2)}) collective-permute-start(bf16[8,128,384]{2,1,0:T(8,128)(2,1)S(1)} %get-tuple-element.35), channel_id=1, source_target_pairs={{0,1},{1,0},{2,3},{3,2},{4,5},{5,4},{6,7},{7,6},{8,9},{9,8},{10,11... | collective-permute-start | bytes 2359304 | tf_op jit(solution)/shard_map/ppermute | solution.py:285
  127.7 22.9 %collective-permute-start.28 = (bf16[128,384]{1,0:T(8,128)(2,1)S(1)}, bf16[128,384]{1,0:T(8,128)(2,1)S(1)}, u32[]{:S(2)}, u32[]{:S(2)}) collective-permute-start(bf16[128,384]{1,0:T(8,128)(2,1)S(1)} %get-tuple-element.55), channel_id=1, source_target_pairs={{0,2},{1,3},{2,0},{3,1},{4,6},{5,7},{6,4},{7,5},{8,10},{9,11},{10,... | collective-permute-start | bytes 294920 | tf_op jit(solution)/shard_map/ppermute | solution.py:285
  129.3 11.4 %collective-permute-start.24 = (bf16[256,384]{1,0:T(8,128)(2,1)S(1)}, bf16[256,384]{1,0:T(8,128)(2,1)S(1)}, u32[]{:S(2)}, u32[]{:S(2)}) collective-permute-start(bf16[256,384]{1,0:T(8,128)(2,1)S(1)} %get-tuple-element.49), channel_id=1, source_target_pairs={{0,2},{1,3},{2,0},{3,1},{4,6},{5,7},{6,4},{7,5},{8,10},{9,11},{10,... | collective-permute-start | bytes 589832 | tf_op jit(solution)/shard_map/ppermute | solution.py:285
  130.4 14.5 %collective-permute-start.21 = (bf16[256,384]{1,0:T(8,128)(2,1)S(1)}, bf16[256,384]{1,0:T(8,128)(2,1)S(1)}, u32[]{:S(2)}, u32[]{:S(2)}) collective-permute-start(bf16[256,384]{1,0:T(8,128)(2,1)S(1)} %get-tuple-element.50), channel_id=1, source_target_pairs={{0,2},{1,3},{2,0},{3,1},{4,6},{5,7},{6,4},{7,5},{8,10},{9,11},{10,... | collective-permute-start | bytes 589832 | tf_op jit(solution)/shard_map/ppermute | solution.py:285
  132.3 16.9 %collective-permute-start.19 = (bf16[256,384]{1,0:T(8,128)(2,1)S(1)}, bf16[256,384]{1,0:T(8,128)(2,1)S(1)}, u32[]{:S(2)}, u32[]{:S(2)}) collective-permute-start(bf16[256,384]{1,0:T(8,128)(2,1)S(1)} %get-tuple-element.52), channel_id=1, source_target_pairs={{0,2},{1,3},{2,0},{3,1},{4,6},{5,7},{6,4},{7,5},{8,10},{9,11},{10,... | collective-permute-start | bytes 589832 | tf_op jit(solution)/shard_map/ppermute | solution.py:285
  134.5 16.1 %collective-permute-start.30 = (bf16[128,384]{1,0:T(8,128)(2,1)S(1)}, bf16[128,384]{1,0:T(8,128)(2,1)S(1)}, u32[]{:S(2)}, u32[]{:S(2)}) collective-permute-start(bf16[128,384]{1,0:T(8,128)(2,1)S(1)} %get-tuple-element.47), channel_id=1, source_target_pairs={{0,4},{1,5},{2,6},{3,7},{4,0},{5,1},{6,2},{7,3},{8,12},{9,13},{10,... | collective-permute-start | bytes 294920 | tf_op jit(solution)/shard_map/ppermute | solution.py:285
  140.7 29.3 %collective-permute-start.33 = (bf16[128,384]{1,0:T(8,128)(2,1)S(1)}, bf16[128,384]{1,0:T(8,128)(2,1)S(1)}, u32[]{:S(2)}, u32[]{:S(2)}) collective-permute-start(bf16[128,384]{1,0:T(8,128)(2,1)S(1)} %get-tuple-element.46), channel_id=1, source_target_pairs={{0,4},{1,5},{2,6},{3,7},{4,0},{5,1},{6,2},{7,3},{8,12},{9,13},{10,... | collective-permute-start | bytes 294920 | tf_op jit(solution)/shard_map/ppermute | solution.py:285
  145.0 8.3 %collective-permute-start.20 = (bf16[256,384]{1,0:T(8,128)(2,1)S(1)}, bf16[256,384]{1,0:T(8,128)(2,1)S(1)}, u32[]{:S(2)}, u32[]{:S(2)}) collective-permute-start(bf16[256,384]{1,0:T(8,128)(2,1)S(1)} %get-tuple-element.51), channel_id=1, source_target_pairs={{0,2},{1,3},{2,0},{3,1},{4,6},{5,7},{6,4},{7,5},{8,10},{9,11},{10,... | collective-permute-start | bytes 589832 | tf_op jit(solution)/shard_map/ppermute | solution.py:285
  149.3 10.8 %collective-permute-start.22 = (bf16[256,384]{1,0:T(8,128)(2,1)S(1)}, bf16[256,384]{1,0:T(8,128)(2,1)S(1)}, u32[]{:S(2)}, u32[]{:S(2)}) collective-permute-start(bf16[256,384]{1,0:T(8,128)(2,1)S(1)} %get-tuple-element.44), channel_id=1, source_target_pairs={{0,4},{1,5},{2,6},{3,7},{4,0},{5,1},{6,2},{7,3},{8,12},{9,13},{10,... | collective-permute-start | bytes 589832 | tf_op jit(solution)/shard_map/ppermute | solution.py:285
  150.6 19.5 %collective-permute-start.31 = (bf16[128,384]{1,0:T(8,128)(2,1)S(1)}, bf16[128,384]{1,0:T(8,128)(2,1)S(1)}, u32[]{:S(2)}, u32[]{:S(2)}) collective-permute-start(bf16[128,384]{1,0:T(8,128)(2,1)S(1)} %fusion.14), channel_id=1, source_target_pairs={{0,8},{1,9},{2,10},{3,11},{4,12},{5,13},{6,14},{7,15},{8,0},{9,1},... | collective-permute-start | bytes 294920 | tf_op jit(solution)/shard_map/ppermute | solution.py:285
  153.0 18.1 %collective-permute-start.25 = (bf16[256,384]{1,0:T(8,128)(2,1)S(1)}, bf16[256,384]{1,0:T(8,128)(2,1)S(1)}, u32[]{:S(2)}, u32[]{:S(2)}) collective-permute-start(bf16[256,384]{1,0:T(8,128)(2,1)S(1)} %get-tuple-element.43), channel_id=1, source_target_pairs={{0,4},{1,5},{2,6},{3,7},{4,0},{5,1},{6,2},{7,3},{8,12},{9,13},{10,... | collective-permute-start | bytes 589832 | tf_op jit(solution)/shard_map/ppermute | solution.py:285
  160.1 10.9 %collective-permute-start.23 = (bf16[256,384]{1,0:T(8,128)(2,1)S(1)}, bf16[256,384]{1,0:T(8,128)(2,1)S(1)}, u32[]{:S(2)}, u32[]{:S(2)}) collective-permute-start(bf16[256,384]{1,0:T(8,128)(2,1)S(1)} %fusion.6), channel_id=1, source_target_pairs={{0,8},{1,9},{2,10},{3,11},{4,12},{5,13},{6,14},{7,15},{8,0},{9,1},... | collective-permute-start | bytes 589832 | tf_op jit(solution)/shard_map/ppermute | solution.py:285
  (15 other events, 73.3 us)

commit v2 on v0

v2 whole, which is shorter than its diff:
```python
import functools

import jax
import jax.numpy as jnp
from jax import lax
from jax.experimental import pallas as pl
from jax.experimental.pallas import tpu as pltpu
from jax.sharding import PartitionSpec as P

F32 = jnp.float32
BF16 = jnp.bfloat16
VMEM_BYTES = 52 * 1024 * 1024


def dot(a, b, ca, cb):
    return lax.dot_general(a, b, (((ca,), (cb,)), ((), ())), preferred_element_type=F32)


def params():
    return pltpu.CompilerParams(vmem_limit_bytes=VMEM_BYTES)


def my_core():
    return lax.axis_index("hid") % 2


def chip_columns(k, width):
    chip = (lax.axis_index("hid") // 2) ^ k
    return pl.ds(pl.multiple_of(chip * (2 * width), 2 * width), 2 * width)


def call(kernel, name, operands, outs, scratch, flops, nbytes, alias=None):
    return pl.pallas_call(
        kernel,
        in_specs=[pl.BlockSpec(memory_space=pl.ANY)] * len(operands),
        out_specs=[pl.BlockSpec(memory_space=pl.ANY)] * len(outs),
        out_shape=[jax.ShapeDtypeStruct(shape, kind) for shape, kind in outs],
        scratch_shapes=scratch,
        input_output_aliases={} if alias is None else {alias: 0},
        compiler_params=params(),
        cost_estimate=pl.CostEstimate(flops=flops, bytes_accessed=nbytes, transcendentals=0),
        name=name,
    )(*operands)


def copies(sems, *pairs):
    made = [pltpu.make_async_copy(src, dst, sems.at[i]) for i, (src, dst) in enumerate(pairs)]
    for c in made:
        c.start()
    return made


def wait_all(made):
    for c in made:
        c.wait()


def dma(count):
    return pltpu.SemaphoreType.DMA((count,))


def start_each(steps, make):
    def one(j, carry):
        make(j).start()
        return carry

    lax.fori_loop(0, steps, one, 0)


def wait_each(steps, make):
    def one(j, carry):
        make(j).wait()
        return carry

    lax.fori_loop(0, steps, one, 0)


def each(steps, body):
    def one(j, carry):
        body(j)
        return carry

    lax.fori_loop(0, steps, one, 0)


def stream(steps, ahead, make, body):
    for j in range(min(ahead, steps)):
        make(j).start()

    def one(j):
        make(j).wait()

        @pl.when(j + ahead < steps)
        def _():
            make(j + ahead).start()

        body(j)

    each(steps, one)


def order_kernel(
    mask_ref, tokens_ref, upstream_ref, one_hot_ref, tokens_out, grad_out, mask_v, tokens_v, upstream_v, one_hot_v, out_v, grad_v, sems
):
    made = copies(sems, (mask_ref, mask_v), (tokens_ref, tokens_v), (upstream_ref, upstream_v))
    tok = tokens_v.shape[0]
    live = tok // 2
    made[0].wait()
    mask = mask_v[...].astype(F32)
    before = lax.broadcasted_iota(jnp.int32, (tok, tok), 0) < lax.broadcasted_iota(jnp.int32, (tok, tok), 1)
    rank = dot(jnp.broadcast_to(mask, (8, tok)).astype(BF16), before.astype(F32).astype(BF16), 1, 0)[:1]
    column = lax.broadcasted_iota(jnp.int32, (1, tok), 1).astype(F32)
    place = jnp.where(mask > 0, rank, live + column - rank)
    row = lax.broadcasted_iota(jnp.int32, (tok, tok), 0).astype(F32)
    one_hot = (row == place).astype(F32).astype(BF16)
    one_hot_v[...] = one_hot
    made[1].wait()
    out_v[...] = dot(tokens_v[...], one_hot, 0, 1).astype(BF16)
    made[2].wait()
    out = copies(sems, (one_hot_v, one_hot_ref), (out_v, tokens_out))
    grad_v[...] = dot(upstream_v[...], one_hot[:live], 0, 1).astype(BF16)
    wait_all(out + copies(sems.at[pl.ds(2, 1)], (grad_v, grad_out)))


def order_tokens(tokens, upstream, loss_mask):
    tok, width = tokens.shape
    outs = [((tok, tok), BF16), ((width, tok), BF16), ((width, tok // 2), BF16)]
    return call(
        order_kernel,
        "order_tokens",
        (loss_mask.reshape(1, tok), tokens, upstream),
        outs,
        [
            pltpu.VMEM((1, tok), jnp.int32),
            pltpu.VMEM((tok, width), BF16),
            pltpu.VMEM((tok, width), BF16),
            *[pltpu.VMEM(*out) for out in outs],
            dma(3),
        ],
        3 * tok * tok * width,
        8 * tok * width,
    )


def pair_copies(mine, other, dst):
    width = mine.shape[1]
    core = my_core()
    return (
        (mine, dst.at[:, pl.ds(pl.multiple_of(core * width, width), width)]),
        (other, dst.at[:, pl.ds(pl.multiple_of((1 - core) * width, width), width)]),
    )


def row_columns(k, wide):
    row = (lax.axis_index("hid") // 4) ^ k
    return pl.ds(pl.multiple_of(row * wide, wide), wide)


def row_copies(mine, other, dst):
    rows, wide, _ = dst.shape
    width = wide // 4
    in_row = lax.axis_index("hid") % 4
    pairs = []
    for row in range(rows):
        for side in range(2):
            for flipped, part in enumerate((mine, other)):
                at = pl.ds(pl.multiple_of((in_row ^ (2 * side + flipped)) * width, width), width)
                pairs.append((part.at[2 * row + side], dst.at[row, at]))
    return pairs


def piece_copies(sems, total, rounded, keep_ref, send_ref):
    rows, _, wide = total.shape
    width = wide // 4
    in_row = lax.axis_index("hid") % 4
    pairs = []
    for row in range(rows):
        for side in range(2):
            at = [pl.ds(pl.multiple_of((in_row ^ (2 * side + i)) * width, width), width) for i in range(2)]
            pairs.append((total.at[row, :, at[0]], keep_ref.at[2 * row + side]))
            pairs.append((rounded.at[row, :, at[1]], send_ref.at[2 * row + side]))
    return copies(sems, *pairs)


def start_gate_up(gate_w, up_w, base, j, buffer, sem):
    wide = buffer.shape[1]
    for i, weight in enumerate((gate_w, up_w)):

        @pl.when(j % 2 == i)
        def _():
            pltpu.make_async_copy(weight.at[:, row_columns(base + j // 2, wide)], buffer, sem).start()


def start_down(down_w, j, buffer, sem):
    pltpu.make_async_copy(down_w.at[:, row_columns(j, buffer.shape[1])], buffer, sem).start()


def wait_block(down_w, buffer, sem):
    pltpu.make_async_copy(down_w.at[:, pl.ds(0, buffer.shape[1])], buffer, sem).wait()


def forward_kernel(
    mine, other, gate_w, up_w, down_w, hidden_t_ref, act_ref, slope_ref, keep_ref, send_ref, x, w, acc, *rest
):
    hidden_v, hidden_t_v, act_v, slope_v, total, rounded, sems, x_sems, w_sems, out_sems = rest
    slots = w.shape[0]
    rows = x.shape[0]
    steps = 2 * rows

    def start(j):
        slot = j % slots
        start_gate_up(gate_w, up_w, 0, j, w.at[slot], w_sems.at[slot])

    def start_last(j):
        start_down(down_w, j, w.at[j % slots], w_sems.at[j % slots])

    x_in = copies(x_sems, *row_copies(mine, other, x))
    start(0)
    start(1)
    acc[...] = jnp.zeros_like(acc)
    wait_all(x_in)

    def one(j):
        slot = j % slots
        wait_block(gate_w, w.at[slot], w_sems.at[slot])

        @pl.when(j + 2 < steps)
        def _():
            start(j + 2)

        @pl.when(j + 2 >= steps)
        def _():
            start_last(j + 2 - steps)

        acc[j % 2] += dot(w[slot], x[j // 2], 1, 0)

    each(steps, one)
    live = act_v.shape[1]
    gate_lin = acc[0]
    up_lin = acc[1]
    sig = jax.nn.sigmoid(gate_lin)
    act = gate_lin * sig
    hidden = (act * up_lin).astype(BF16)
    hidden_t_v[...] = hidden[:, :live]
    act_v[...] = act[:, :live]
    slope_v[...] = (up_lin * sig * (1.0 + gate_lin * (1.0 - sig)))[:, :live]
    hidden_v[...] = hidden.T
    out = copies(sems, (hidden_t_v, hidden_t_ref), (act_v, act_ref), (slope_v, slope_ref))

    def two(j):
        slot = j % slots
        wait_block(down_w, w.at[slot], w_sems.at[slot])

        @pl.when(j + 2 < rows)
        def _():
            start_last(j + 2)

        part = dot(hidden_v[...], w[slot], 1, 0)
        total[j] = part
        rounded[j] = part.astype(BF16)

    each(rows, two)
    wait_all(out + piece_copies(out_sems, total, rounded, keep_ref, send_ref))


def forward(mine, other, gate_w, up_w, down_w, live):
    chips, width, tok = mine.shape
    ff = gate_w.shape[0]
    rows, slots = chips // 2, 4
    return call(
        forward_kernel,
        "forward",
        (mine, other, gate_w, up_w, down_w),
        [
            ((ff, live), BF16),
            ((ff, live), F32),
            ((ff, live), F32),
            ((chips, tok, width), F32),
            ((chips, tok, width), BF16),
        ],
        [
            pltpu.VMEM((rows, 4 * width, tok), BF16),
            pltpu.VMEM((slots, ff, 4 * width), BF16),
            pltpu.VMEM((2, ff, tok), F32),
            pltpu.VMEM((tok, ff), BF16),
            pltpu.VMEM((ff, live), BF16),
            pltpu.VMEM((ff, live), F32),
            pltpu.VMEM((ff, live), F32),
            pltpu.VMEM((rows, tok, 4 * width), F32),
            pltpu.VMEM((rows, tok, 4 * width), BF16),
            dma(3),
            dma(2 * chips),
            dma(slots),
            dma(2 * chips),
        ],
        12 * chips * width * ff * tok,
        12 * chips * width * ff,
    )


def token_grad_loop(base, gate_w, up_w, d_hid, w, total, rounded, w_sems):
    steps = w.shape[0]
    total[...] = jnp.zeros_like(total)

    def one(j):
        wait_block(gate_w, w.at[j], w_sems.at[j])

        @pl.when(j + 2 < steps)
        def _():
            start_gate_up(gate_w, up_w, base, j + 2, w.at[j + 2], w_sems.at[j + 2])

        part = total[j // 2] + dot(d_hid[j % 2], w[j], 1, 0)
        total[j // 2] = part
        rounded[j // 2] = part.astype(BF16)

    each(steps, one)


def backward_first_kernel(
    base, mine, other, act_ref, slope_ref, gate_w, up_w, down_w, d_hid_ref, d_hid_t_ref, keep_ref, send_ref, g, act, slope, *rest
):
    w, acc, d_hid, d_hid_t, total, rounded, sems, g_sems, w_sems, t_sems, out_sems = rest
    steps = w.shape[0]
    first = copies(g_sems, *row_copies(mine, other, g))
    for j in range(2):
        start_down(down_w, j, w.at[j], w_sems.at[j])
    late = copies(sems, (act_ref, act), (slope_ref, slope))
    acc[...] = jnp.zeros_like(acc)
    wait_all(first)

    def one(j):
        wait_block(down_w, w.at[j], w_sems.at[j])

        @pl.when(j + 2 < steps)
        def _():
            start_down(down_w, j + 2, w.at[j + 2], w_sems.at[j + 2])

        acc[...] += dot(w[j], g[j], 1, 0)

        @pl.when(j + 2 >= steps)
        def _():
            start_gate_up(gate_w, up_w, base, j + 2 - steps, w.at[j + 2 - steps], t_sems.at[j + 2 - steps])

    each(steps, one)
    wait_all(late)
    d_gate = (acc[...] * slope[...]).astype(BF16)
    d_up = (acc[...] * act[...]).astype(BF16)
    d_hid_t[0] = d_gate
    d_hid_t[1] = d_up
    d_hid[0] = d_gate.T
    d_hid[1] = d_up.T
    out = copies(sems, (d_hid, d_hid_ref), (d_hid_t, d_hid_t_ref))
    token_grad_loop(base, gate_w, up_w, d_hid, w, total, rounded, t_sems)
    wait_all(out + piece_copies(out_sems, total, rounded, keep_ref, send_ref))


def backward_first(base, mine, other, act, slope, gate_w, up_w, down_w):
    chips, width, live = mine.shape
    ff = act.shape[0]
    rows = chips // 2
    steps = rows
    d_hid, d_hid_t = ((2, live, ff), BF16), ((2, ff, live), BF16)
    return call(
        functools.partial(backward_first_kernel, base),
        "backward_first",
        (mine, other, act, slope, gate_w, up_w, down_w),
        [d_hid, d_hid_t, ((steps, live, width), F32), ((steps, live, width), BF16)],
        [
            pltpu.VMEM((rows, 4 * width, live), BF16),
            pltpu.VMEM((ff, live), F32),
            pltpu.VMEM((ff, live), F32),
            pltpu.VMEM((steps, ff, 4 * width), BF16),
            pltpu.VMEM((ff, live), F32),
            pltpu.VMEM(*d_hid),
            pltpu.VMEM(*d_hid_t),
            pltpu.VMEM((steps // 2, live, 4 * width), F32),
            pltpu.VMEM((steps // 2, live, 4 * width), BF16),
            dma(2),
            dma(2 * chips),
            dma(steps),
            dma(steps),
            dma(2 * steps),
        ],
        4 * live * down_w.size,
        4 * down_w.size,
    )


def backward_rest_kernel(base, d_hid_ref, gate_w, up_w, keep_ref, send_ref, d_hid, w, total, rounded, sems, w_sems, out_sems):
    first = copies(sems, (d_hid_ref, d_hid))
    for j in range(2):
        start_gate_up(gate_w, up_w, base, j, w.at[j], w_sems.at[j])
    wait_all(first)
    token_grad_loop(base, gate_w, up_w, d_hid, w, total, rounded, w_sems)
    wait_all(piece_copies(out_sems, total, rounded, keep_ref, send_ref))


def backward_rest(base, steps, d_hid, gate_w, up_w, width):
    _, live, ff = d_hid.shape
    return call(
        functools.partial(backward_rest_kernel, base),
        "backward_rest",
        (d_hid, gate_w, up_w),
        [((steps, live, width), F32), ((steps, live, width), BF16)],
        [
            pltpu.VMEM((2, live, ff), BF16),
            pltpu.VMEM((steps, ff, 4 * width), BF16),
            pltpu.VMEM((steps // 2, live, 4 * width), F32),
            pltpu.VMEM((steps // 2, live, 4 * width), BF16),
            dma(1),
            dma(steps),
            dma(2 * steps),
        ],
        8 * live * steps * ff * width,
        8 * steps * ff * width,
    )


def weight_grad_kernel(which, hid_ref, mine, other, *refs):
    out_ref, hid, x, out_v, sems, out_sems = refs[-6:]
    steps = x.shape[0]
    width = mine.shape[1]
    live = hid.shape[1]
    parts = [part.at[:, :, pl.ds(0, live)] for part in (mine, other)]
    source = hid_ref if which is None else hid_ref.at[which]
    wait_all(copies(sems, (source, hid), *pair_copies(*parts, x)))

    def out_copy(j):
        return pltpu.make_async_copy(out_v.at[j], out_ref.at[:, chip_columns(j, width)], out_sems.at[j])

    def step(j):
        out_v[j] = dot(hid[...], x[j], 1, 1).astype(BF16)
        out_copy(j).start()

    each(steps, step)
    wait_each(steps, out_copy)


def weight_grad(hid, which, mine, other, name):
    steps, width, _ = mine.shape
    ff, live = hid.shape[-2:]
    return call(
        functools.partial(weight_grad_kernel, which),
        name,
        (hid, mine, other),
        [((ff, 2 * steps * width), BF16)],
        [
            pltpu.VMEM((ff, live), BF16),
            pltpu.VMEM((steps, 2 * width, live), BF16),
            pltpu.VMEM((steps, ff, 2 * width), BF16),
            dma(3),
            dma(steps),
        ],
        4 * live * ff * steps * width,
        4 * ff * steps * width,
    )[0]


def last_kernel(one_hot, *refs):
    total = refs[0][...].astype(F32)
    for part in refs[1:-1]:
        total = total + part[...].astype(F32)
    refs[-1][...] = dot(one_hot[...], total.astype(BF16), 0, 0).astype(BF16)


def last_sum(one_hot, parts, name):
    return pl.pallas_call(
        last_kernel,
        out_shape=jax.ShapeDtypeStruct((one_hot.shape[1], parts[0].shape[1]), BF16),
        compiler_params=params(),
        name=name,
    )(one_hot, *parts)


def flip(x, bits):
    return lax.ppermute(x, "hid", [(i, i ^ bits) for i in range(16)])


def plus(a, b):
    return a.astype(F32) + b.astype(F32)


def join(*arrays):
    return lax.optimization_barrier(arrays)


def body16(tokens, upstream, loss_mask, gate_weight, up_weight, down_weight):
    tok, width = tokens.shape
    live = tok // 2
    gate_w, up_w = gate_weight.T, up_weight.T
    one_hot, x, g = order_tokens(tokens, upstream, loss_mask)
    z2, z1, y = flip(x, 8), flip(x, 4), flip(x, 2)
    gz1, gy = flip(g, 4), flip(g, 2)
    z2, z1, y, gz1, gy, g = join(z2, z1, y, gz1, gy, g)
    z3, yz1, yz2 = flip(z2, 4), flip(z1, 2), flip(z2, 2)
    gz2 = flip(g, 8)
    z3, yz1, yz2, gz2, gz1 = join(z3, yz1, yz2, gz2, gz1)
    yz3 = flip(z3, 2)
    most = jnp.stack([x, y, z1, yz1, z2, yz2, z3])
    most_other = flip(most, 1)
    gz3, gyz1, gyz2 = flip(gz2, 4), flip(gz1, 2), flip(gz2, 2)
    most_other, yz3, gz3, gyz1, gyz2 = join(most_other, yz3, gz3, gyz1, gyz2)
    x_mine = jnp.concatenate([most, yz3[None]])
    x_other = jnp.concatenate([most_other, flip(yz3, 1)[None]])
    gyz3 = flip(gz3, 2)
    g_most = jnp.stack([g, gy, gz1, gyz1, gz2, gyz2, gz3])
    g_most_other = flip(g_most, 1)
    hidden_t, act, slope, out_keep, out_send = forward(x_mine, x_other, gate_w, up_w, down_weight, live)
    out_send, gyz3, g_most_other = join(out_send, gyz3, g_most_other)
    g_mine = jnp.concatenate([g_most, gyz3[None]])
    g_other = jnp.concatenate([g_most_other, flip(gyz3, 1)[None]])
    recv = flip(out_send, 1)
    d_hid, d_hid_t, tk1, ts1 = backward_first(2, g_mine, g_other, act, slope, gate_w, up_w, down_weight)
    d_hid, recv, ts1 = join(d_hid, recv, ts1)
    y23 = flip(plus(out_keep[5::2], recv[5::2]).astype(BF16), 2)
    recv1 = flip(ts1, 1)
    tk0, ts0 = backward_rest(0, 4, d_hid, gate_w, up_w, width)
    ts0, y23, recv1, recv, hidden_t = join(ts0, y23, recv1, recv, hidden_t)
    z13 = flip((plus(out_keep[6], recv[6]) + y23[1].astype(F32)).astype(BF16), 4)
    y01 = jnp.concatenate([plus(out_keep[1:4:2], recv[1:4:2]), plus(tk1[1::2], recv1[1::2])], axis=1)
    y01 = flip(y01.astype(BF16), 2)
    recv0 = flip(ts0, 1)
    down_grad = weight_grad(hidden_t, None, g_mine, g_other, "down_grad")
    down_grad, z13, y01, recv0, d_hid_t = join(down_grad, z13, y01, recv0, d_hid_t)
    y01, ty1 = y01[:, :tok], y01[:, tok:]
    z2 = flip((plus(out_keep[4], recv[4]) + plus(y23[0], z13)).astype(BF16), 8)
    z1 = jnp.concatenate([plus(out_keep[2], recv[2]) + y01[1].astype(F32), plus(tk1[2], recv1[2]) + ty1[1].astype(F32)])
    z1 = flip(z1.astype(BF16), 4)
    ty0 = flip(plus(tk0[1::2], recv0[1::2]).astype(BF16), 2)
    gate_grad = weight_grad(d_hid_t, 0, x_mine, x_other, "gate_grad")
    gate_grad, d_hid_t, ty0, z2, z1 = join(gate_grad, d_hid_t, ty0, z2, z1)
    z1, tz13 = z1[:tok], z1[tok:]
    tz2 = flip((plus(tk1[0], recv1[0]) + plus(ty1[0], tz13)).astype(BF16), 8)
    tz1 = flip((plus(tk0[2], recv0[2]) + ty0[1].astype(F32)).astype(BF16), 4)
    ffn_output = last_sum(one_hot, (plus(out_keep[0], recv[0]) + y01[0].astype(F32), z2, z1), "ffn_output")
    up_grad = weight_grad(d_hid_t, 1, x_mine, x_other, "up_grad")
    up_grad, tz2, tz1 = join(up_grad, tz2, tz1)
    token_grad = last_sum(one_hot[:live], (plus(tk0[0], recv0[0]) + ty0[0].astype(F32), tz2, tz1), "token_grad")
    return ffn_output, token_grad, gate_grad.T, up_grad.T, down_grad


def body_any(tokens, upstream, loss_mask, gate_weight, up_weight, down_weight):
    masked = upstream * loss_mask[:, None].astype(upstream.dtype)
    tokens = lax.all_gather(tokens, "hid", axis=1, tiled=True)
    grad = lax.all_gather(masked, "hid", axis=1, tiled=True)
    gate_lin = dot(tokens, gate_weight, 1, 0)
    up_lin = dot(tokens, up_weight, 1, 0)
    sig = jax.nn.sigmoid(gate_lin)
    act = gate_lin * sig
    hidden = (act * up_lin).astype(BF16)
    out = lax.psum_scatter(dot(down_weight, hidden, 0, 1), "hid", scatter_dimension=0, tiled=True)
    d_hidden = dot(grad, down_weight, 1, 1)
    d_up = (d_hidden * act).astype(BF16)
    d_gate = (d_hidden * up_lin * sig * (1.0 + gate_lin * (1.0 - sig))).astype(BF16)
    down_grad = dot(hidden, grad, 0, 0).astype(BF16)
    gate_grad = dot(tokens, d_gate, 0, 0).astype(BF16)
    up_grad = dot(tokens, d_up, 0, 0).astype(BF16)
    back = dot(gate_weight, d_gate, 1, 1) + dot(up_weight, d_up, 1, 1)
    back = lax.psum_scatter(back, "hid", scatter_dimension=0, tiled=True)
    return out.T.astype(BF16), back.T.astype(BF16), gate_grad, up_grad, down_grad


def solution(mesh):
    spec = P("groups", "hid")
    in_specs = (spec, spec, P("groups"), P(None, "hid"), P(None, "hid"), P("hid", None))
    out_specs = (spec, spec, spec, spec, P("hid", "groups"))
    body = body16 if mesh.shape["hid"] == 16 else body_any
    return jax.shard_map(body, mesh=mesh, in_specs=in_specs, out_specs=out_specs, check_vma=False)
```

time: 327 us -> 146 us (0.45)
  waiting for transfers between devices: 200 us -> 31.4 us
  matrix products: 107 us -> 0 us
  Pallas kernels: 0 us -> 76.7 us
  starting transfers between devices: 0.16 us -> 30.5 us
  between operations: 13.8 us -> 1.05 us
    reduce_scatter x2 -> x0, waiting for transfers between devices: 125 us -> none  [the longest x1 87 us: body(): lax.psum_scatter(lax.dot_general(down_weight, hidden, (((0,), (1,)), ((),...]
    dot_general x9 -> x0, matrix products: 107 us -> none  [the longest x1 14.4 us: body(): lax.dot_general(whole_grad, down_weight, (((1,), (1,)), ((), ())), prefer...]
    pallas_call x0 -> x9, Pallas kernels: none -> 76.7 us  [the longest x7 74.9 us: call(): pl.pallas_call(kernel, in_specs=[pl.BlockSpec(memory_space=pl.ANY)] * len...]
    all_gather x2 -> x0, waiting for transfers between devices: 74.6 us -> none  [the longest x1 49.7 us: body(): lax.all_gather(tokens, 'hid', axis=1, tiled=True)]
    ppermute x0 -> x29, waiting for transfers between devices: none -> 31.4 us  [flip(): return lax.ppermute(x, 'hid', [(i, i ^ bits) for i in range(16)])]
    ppermute x0 -> x29, starting transfers between devices: none -> 30.5 us  [flip(): return lax.ppermute(x, 'hid', [(i, i ^ bits) for i in range(16)])]
    convert_element_type x3 -> x6, other arithmetic: 4.07 us -> 0.38 us  [the longest x1 0.09 us: body16(): z2 = flip((plus(out_keep[4], recv[4]) + plus(y23[0], z13)).astype(BF16), 8)]
  transfers between devices with their start and end apart: 4 -> 29, of which waited for: 4 -> 10; matrix products, arithmetic and copies ran while one was open for 22% -> 2% of each run, Pallas kernels for 0% -> 51%
where the time goes in v2:
time: 146 us
  Pallas kernels  76.7 us (53%)
  waiting for transfers between devices  31.4 us (22%)
  starting transfers between devices  30.5 us (21%)
  local copies, waits for them, and re-layouts  3.02 us (2%)
  other arithmetic  2.95 us (2%)
    pallas_call x7, Pallas kernels, call(): pl.pallas_call(kernel, in_specs=[pl.BlockSpec(memory_space=pl.ANY)] * len...  74.9 us
    ppermute x29, waiting for transfers between devices, flip(): return lax.ppermute(x, 'hid', [(i, i ^ bits) for i in range(16)])  31.4 us
    ppermute x29, starting transfers between devices, flip(): return lax.ppermute(x, 'hid', [(i, i ^ bits) for i in range(16)])  30.5 us
  transfers between devices with their start and end apart: 29, of which 10 were waited for; matrix products, arithmetic and copies ran while one was open for 2% of the time, Pallas kernels for 51%

profile of v2, /device:TPU:0, one launch (start us, length us, event | category | flops | bytes accessed | tf_op | source)
XLA Modules:
  0.0 145.6 jit_solution(4995884146307824640)
XLA Ops:
  3.2 1.8 %order_tokens.1 = (bf16[256,256]{1,0:T(8,128)(2,1)S(1)}, bf16[384,256]{1,0:T(8,128)(2,1)S(1)}, bf16[384,128]{1,0:T(8,128)(2,1)S(1)}) custom-call(s32[1,256]{1,0:T(1,128)S(1)} %bitcast.75, bf16[256,384]{1,0:T(8,128)(2,1)S(1)} %copy-done.5, bf16[256,384]{1,0:T(8,128)(2,1)S(1)} %copy-done.6), custom_call_target="tpu_custom_call" | custom-call | flops 75497472 | bytes 786432 | tf_op jit(solution)/shard_map/order_tokens/pallas_call | solution.py:33
  4.9 3.0 %collective-permute-start.4 = (bf16[384,128]{1,0:T(8,128)(2,1)S(1)}, bf16[384,128]{1,0:T(8,128)(2,1)S(1)}, u32[]{:S(2)}, u32[]{:S(2)}) collective-permute-start(bf16[384,128]{1,0:T(8,128)(2,1)S(1)} %get-tuple-element.65), channel_id=1, source_target_pairs={{0,2},{1,3},{2,0},{3,1},{4,6},{5,7},{6,4},{7,5},{8,10},{9,11},{10,... | collective-permute-start | bytes 294920 | tf_op jit(solution)/shard_map/ppermute | solution.py:476
  10.1 3.0 %collective-permute-start = (bf16[384,256]{1,0:T(8,128)(2,1)S(1)}, bf16[384,256]{1,0:T(8,128)(2,1)S(1)}, u32[]{:S(2)}, u32[]{:S(2)}) collective-permute-start(bf16[384,256]{1,0:T(8,128)(2,1)S(1)} %get-tuple-element.60), channel_id=1, source_target_pairs={{0,8},{1,9},{2,10},{3,11},{4,12},{5,13},{6,14},{7,15},{8,0},{9,1},... | collective-permute-start | bytes 589832 | tf_op jit(solution)/shard_map/ppermute | solution.py:476
  13.1 4.6 %collective-permute-done.3 = bf16[384,128]{1,0:T(8,128)(2,1)S(1)} collective-permute-done((bf16[384,128]{1,0:T(8,128)(2,1)S(1)}, bf16[384,128]{1,0:T(8,128)(2,1)S(1)}, u32[]{:S(2)}, u32[]{:S(2)}) %collective-permute-start.3) | collective-permute-done | bytes 98336 | tf_op jit(solution)/shard_map/ppermute | solution.py:476
  17.8 3.3 %collective-permute-done.1 = bf16[384,256]{1,0:T(8,128)(2,1)S(1)} collective-permute-done((bf16[384,256]{1,0:T(8,128)(2,1)S(1)}, bf16[384,256]{1,0:T(8,128)(2,1)S(1)}, u32[]{:S(2)}, u32[]{:S(2)}) %collective-permute-start.1) | collective-permute-done | bytes 196640 | tf_op jit(solution)/shard_map/ppermute | solution.py:476
  21.6 2.6 %collective-permute-start.5 = (bf16[384,256]{1,0:T(8,128)(2,1)S(1)}, bf16[384,256]{1,0:T(8,128)(2,1)S(1)}, u32[]{:S(2)}, u32[]{:S(2)}) collective-permute-start(bf16[384,256]{1,0:T(8,128)(2,1)S(1)} %collective-permute-done), channel_id=1, source_target_pairs={{0,4},{1,5},{2,6},{3,7},{4,0},{5,1},{6,2},{7,3},{8,12},{9,13},{10,... | collective-permute-start | bytes 589832 | tf_op jit(solution)/shard_map/ppermute | solution.py:476
  24.2 2.7 %collective-permute-start.8 = (bf16[384,128]{1,0:T(8,128)(2,1)S(1)}, bf16[384,128]{1,0:T(8,128)(2,1)S(1)}, u32[]{:S(2)}, u32[]{:S(2)}) collective-permute-start(bf16[384,128]{1,0:T(8,128)(2,1)S(1)} %get-tuple-element.65), channel_id=1, source_target_pairs={{0,8},{1,9},{2,10},{3,11},{4,12},{5,13},{6,14},{7,15},{8,0},{9,1},... | collective-permute-start | bytes 294920 | tf_op jit(solution)/shard_map/ppermute | solution.py:476
  27.5 2.4 %collective-permute-done.8 = bf16[384,128]{1,0:T(8,128)(2,1)S(1)} collective-permute-done((bf16[384,128]{1,0:T(8,128)(2,1)S(1)}, bf16[384,128]{1,0:T(8,128)(2,1)S(1)}, u32[]{:S(2)}, u32[]{:S(2)}) %collective-permute-start.8) | collective-permute-done | bytes 98336 | tf_op jit(solution)/shard_map/ppermute | solution.py:476
  29.8 2.7 %collective-permute-done.6 = bf16[384,256]{1,0:T(8,128)(2,1)S(1)} collective-permute-done((bf16[384,256]{1,0:T(8,128)(2,1)S(1)}, bf16[384,256]{1,0:T(8,128)(2,1)S(1)}, u32[]{:S(2)}, u32[]{:S(2)}) %collective-permute-start.6) | collective-permute-done | bytes 196640 | tf_op jit(solution)/shard_map/ppermute | solution.py:476
  34.3 1.7 %collective-permute-start.10 = (bf16[384,256]{1,0:T(8,128)(2,1)S(1)}, bf16[384,256]{1,0:T(8,128)(2,1)S(1)}, u32[]{:S(2)}, u32[]{:S(2)}) collective-permute-start(bf16[384,256]{1,0:T(8,128)(2,1)S(1)} %collective-permute-done.5), channel_id=1, source_target_pairs={{0,2},{1,3},{2,0},{3,1},{4,6},{5,7},{6,4},{7,5},{8,10},{9,11},{10,... | collective-permute-start | bytes 589832 | tf_op jit(solution)/shard_map/ppermute | solution.py:476
  36.4 8.0 %collective-permute-done.12 = bf16[384,128]{1,0:T(8,128)(2,1)S(1)} collective-permute-done((bf16[384,128]{1,0:T(8,128)(2,1)S(1)}, bf16[384,128]{1,0:T(8,128)(2,1)S(1)}, u32[]{:S(2)}, u32[]{:S(2)}) %collective-permute-start.12) | collective-permute-done | bytes 98336 | tf_op jit(solution)/shard_map/ppermute | solution.py:476
  47.7 23.7 %forward.1 = (bf16[1472,128]{1,0:T(8,128)(2,1)S(1)}, f32[1472,128]{1,0:T(8,128)S(1)}, f32[1472,128]{1,0:T(8,128)S(1)}, f32[8,256,384]{2,1,0:T(8,128)}, bf16[8,256,384]{2,1,0:T(8,128)(2,1)}) custom-call(bf16[8,384,256]{2,1,0:T(8,128)(2,1)} %copy-done.8, bf16[8,384,256]{2,1,0:T(8,128)(2,1)} %pad_maximum_fusion.other, bf16[1472,6144]{1,0:T(8,128)(2,1)} %bitcast.76, ...), custom_call_target="tpu_custom_call" | custom-call | flops 13891534848 | bytes 54263808 | tf_op jit(solution)/shard_map/forward/pallas_call | solution.py:33
  72.0 2.8 %collective-permute-done.17 = bf16[384,128]{1,0:T(8,128)(2,1)S(1)} collective-permute-done((bf16[384,128]{1,0:T(8,128)(2,1)S(1)}, bf16[384,128]{1,0:T(8,128)(2,1)S(1)}, u32[]{:S(2)}, u32[]{:S(2)}) %collective-permute-start.17) | collective-permute-done | bytes 98336 | tf_op jit(solution)/shard_map/ppermute | solution.py:476
  75.8 16.0 %backward_first.1 = (bf16[2,128,1472]{2,1,0:T(8,128)(2,1)}, bf16[2,1472,128]{2,1,0:T(8,128)(2,1)S(1)}, f32[4,128,384]{2,1,0:T(8,128)}, bf16[4,128,384]{2,1,0:T(8,128)(2,1)S(1)}) custom-call(bf16[8,384,128]{2,1,0:T(8,128)(2,1)} %copy-done.1, bf16[8,384,128]{2,1,0:T(8,128)(2,1)} %pad_maximum_fusion.1.other, f32[1472,128]{1,0:T(8,128)S(1)} %get-tuple-element.82.act_ref, ...), custom_call_target="tpu_custom_call" | custom-call | flops 4630511616 | bytes 36175872 | tf_op jit(solution)/shard_map/backward_first/pallas_call | solution.py:33
  91.9 1.6 %collective-permute-start.19 = (bf16[2,256,384]{2,1,0:T(8,128)(2,1)S(1)}, bf16[2,256,384]{2,1,0:T(8,128)(2,1)S(1)}, u32[]{:S(2)}, u32[]{:S(2)}) collective-permute-start(bf16[2,256,384]{2,1,0:T(8,128)(2,1)S(1)} %add_convert_fusion.1), channel_id=1, source_target_pairs={{0,2},{1,3},{2,0},{3,1},{4,6},{5,7},{6,4},{7,5},{8,10},{9,11},{10,... | collective-permute-start | bytes 1179656 | tf_op jit(solution)/shard_map/ppermute | solution.py:476
  93.6 7.6 %backward_rest.1 = (f32[4,128,384]{2,1,0:T(8,128)S(1)}, bf16[4,128,384]{2,1,0:T(8,128)(2,1)S(1)}) custom-call(bf16[2,128,1472]{2,1,0:T(8,128)(2,1)S(1)} %copy-done.3, bf16[1472,6144]{1,0:T(8,128)(2,1)} %bitcast.78, bf16[1472,6144]{1,0:T(8,128)(2,1)} %bitcast.81), custom_call_target="tpu_custom_call" | custom-call | flops 2315255808 | bytes 18087936 | tf_op jit(solution)/shard_map/backward_rest/pallas_call | solution.py:33
  101.2 2.2 %collective-permute-done.19 = bf16[2,256,384]{2,1,0:T(8,128)(2,1)S(1)} collective-permute-done((bf16[2,256,384]{2,1,0:T(8,128)(2,1)S(1)}, bf16[2,256,384]{2,1,0:T(8,128)(2,1)S(1)}, u32[]{:S(2)}, u32[]{:S(2)}) %collective-permute-start.19) | collective-permute-done | bytes 393248 | tf_op jit(solution)/shard_map/ppermute | solution.py:476
  103.6 1.6 %collective-permute-start.22 = (bf16[2,384,384]{2,1,0:T(8,128)(2,1)S(1)}, bf16[2,384,384]{2,1,0:T(8,128)(2,1)S(1)}, u32[]{:S(2)}, u32[]{:S(2)}) collective-permute-start(bf16[2,384,384]{2,1,0:T(8,128)(2,1)S(1)} %pad_maximum_fusion.2), channel_id=1, source_target_pairs={{0,2},{1,3},{2,0},{3,1},{4,6},{5,7},{6,4},{7,5},{8,10},{9,11},{10,... | collective-permute-start | bytes 1769480 | tf_op jit(solution)/shard_map/ppermute | solution.py:476
  106.4 7.8 %down_grad.1 = bf16[1472,6144]{1,0:T(8,128)(2,1)} custom-call(bf16[1472,128]{1,0:T(8,128)(2,1)S(1)} %get-tuple-element.93.hid_ref, bf16[8,384,128]{2,1,0:T(8,128)(2,1)S(1)} %copy-done.2, bf16[8,384,128]{2,1,0:T(8,128)(2,1)S(1)} %copy-done), custom_call_target="tpu_custom_call" | custom-call | flops 2315255808 | bytes 18087936 | tf_op jit(solution)/shard_map/down_grad/pallas_call | solution.py:33
  114.3 4.2 %collective-permute-done.22 = bf16[2,384,384]{2,1,0:T(8,128)(2,1)S(1)} collective-permute-done((bf16[2,384,384]{2,1,0:T(8,128)(2,1)S(1)}, bf16[2,384,384]{2,1,0:T(8,128)(2,1)S(1)}, u32[]{:S(2)}, u32[]{:S(2)}) %collective-permute-start.22) | collective-permute-done | bytes 589856 | tf_op jit(solution)/shard_map/ppermute | solution.py:476
  119.8 1.8 %collective-permute-start.24 = (bf16[2,128,384]{2,1,0:T(8,128)(2,1)S(1)}, bf16[2,128,384]{2,1,0:T(8,128)(2,1)S(1)}, u32[]{:S(2)}, u32[]{:S(2)}) collective-permute-start(bf16[2,128,384]{2,1,0:T(8,128)(2,1)S(1)} %add_convert_fusion.3), channel_id=1, source_target_pairs={{0,2},{1,3},{2,0},{3,1},{4,6},{5,7},{6,4},{7,5},{8,10},{9,11},{10,... | collective-permute-start | bytes 589832 | tf_op jit(solution)/shard_map/ppermute | solution.py:476
  122.1 9.0 %gate_grad.1 = bf16[1472,6144]{1,0:T(8,128)(2,1)} custom-call(bf16[2,1472,128]{2,1,0:T(8,128)(2,1)S(1)} %get-tuple-element.107.hid_ref, bf16[8,384,256]{2,1,0:T(8,128)(2,1)} %copy-done.8, bf16[8,384,256]{2,1,0:T(8,128)(2,1)} %pad_maximum_fusion.other), custom_call_target="tpu_custom_call" | custom-call | flops 2315255808 | bytes 18087936 | tf_op jit(solution)/shard_map/gate_grad/pallas_call | solution.py:33
  132.5 2.2 %collective-permute-start.27 = (bf16[128,384]{1,0:T(8,128)(2,1)S(1)}, bf16[128,384]{1,0:T(8,128)(2,1)S(1)}, u32[]{:S(2)}, u32[]{:S(2)}) collective-permute-start(bf16[128,384]{1,0:T(8,128)(2,1)S(1)} %fusion.5), channel_id=1, source_target_pairs={{0,8},{1,9},{2,10},{3,11},{4,12},{5,13},{6,14},{7,15},{8,0},{9,1},... | collective-permute-start | bytes 294920 | tf_op jit(solution)/shard_map/ppermute | solution.py:476
  134.7 9.0 %up_grad.1 = bf16[1472,6144]{1,0:T(8,128)(2,1)} custom-call(bf16[2,1472,128]{2,1,0:T(8,128)(2,1)S(1)} %get-tuple-element.107.hid_ref, bf16[8,384,256]{2,1,0:T(8,128)(2,1)} %copy-done.8, bf16[8,384,256]{2,1,0:T(8,128)(2,1)} %pad_maximum_fusion.other), custom_call_target="tpu_custom_call" | custom-call | flops 2315255808 | bytes 18087936 | tf_op jit(solution)/shard_map/up_grad/pallas_call | solution.py:33
  (97 shorter events, 19.3 us)
Async XLA Ops:
  8.0 9.8 %collective-permute-start.3 = (bf16[384,128]{1,0:T(8,128)(2,1)S(1)}, bf16[384,128]{1,0:T(8,128)(2,1)S(1)}, u32[]{:S(2)}, u32[]{:S(2)}) collective-permute-start(bf16[384,128]{1,0:T(8,128)(2,1)S(1)} %get-tuple-element.65), channel_id=1, source_target_pairs={{0,4},{1,5},{2,6},{3,7},{4,0},{5,1},{6,2},{7,3},{8,12},{9,13},{10,... | collective-permute-start | bytes 294920 | tf_op jit(solution)/shard_map/ppermute | solution.py:476
  9.6 8.2 %collective-permute-start.2 = (bf16[384,256]{1,0:T(8,128)(2,1)S(1)}, bf16[384,256]{1,0:T(8,128)(2,1)S(1)}, u32[]{:S(2)}, u32[]{:S(2)}) collective-permute-start(bf16[384,256]{1,0:T(8,128)(2,1)S(1)} %get-tuple-element.60), channel_id=1, source_target_pairs={{0,2},{1,3},{2,0},{3,1},{4,6},{5,7},{6,4},{7,5},{8,10},{9,11},{10,... | collective-permute-start | bytes 589832 | tf_op jit(solution)/shard_map/ppermute | solution.py:476
  10.1 11.0 %collective-permute-start.1 = (bf16[384,256]{1,0:T(8,128)(2,1)S(1)}, bf16[384,256]{1,0:T(8,128)(2,1)S(1)}, u32[]{:S(2)}, u32[]{:S(2)}) collective-permute-start(bf16[384,256]{1,0:T(8,128)(2,1)S(1)} %get-tuple-element.60), channel_id=1, source_target_pairs={{0,4},{1,5},{2,6},{3,7},{4,0},{5,1},{6,2},{7,3},{8,12},{9,13},{10,... | collective-permute-start | bytes 589832 | tf_op jit(solution)/shard_map/ppermute | solution.py:476
  10.1 10.9 %collective-permute-start = (bf16[384,256]{1,0:T(8,128)(2,1)S(1)}, bf16[384,256]{1,0:T(8,128)(2,1)S(1)}, u32[]{:S(2)}, u32[]{:S(2)}) collective-permute-start(bf16[384,256]{1,0:T(8,128)(2,1)S(1)} %get-tuple-element.60), channel_id=1, source_target_pairs={{0,8},{1,9},{2,10},{3,11},{4,12},{5,13},{6,14},{7,15},{8,0},{9,1},... | collective-permute-start | bytes 589832 | tf_op jit(solution)/shard_map/ppermute | solution.py:476
  21.0 11.5 %collective-permute-start.7 = (bf16[384,256]{1,0:T(8,128)(2,1)S(1)}, bf16[384,256]{1,0:T(8,128)(2,1)S(1)}, u32[]{:S(2)}, u32[]{:S(2)}) collective-permute-start(bf16[384,256]{1,0:T(8,128)(2,1)S(1)} %collective-permute-done), channel_id=1, source_target_pairs={{0,2},{1,3},{2,0},{3,1},{4,6},{5,7},{6,4},{7,5},{8,10},{9,11},{10,... | collective-permute-start | bytes 589832 | tf_op jit(solution)/shard_map/ppermute | solution.py:476
  21.6 11.0 %collective-permute-start.5 = (bf16[384,256]{1,0:T(8,128)(2,1)S(1)}, bf16[384,256]{1,0:T(8,128)(2,1)S(1)}, u32[]{:S(2)}, u32[]{:S(2)}) collective-permute-start(bf16[384,256]{1,0:T(8,128)(2,1)S(1)} %collective-permute-done), channel_id=1, source_target_pairs={{0,4},{1,5},{2,6},{3,7},{4,0},{5,1},{6,2},{7,3},{8,12},{9,13},{10,... | collective-permute-start | bytes 589832 | tf_op jit(solution)/shard_map/ppermute | solution.py:476
  32.7 11.7 %collective-permute-start.9 = (bf16[7,384,256]{2,1,0:T(8,128)(2,1)S(1)}, bf16[7,384,256]{2,1,0:T(8,128)(2,1)S(1)}, u32[]{:S(2)}, u32[]{:S(2)}) collective-permute-start(bf16[7,384,256]{2,1,0:T(8,128)(2,1)S(1)} %get-tuple-element.117), channel_id=1, source_target_pairs={{0,1},{1,0},{2,3},{3,2},{4,5},{5,4},{6,7},{7,6},{8,9},{9,8},{10,11... | collective-permute-start | bytes 4128776 | tf_op jit(solution)/shard_map/ppermute | solution.py:476
  32.8 11.6 %collective-permute-start.13 = (bf16[384,128]{1,0:T(8,128)(2,1)S(1)}, bf16[384,128]{1,0:T(8,128)(2,1)S(1)}, u32[]{:S(2)}, u32[]{:S(2)}) collective-permute-start(bf16[384,128]{1,0:T(8,128)(2,1)S(1)} %collective-permute-done.8), channel_id=1, source_target_pairs={{0,2},{1,3},{2,0},{3,1},{4,6},{5,7},{6,4},{7,5},{8,10},{9,11},{10,... | collective-permute-start | bytes 294920 | tf_op jit(solution)/shard_map/ppermute | solution.py:476
  33.4 11.0 %collective-permute-start.11 = (bf16[384,128]{1,0:T(8,128)(2,1)S(1)}, bf16[384,128]{1,0:T(8,128)(2,1)S(1)}, u32[]{:S(2)}, u32[]{:S(2)}) collective-permute-start(bf16[384,128]{1,0:T(8,128)(2,1)S(1)} %collective-permute-done.8), channel_id=1, source_target_pairs={{0,4},{1,5},{2,6},{3,7},{4,0},{5,1},{6,2},{7,3},{8,12},{9,13},{10,... | collective-permute-start | bytes 294920 | tf_op jit(solution)/shard_map/ppermute | solution.py:476
  34.3 10.1 %collective-permute-start.10 = (bf16[384,256]{1,0:T(8,128)(2,1)S(1)}, bf16[384,256]{1,0:T(8,128)(2,1)S(1)}, u32[]{:S(2)}, u32[]{:S(2)}) collective-permute-start(bf16[384,256]{1,0:T(8,128)(2,1)S(1)} %collective-permute-done.5), channel_id=1, source_target_pairs={{0,2},{1,3},{2,0},{3,1},{4,6},{5,7},{6,4},{7,5},{8,10},{9,11},{10,... | collective-permute-start | bytes 589832 | tf_op jit(solution)/shard_map/ppermute | solution.py:476
  36.0 8.4 %collective-permute-start.12 = (bf16[384,128]{1,0:T(8,128)(2,1)S(1)}, bf16[384,128]{1,0:T(8,128)(2,1)S(1)}, u32[]{:S(2)}, u32[]{:S(2)}) collective-permute-start(bf16[384,128]{1,0:T(8,128)(2,1)S(1)} %collective-permute-done.3), channel_id=1, source_target_pairs={{0,2},{1,3},{2,0},{3,1},{4,6},{5,7},{6,4},{7,5},{8,10},{9,11},{10,... | collective-permute-start | bytes 294920 | tf_op jit(solution)/shard_map/ppermute | solution.py:476
  44.4 27.0 %collective-permute-start.15 = (bf16[384,128]{1,0:T(8,128)(2,1)S(1)}, bf16[384,128]{1,0:T(8,128)(2,1)S(1)}, u32[]{:S(2)}, u32[]{:S(2)}) collective-permute-start(bf16[384,128]{1,0:T(8,128)(2,1)S(1)} %collective-permute-done.11), channel_id=1, source_target_pairs={{0,2},{1,3},{2,0},{3,1},{4,6},{5,7},{6,4},{7,5},{8,10},{9,11},{10,... | collective-permute-start | bytes 294920 | tf_op jit(solution)/shard_map/ppermute | solution.py:476
  45.2 26.3 %collective-permute-start.16 = (bf16[7,384,128]{2,1,0:T(8,128)(2,1)S(1)}, bf16[7,384,128]{2,1,0:T(8,128)(2,1)S(1)}, u32[]{:S(2)}, u32[]{:S(2)}) collective-permute-start(bf16[7,384,128]{2,1,0:T(8,128)(2,1)S(1)} %get-tuple-element.131), channel_id=1, source_target_pairs={{0,1},{1,0},{2,3},{3,2},{4,5},{5,4},{6,7},{7,6},{8,9},{9,8},{10,11... | collective-permute-start | bytes 2064392 | tf_op jit(solution)/shard_map/ppermute | solution.py:476
  71.4 20.4 %collective-permute-start.18 = (bf16[8,256,384]{2,1,0:T(8,128)(2,1)}, bf16[8,256,384]{2,1,0:T(8,128)(2,1)S(1)}, u32[]{:S(2)}, u32[]{:S(2)}) collective-permute-start(bf16[8,256,384]{2,1,0:T(8,128)(2,1)} %get-tuple-element.85), channel_id=1, source_target_pairs={{0,1},{1,0},{2,3},{3,2},{4,5},{5,4},{6,7},{7,6},{8,9},{9,8},{10,11... | collective-permute-start | bytes 4718600 | tf_op jit(solution)/shard_map/ppermute | solution.py:476
  91.9 11.5 %collective-permute-start.19 = (bf16[2,256,384]{2,1,0:T(8,128)(2,1)S(1)}, bf16[2,256,384]{2,1,0:T(8,128)(2,1)S(1)}, u32[]{:S(2)}, u32[]{:S(2)}) collective-permute-start(bf16[2,256,384]{2,1,0:T(8,128)(2,1)S(1)} %add_convert_fusion.1), channel_id=1, source_target_pairs={{0,2},{1,3},{2,0},{3,1},{4,6},{5,7},{6,4},{7,5},{8,10},{9,11},{10,... | collective-permute-start | bytes 1179656 | tf_op jit(solution)/shard_map/ppermute | solution.py:476
  93.5 9.9 %collective-permute-start.20 = (bf16[4,128,384]{2,1,0:T(8,128)(2,1)S(1)}, bf16[4,128,384]{2,1,0:T(8,128)(2,1)S(1)}, u32[]{:S(2)}, u32[]{:S(2)}) collective-permute-start(bf16[4,128,384]{2,1,0:T(8,128)(2,1)S(1)} %get-tuple-element.90), channel_id=1, source_target_pairs={{0,1},{1,0},{2,3},{3,2},{4,5},{5,4},{6,7},{7,6},{8,9},{9,8},{10,11... | collective-permute-start | bytes 1179656 | tf_op jit(solution)/shard_map/ppermute | solution.py:476
  103.6 14.8 %collective-permute-start.22 = (bf16[2,384,384]{2,1,0:T(8,128)(2,1)S(1)}, bf16[2,384,384]{2,1,0:T(8,128)(2,1)S(1)}, u32[]{:S(2)}, u32[]{:S(2)}) collective-permute-start(bf16[2,384,384]{2,1,0:T(8,128)(2,1)S(1)} %pad_maximum_fusion.2), channel_id=1, source_target_pairs={{0,2},{1,3},{2,0},{3,1},{4,6},{5,7},{6,4},{7,5},{8,10},{9,11},{10,... | collective-permute-start | bytes 1769480 | tf_op jit(solution)/shard_map/ppermute | solution.py:476
  105.2 9.0 %collective-permute-start.23 = (bf16[4,128,384]{2,1,0:T(8,128)(2,1)S(1)}, bf16[4,128,384]{2,1,0:T(8,128)(2,1)S(1)}, u32[]{:S(2)}, u32[]{:S(2)}) collective-permute-start(bf16[4,128,384]{2,1,0:T(8,128)(2,1)S(1)} %get-tuple-element.97), channel_id=1, source_target_pairs={{0,1},{1,0},{2,3},{3,2},{4,5},{5,4},{6,7},{7,6},{8,9},{9,8},{10,11... | collective-permute-start | bytes 1179656 | tf_op jit(solution)/shard_map/ppermute | solution.py:476
  105.3 9.0 %collective-permute-start.21 = (bf16[256,384]{1,0:T(8,128)(2,1)S(1)}, bf16[256,384]{1,0:T(8,128)(2,1)S(1)}, u32[]{:S(2)}, u32[]{:S(2)}) collective-permute-start(bf16[256,384]{1,0:T(8,128)(2,1)S(1)} %fusion.2), channel_id=1, source_target_pairs={{0,4},{1,5},{2,6},{3,7},{4,0},{5,1},{6,2},{7,3},{8,12},{9,13},{10,... | collective-permute-start | bytes 589832 | tf_op jit(solution)/shard_map/ppermute | solution.py:476
  118.8 12.9 %collective-permute-start.26 = (bf16[384,384]{1,0:T(8,128)(2,1)S(1)}, bf16[384,384]{1,0:T(8,128)(2,1)S(1)}, u32[]{:S(2)}, u32[]{:S(2)}) collective-permute-start(bf16[384,384]{1,0:T(8,128)(2,1)S(1)} %pad_maximum_fusion.3), channel_id=1, source_target_pairs={{0,4},{1,5},{2,6},{3,7},{4,0},{5,1},{6,2},{7,3},{8,12},{9,13},{10,... | collective-permute-start | bytes 884744 | tf_op jit(solution)/shard_map/ppermute | solution.py:476
  119.8 11.4 %collective-permute-start.24 = (bf16[2,128,384]{2,1,0:T(8,128)(2,1)S(1)}, bf16[2,128,384]{2,1,0:T(8,128)(2,1)S(1)}, u32[]{:S(2)}, u32[]{:S(2)}) collective-permute-start(bf16[2,128,384]{2,1,0:T(8,128)(2,1)S(1)} %add_convert_fusion.3), channel_id=1, source_target_pairs={{0,2},{1,3},{2,0},{3,1},{4,6},{5,7},{6,4},{7,5},{8,10},{9,11},{10,... | collective-permute-start | bytes 589832 | tf_op jit(solution)/shard_map/ppermute | solution.py:476
  121.5 10.1 %collective-permute-start.25 = (bf16[256,384]{1,0:T(8,128)(2,1)S(1)}, bf16[256,384]{1,0:T(8,128)(2,1)S(1)}, u32[]{:S(2)}, u32[]{:S(2)}) collective-permute-start(bf16[256,384]{1,0:T(8,128)(2,1)S(1)} %fusion.1), channel_id=1, source_target_pairs={{0,8},{1,9},{2,10},{3,11},{4,12},{5,13},{6,14},{7,15},{8,0},{9,1},... | collective-permute-start | bytes 589832 | tf_op jit(solution)/shard_map/ppermute | solution.py:476
  131.8 12.9 %collective-permute-start.28 = (bf16[128,384]{1,0:T(8,128)(2,1)S(1)}, bf16[128,384]{1,0:T(8,128)(2,1)S(1)}, u32[]{:S(2)}, u32[]{:S(2)}) collective-permute-start(bf16[128,384]{1,0:T(8,128)(2,1)S(1)} %get-tuple-element.115), channel_id=1, source_target_pairs={{0,4},{1,5},{2,6},{3,7},{4,0},{5,1},{6,2},{7,3},{8,12},{9,13},{10,... | collective-permute-start | bytes 294920 | tf_op jit(solution)/shard_map/ppermute | solution.py:476
  132.5 12.2 %collective-permute-start.27 = (bf16[128,384]{1,0:T(8,128)(2,1)S(1)}, bf16[128,384]{1,0:T(8,128)(2,1)S(1)}, u32[]{:S(2)}, u32[]{:S(2)}) collective-permute-start(bf16[128,384]{1,0:T(8,128)(2,1)S(1)} %fusion.5), channel_id=1, source_target_pairs={{0,8},{1,9},{2,10},{3,11},{4,12},{5,13},{6,14},{7,15},{8,0},{9,1},... | collective-permute-start | bytes 294920 | tf_op jit(solution)/shard_map/ppermute | solution.py:476
  (16 other events, 62.8 us)

commit v3 on v2

v3 whole, which is shorter than its diff:
```python
import functools

import jax
import jax.numpy as jnp
from jax import lax
from jax.experimental import pallas as pl
from jax.experimental.pallas import tpu as pltpu
from jax.sharding import PartitionSpec as P

F32 = jnp.float32
BF16 = jnp.bfloat16
VMEM_BYTES = 52 * 1024 * 1024


def dot(a, b, ca, cb):
    return lax.dot_general(a, b, (((ca,), (cb,)), ((), ())), preferred_element_type=F32)


def params():
    return pltpu.CompilerParams(vmem_limit_bytes=VMEM_BYTES)


def my_core():
    return lax.axis_index("hid") % 2


def chip_columns(k, width):
    chip = (lax.axis_index("hid") // 2) ^ k
    return pl.ds(pl.multiple_of(chip * (2 * width), 2 * width), 2 * width)


def call(kernel, name, operands, outs, scratch, flops, nbytes, alias=None, vmem=VMEM_BYTES):
    return pl.pallas_call(
        kernel,
        in_specs=[pl.BlockSpec(memory_space=pl.ANY)] * len(operands),
        out_specs=[pl.BlockSpec(memory_space=pl.ANY)] * len(outs),
        out_shape=[jax.ShapeDtypeStruct(shape, kind) for shape, kind in outs],
        scratch_shapes=scratch,
        input_output_aliases={} if alias is None else {alias: 0},
        compiler_params=pltpu.CompilerParams(vmem_limit_bytes=vmem),
        cost_estimate=pl.CostEstimate(flops=flops, bytes_accessed=nbytes, transcendentals=0),
        name=name,
    )(*operands)


def copies(sems, *pairs):
    made = [pltpu.make_async_copy(src, dst, sems.at[i]) for i, (src, dst) in enumerate(pairs)]
    for c in made:
        c.start()
    return made


def wait_all(made):
    for c in made:
        c.wait()


def dma(count):
    return pltpu.SemaphoreType.DMA((count,))


def start_each(steps, make):
    def one(j, carry):
        make(j).start()
        return carry

    lax.fori_loop(0, steps, one, 0)


def wait_each(steps, make):
    def one(j, carry):
        make(j).wait()
        return carry

    lax.fori_loop(0, steps, one, 0)


def each(steps, body):
    def one(j, carry):
        body(j)
        return carry

    lax.fori_loop(0, steps, one, 0)


def stream(steps, ahead, make, body):
    for j in range(min(ahead, steps)):
        make(j).start()

    def one(j):
        make(j).wait()

        @pl.when(j + ahead < steps)
        def _():
            make(j + ahead).start()

        body(j)

    each(steps, one)


def order_kernel(
    mask_ref, tokens_ref, upstream_ref, one_hot_ref, tokens_out, grad_out, mask_v, tokens_v, upstream_v, one_hot_v, out_v, grad_v, sems
):
    made = copies(sems, (mask_ref, mask_v), (tokens_ref, tokens_v), (upstream_ref, upstream_v))
    tok = tokens_v.shape[0]
    live = tok // 2
    made[0].wait()
    mask = mask_v[...].astype(F32)
    before = lax.broadcasted_iota(jnp.int32, (tok, tok), 0) < lax.broadcasted_iota(jnp.int32, (tok, tok), 1)
    rank = dot(jnp.broadcast_to(mask, (8, tok)).astype(BF16), before.astype(F32).astype(BF16), 1, 0)[:1]
    column = lax.broadcasted_iota(jnp.int32, (1, tok), 1).astype(F32)
    place = jnp.where(mask > 0, rank, live + column - rank)
    row = lax.broadcasted_iota(jnp.int32, (tok, tok), 0).astype(F32)
    one_hot = (row == place).astype(F32).astype(BF16)
    one_hot_v[...] = one_hot
    made[1].wait()
    out_v[...] = dot(tokens_v[...], one_hot, 0, 1).astype(BF16)
    made[2].wait()
    out = copies(sems, (one_hot_v, one_hot_ref), (out_v, tokens_out))
    grad_v[...] = dot(upstream_v[...], one_hot[:live], 0, 1).astype(BF16)
    wait_all(out + copies(sems.at[pl.ds(2, 1)], (grad_v, grad_out)))


def order_tokens(tokens, upstream, loss_mask):
    tok, width = tokens.shape
    outs = [((tok, tok), BF16), ((width, tok), BF16), ((width, tok // 2), BF16)]
    return call(
        order_kernel,
        "order_tokens",
        (loss_mask.reshape(1, tok), tokens, upstream),
        outs,
        [
            pltpu.VMEM((1, tok), jnp.int32),
            pltpu.VMEM((tok, width), BF16),
            pltpu.VMEM((tok, width), BF16),
            *[pltpu.VMEM(*out) for out in outs],
            dma(3),
        ],
        3 * tok * tok * width,
        8 * tok * width,
        vmem=62 * 1024 * 1024,
    )


def row_columns(k, wide):
    row = (lax.axis_index("hid") // 4) ^ k
    return pl.ds(pl.multiple_of(row * wide, wide), wide)


def row_copies(mine, other, dst):
    rows, wide, _ = dst.shape
    width = wide // 4
    in_row = lax.axis_index("hid") % 4
    pairs = []
    for chip in range(2 * rows):
        for flipped, part in enumerate((mine, other)):
            at = pl.ds(pl.multiple_of((in_row ^ (2 * (chip % 2) + flipped)) * width, width), width)
            pairs.append((part[chip], dst.at[chip // 2, at]))
    return pairs


def with_last(most, last):
    return [most.at[k] for k in range(most.shape[0])] + [last.at[0]]


def even_odd(even, odd):
    return [(even, odd)[k % 2].at[k // 2] for k in range(2 * even.shape[0])]


def piece_copies(sems, total, rounded, keep_ref, send_ref):
    rows, _, wide = total.shape
    width = wide // 4
    in_row = lax.axis_index("hid") % 4
    pairs = []
    for row in range(rows):
        for side in range(2):
            at = [pl.ds(pl.multiple_of((in_row ^ (2 * side + i)) * width, width), width) for i in range(2)]
            pairs.append((total.at[row, :, at[0]], keep_ref.at[2 * row + side]))
            pairs.append((rounded.at[row, :, at[1]], send_ref.at[2 * row + side]))
    return copies(sems, *pairs)


def start_gate_up(gate_w, up_w, base, j, buffer, sem):
    wide = buffer.shape[1]
    for i, weight in enumerate((gate_w, up_w)):

        @pl.when(j % 2 == i)
        def _():
            pltpu.make_async_copy(weight.at[:, row_columns(base + j // 2, wide)], buffer, sem).start()


def start_down(down_w, j, buffer, sem):
    pltpu.make_async_copy(down_w.at[:, row_columns(j, buffer.shape[1])], buffer, sem).start()


def wait_block(down_w, buffer, sem):
    pltpu.make_async_copy(down_w.at[:, pl.ds(0, buffer.shape[1])], buffer, sem).wait()


def forward_kernel(
    mine, mine_last, other, other_last, gate_w, up_w, down_w, x_ref, hidden_t_ref, act_ref, slope_ref, *rest
):
    keep_even, keep_odd, send_even, send_odd = rest[:4]
    x, w, acc, hidden_v, hidden_t_v, act_v, slope_v, total, rounded, sems, x_sems, w_sems, out_sems = rest[4:]
    slots = w.shape[0]
    rows = x.shape[0]
    steps = 2 * rows

    def start(j):
        slot = j % slots
        start_gate_up(gate_w, up_w, 0, j, w.at[slot], w_sems.at[slot])

    def start_last(j):
        start_down(down_w, j, w.at[j % slots], w_sems.at[j % slots])

    x_pairs = row_copies(with_last(mine, mine_last), with_last(other, other_last), x)
    x_in = copies(x_sems, *x_pairs[:4])
    start(0)
    x_in += copies(x_sems.at[pl.ds(4, 4 * rows - 4)], *x_pairs[4:])
    start(1)
    acc[...] = jnp.zeros_like(acc)

    def one(j):
        slot = j % slots
        for row in range(rows):

            @pl.when(j == 2 * row)
            def _():
                wait_all(x_in[4 * row : 4 * row + 4])

        wait_block(gate_w, w.at[slot], w_sems.at[slot])

        @pl.when(j + 2 < steps)
        def _():
            start(j + 2)

        @pl.when(j + 2 >= steps)
        def _():
            start_last(j + 2 - steps)

        acc[j % 2] += dot(w[slot], x[j // 2], 1, 0)

    each(steps, one)
    live = act_v.shape[1]
    out = copies(sems, (x.at[:, :, pl.ds(0, live)], x_ref))
    gate_lin = acc[0]
    up_lin = acc[1]
    sig = jax.nn.sigmoid(gate_lin)
    act = gate_lin * sig
    hidden = (act * up_lin).astype(BF16)
    hidden_t_v[...] = hidden[:, :live]
    act_v[...] = act[:, :live]
    slope_v[...] = (up_lin * sig * (1.0 + gate_lin * (1.0 - sig)))[:, :live]
    hidden_v[...] = hidden.T
    out += copies(sems.at[pl.ds(1, 3)], (hidden_t_v, hidden_t_ref), (act_v, act_ref), (slope_v, slope_ref))

    wide = x.shape[1]
    width = wide // 4
    in_row = lax.axis_index("hid") % 4
    at = [pl.ds(pl.multiple_of((in_row ^ i) * width, width), width) for i in range(4)]

    def out_copies(j):
        pairs = (
            (rounded.at[j, :, at[3]], send_odd.at[j]),
            (rounded.at[j, :, at[2]], keep_odd.at[j]),
            (rounded.at[j, :, at[1]], send_even.at[j]),
            (total.at[j, :, at[0]], keep_even.at[j]),
        )
        return [pltpu.make_async_copy(src, dst, out_sems.at[4 * j + i]) for i, (src, dst) in enumerate(pairs)]

    def two(j):
        slot = j % slots
        wait_block(down_w, w.at[slot], w_sems.at[slot])

        @pl.when(j + 2 < rows)
        def _():
            start_last(j + 2)

        part = dot(hidden_v[...], w[slot], 1, 0)
        total[j] = part
        rounded[j] = part.astype(BF16)
        for c in out_copies(j):
            c.start()

    each(rows, two)
    for j in range(rows):
        wait_all(out_copies(j))
    wait_all(out)


def forward(mine, other, gate_w, up_w, down_w, live):
    _, width, tok = mine[0].shape
    ff, features = gate_w.shape
    chips = features // (2 * width)
    rows, slots = chips // 2, 4
    return call(
        forward_kernel,
        "forward",
        (*mine, *other, gate_w, up_w, down_w),
        [
            ((rows, 4 * width, live), BF16),
            ((ff, live), BF16),
            ((ff, live), F32),
            ((ff, live), F32),
            ((rows, tok, width), F32),
            ((rows, tok, width), BF16),
            ((rows, tok, width), BF16),
            ((rows, tok, width), BF16),
        ],
        [
            pltpu.VMEM((rows, 4 * width, tok), BF16),
            pltpu.VMEM((slots, ff, 4 * width), BF16),
            pltpu.VMEM((2, ff, tok), F32),
            pltpu.VMEM((tok, ff), BF16),
            pltpu.VMEM((ff, live), BF16),
            pltpu.VMEM((ff, live), F32),
            pltpu.VMEM((ff, live), F32),
            pltpu.VMEM((rows, tok, 4 * width), F32),
            pltpu.VMEM((rows, tok, 4 * width), BF16),
            dma(4),
            dma(2 * chips),
            dma(slots),
            dma(4 * rows),
        ],
        12 * chips * width * ff * tok,
        12 * chips * width * ff,
    )


def backward_kernel(
    mine, mine_odd, other, other_odd, act_ref, slope_ref, gate_w, up_w, down_w, g_ref, d_gate_ref, d_up_ref, *rest
):
    keep_ref, send_ref, g, act, slope, w, acc, *rest = rest
    d_hid, d_hid_t, total, rounded, sems, g_sems, w_sems, out_sems = rest
    slots = w.shape[0]
    rows = g.shape[0]
    steps = 2 * rows

    def start_first(j):
        start_down(down_w, j, w.at[j % slots], w_sems.at[j % slots])

    def start(j):
        slot = j % slots
        start_gate_up(gate_w, up_w, 0, j, w.at[slot], w_sems.at[slot])

    first = copies(g_sems, *row_copies(even_odd(mine, mine_odd), even_odd(other, other_odd), g))
    start_first(0)
    start_first(1)
    late = copies(sems, (act_ref, act), (slope_ref, slope))
    acc[...] = jnp.zeros_like(acc)
    total[...] = jnp.zeros_like(total)
    wait_all(first)

    def one(j):
        slot = j % slots
        wait_block(down_w, w.at[slot], w_sems.at[slot])

        @pl.when(j + 2 < rows)
        def _():
            start_first(j + 2)

        @pl.when(j + 2 >= rows)
        def _():
            start(j + 2 - rows)

        acc[...] += dot(w[slot], g[j], 1, 0)

    each(rows, one)
    wait_all(late)
    d_gate = (acc[...] * slope[...]).astype(BF16)
    d_up = (acc[...] * act[...]).astype(BF16)
    d_hid_t[0] = d_gate
    d_hid_t[1] = d_up
    d_hid[0] = d_gate.T
    d_hid[1] = d_up.T
    out = copies(sems, (d_hid_t.at[0], d_gate_ref), (d_hid_t.at[1], d_up_ref), (g, g_ref))

    def two(j):
        slot = j % slots
        wait_block(gate_w, w.at[slot], w_sems.at[slot])

        @pl.when(j + 2 < steps)
        def _():
            start(j + 2)

        part = total[j // 2] + dot(d_hid[j % 2], w[slot], 1, 0)
        total[j // 2] = part
        rounded[j // 2] = part.astype(BF16)

    each(steps, two)
    wait_all(out + piece_copies(out_sems, total, rounded, keep_ref, send_ref))


def backward(mine, other, act, slope, gate_w, up_w, down_w):
    _, width, live = mine[0].shape
    ff = act.shape[0]
    chips = down_w.shape[1] // (2 * width)
    rows, slots = chips // 2, 4
    d_hid_t = ((ff, live), BF16)
    return call(
        backward_kernel,
        "backward",
        (*mine, *other, act, slope, gate_w, up_w, down_w),
        [((rows, 4 * width, live), BF16), d_hid_t, d_hid_t, ((chips, live, width), F32), ((chips, live, width), BF16)],
        [
            pltpu.VMEM((rows, 4 * width, live), BF16),
            pltpu.VMEM((ff, live), F32),
            pltpu.VMEM((ff, live), F32),
            pltpu.VMEM((slots, ff, 4 * width), BF16),
            pltpu.VMEM((ff, live), F32),
            pltpu.VMEM((2, live, ff), BF16),
            pltpu.VMEM((2, ff, live), BF16),
            pltpu.VMEM((rows, live, 4 * width), F32),
            pltpu.VMEM((rows, live, 4 * width), BF16),
            dma(3),
            dma(2 * chips),
            dma(slots),
            dma(2 * chips),
        ],
        6 * live * down_w.size,
        6 * down_w.size,
    )


def weight_grad_kernel(base, hid_ref, x_ref, *refs):
    out_ref, hid, x, out_v, sems, out_sems = refs[-6:]
    steps = out_v.shape[0]
    rows, wide, _ = x.shape
    half = wide // 2
    ready = copies(sems, (hid_ref, hid), *[(x_ref.at[base + row], x.at[row]) for row in range(rows)])

    def out_copy(j):
        row = (lax.axis_index("hid") // 4) ^ (base + j // 2)
        at = pl.ds(pl.multiple_of(row * wide + (j % 2) * half, half), half)
        return pltpu.make_async_copy(out_v.at[j], out_ref.at[:, at], out_sems.at[j])

    ready[0].wait()

    def step(j):
        for row in range(rows):

            @pl.when(j == 2 * row)
            def _():
                ready[1 + row].wait()

        out_v[j] = dot(hid[...], x[j // 2, pl.ds(pl.multiple_of((j % 2) * half, half), half), :], 1, 1).astype(BF16)
        out_copy(j).start()

    each(steps, step)
    wait_each(steps, out_copy)


def weight_grad(hid, x, name, base=0, rows=4, before=None):
    all_rows, wide, live = x.shape
    ff = hid.shape[-2]
    steps = 2 * rows
    return call(
        functools.partial(weight_grad_kernel, base),
        name,
        (hid, x) if before is None else (hid, x, before),
        [((ff, all_rows * wide), BF16)],
        [
            pltpu.VMEM((ff, live), BF16),
            pltpu.VMEM((rows, wide, live), BF16),
            pltpu.VMEM((steps, ff, wide // 2), BF16),
            dma(1 + rows),
            dma(steps),
        ],
        2 * live * ff * rows * wide,
        2 * ff * rows * wide,
        None if before is None else 2,
        24 * 1024 * 1024,
    )[0]


def last_kernel(one_hot, *refs):
    total = refs[0][...].astype(F32)
    for part in refs[1:-1]:
        total = total + part[...].astype(F32)
    refs[-1][...] = dot(one_hot[...], total.astype(BF16), 0, 0).astype(BF16)


def last_sum(one_hot, parts, name):
    return pl.pallas_call(
        last_kernel,
        out_shape=jax.ShapeDtypeStruct((one_hot.shape[1], parts[0].shape[1]), BF16),
        compiler_params=params(),
        name=name,
    )(one_hot, *parts)


def flip(x, bits):
    return lax.ppermute(x, "hid", [(i, i ^ bits) for i in range(16)])


def plus(a, b):
    return a.astype(F32) + b.astype(F32)


def join(*arrays):
    return lax.optimization_barrier(arrays)


def body16(tokens, upstream, loss_mask, gate_weight, up_weight, down_weight):
    tok, width = tokens.shape
    live = tok // 2
    gate_w, up_w = gate_weight.T, up_weight.T
    one_hot, x, g = order_tokens(tokens, upstream, loss_mask)
    z2, z1, y, gz1 = flip(x, 8), flip(x, 4), flip(x, 2), flip(g, 4)
    gz1, y, z1, z2, g = join(gz1, y, z1, z2, g)
    z3, yz1, yz2, gz2 = flip(z2, 4), flip(z1, 2), flip(z2, 2), flip(g, 8)
    gz2, yz2, yz1, z3, g = join(gz2, yz2, yz1, z3, g)
    yz3 = flip(z3, 2)
    most = jnp.stack([x, y, z1, yz1, z2, yz2, z3])
    most_other = flip(most, 1)
    gz3 = flip(g, 12)
    gz3, most_other, yz3 = join(gz3, most_other, yz3)
    g_even = jnp.stack([g, gz1, gz2, gz3])
    g_odd, g_even_other = flip(g_even, 2), flip(g_even, 1)
    x_mine, x_other = (most, yz3[None]), (most_other, flip(yz3, 1)[None])
    x_rows, hidden_t, act, slope, keep_even, keep_odd, send_even, send_odd = forward(
        x_mine, x_other, gate_w, up_w, down_weight, live
    )
    send_odd, g_odd, g_even_other = join(send_odd, g_odd, g_even_other)
    recv_odd, g_odd_other = flip(send_odd, 1), flip(g_odd, 1)
    recv_odd, g_odd_other, send_even = join(recv_odd, g_odd_other, send_even)
    recv_even = flip(send_even, 1)
    out_y = flip(plus(keep_odd, recv_odd).astype(BF16), 2)
    g_rows, d_gate_t, d_up_t, tk, ts = backward(
        (g_even, g_odd), (g_even_other, g_odd_other), act, slope, gate_w, up_w, down_weight
    )
    ts, out_y, recv_even, hidden_t = join(ts, out_y, recv_even, hidden_t)
    rows = [plus(keep_even[k], recv_even[k]) + out_y[k].astype(F32) for k in range(4)]
    t_recv = flip(ts, 1)
    z13 = flip(rows[3].astype(BF16), 4)
    down_grad = weight_grad(hidden_t, g_rows, "down_grad")
    down_grad, z13, t_recv, d_gate_t = join(down_grad, z13, t_recv, d_gate_t)
    z2 = flip((rows[2] + z13.astype(F32)).astype(BF16), 8)
    z1 = flip(rows[1].astype(BF16), 4)
    t_y23 = flip(plus(tk[5::2], t_recv[5::2]).astype(BF16), 2)
    gate_grad = weight_grad(d_gate_t, x_rows, "gate_grad")
    gate_grad, d_up_t, t_y23, t_recv = join(gate_grad, d_up_t, t_y23, t_recv)
    tz13 = flip((plus(tk[6], t_recv[6]) + t_y23[1].astype(F32)).astype(BF16), 4)
    t_y01 = flip(plus(tk[1:4:2], t_recv[1:4:2]).astype(BF16), 2)
    up_grad = weight_grad(d_up_t, x_rows, "up_grad_0", 0, 2)
    up_grad, tz13, t_y01, z2, z1 = join(up_grad, tz13, t_y01, z2, z1)
    tz2 = flip((plus(tk[4], t_recv[4]) + plus(t_y23[0], tz13)).astype(BF16), 8)
    tz1 = flip((plus(tk[2], t_recv[2]) + t_y01[1].astype(F32)).astype(BF16), 4)
    ffn_output = last_sum(one_hot, (rows[0], z2, z1), "ffn_output")
    up_grad = weight_grad(d_up_t, x_rows, "up_grad_1", 2, 2, up_grad)
    up_grad, tz2, tz1 = join(up_grad, tz2, tz1)
    token_grad = last_sum(one_hot[:live], (plus(tk[0], t_recv[0]) + t_y01[0].astype(F32), tz2, tz1), "token_grad")
    return ffn_output, token_grad, gate_grad.T, up_grad.T, down_grad


def body_any(tokens, upstream, loss_mask, gate_weight, up_weight, down_weight):
    masked = upstream * loss_mask[:, None].astype(upstream.dtype)
    tokens = lax.all_gather(tokens, "hid", axis=1, tiled=True)
    grad = lax.all_gather(masked, "hid", axis=1, tiled=True)
    gate_lin = dot(tokens, gate_weight, 1, 0)
    up_lin = dot(tokens, up_weight, 1, 0)
    sig = jax.nn.sigmoid(gate_lin)
    act = gate_lin * sig
    hidden = (act * up_lin).astype(BF16)
    out = lax.psum_scatter(dot(down_weight, hidden, 0, 1), "hid", scatter_dimension=0, tiled=True)
    d_hidden = dot(grad, down_weight, 1, 1)
    d_up = (d_hidden * act).astype(BF16)
    d_gate = (d_hidden * up_lin * sig * (1.0 + gate_lin * (1.0 - sig))).astype(BF16)
    down_grad = dot(hidden, grad, 0, 0).astype(BF16)
    gate_grad = dot(tokens, d_gate, 0, 0).astype(BF16)
    up_grad = dot(tokens, d_up, 0, 0).astype(BF16)
    back = dot(gate_weight, d_gate, 1, 1) + dot(up_weight, d_up, 1, 1)
    back = lax.psum_scatter(back, "hid", scatter_dimension=0, tiled=True)
    return out.T.astype(BF16), back.T.astype(BF16), gate_grad, up_grad, down_grad


def solution(mesh):
    spec = P("groups", "hid")
    in_specs = (spec, spec, P("groups"), P(None, "hid"), P(None, "hid"), P("hid", None))
    out_specs = (spec, spec, spec, spec, P("hid", "groups"))
    body = body16 if mesh.shape["hid"] == 16 else body_any
    return jax.shard_map(body, mesh=mesh, in_specs=in_specs, out_specs=out_specs, check_vma=False)
```

time: 146 us -> 131 us (0.90)
  waiting for transfers between devices: 31.4 us -> 21.9 us
  local copies, waits for them, and re-layouts: 3.02 us -> 1.09 us
  starting transfers between devices: 30.5 us -> 28.8 us
    ppermute x29 -> x27, waiting for transfers between devices: 31.4 us -> 21.9 us  [flip(): return lax.ppermute(x, 'hid', [(i, i ^ bits) for i in range(16)])]
    concatenate x4 -> x0, other arithmetic: 2.31 us -> none  [the longest x1 1.27 us: body16(): x_other = jnp.concatenate([most_other, flip(yz3, 1)[None]])]
    unnamed x34 -> x28, local copies, waits for them, and re-layouts: 2.91 us -> 1.07 us
    ppermute x29 -> x27, starting transfers between devices: 30.5 us -> 28.8 us  [flip(): return lax.ppermute(x, 'hid', [(i, i ^ bits) for i in range(16)])]
    convert_element_type x6 -> x8, other arithmetic: 0.38 us -> 1.96 us  [the longest x1 1.47 us: body16(): out_y = flip(plus(keep_odd, recv_odd).astype(BF16), 2)]
  transfers between devices with their start and end apart: 29 -> 27, of which waited for: 10 -> 7; matrix products, arithmetic and copies ran while one was open for 2% -> 1% of each run, Pallas kernels for 51% -> 56%
where the time goes in v3:
time: 131 us
  Pallas kernels  76.3 us (58%)
  starting transfers between devices  28.8 us (22%)
  waiting for transfers between devices  21.9 us (17%)
  other arithmetic  2.01 us (2%)
    pallas_call x7, Pallas kernels, call(): pl.pallas_call(kernel, in_specs=[pl.BlockSpec(memory_space=pl.ANY)] * len...  74.5 us
    ppermute x27, starting transfers between devices, flip(): return lax.ppermute(x, 'hid', [(i, i ^ bits) for i in range(16)])  28.8 us
    ppermute x27, waiting for transfers between devices, flip(): return lax.ppermute(x, 'hid', [(i, i ^ bits) for i in range(16)])  21.9 us
  transfers between devices with their start and end apart: 27, of which 7 were waited for; matrix products, arithmetic and copies ran while one was open for 1% of the time, Pallas kernels for 56%

profile of v3, /device:TPU:0, one launch (start us, length us, event | category | flops | bytes accessed | tf_op | source)
XLA Modules:
  0.0 131.1 jit_solution(4887954752825272717)
XLA Ops:
  0.6 2.2 %order_tokens.1 = (bf16[256,256]{1,0:T(8,128)(2,1)}, bf16[384,256]{1,0:T(8,128)(2,1)}, bf16[384,128]{1,0:T(8,128)(2,1)}) custom-call(s32[1,256]{1,0:T(1,128)} %bitcast.58, bf16[256,384]{1,0:T(8,128)(2,1)} %tokens_ref.1, bf16[256,384]{1,0:T(8,128)(2,1)} %upstream_ref.1), custom_call_target="tpu_custom_call" | custom-call | flops 75497472 | bytes 786432 | tf_op jit(solution)/shard_map/order_tokens/pallas_call | solution.py:33
  2.8 4.1 %collective-permute-start.3 = (bf16[384,256]{1,0:T(8,128)(2,1)}, bf16[384,256]{1,0:T(8,128)(2,1)S(1)}, u32[]{:S(2)}, u32[]{:S(2)}) collective-permute-start(bf16[384,256]{1,0:T(8,128)(2,1)} %get-tuple-element.61), channel_id=1, source_target_pairs={{0,8},{1,9},{2,10},{3,11},{4,12},{5,13},{6,14},{7,15},{8,0},{9,1},... | collective-permute-start | bytes 589832 | tf_op jit(solution)/shard_map/ppermute | solution.py:494
  6.9 1.6 %collective-permute-start.2 = (bf16[384,256]{1,0:T(8,128)(2,1)}, bf16[384,256]{1,0:T(8,128)(2,1)S(1)}, u32[]{:S(2)}, u32[]{:S(2)}) collective-permute-start(bf16[384,256]{1,0:T(8,128)(2,1)} %get-tuple-element.61), channel_id=1, source_target_pairs={{0,4},{1,5},{2,6},{3,7},{4,0},{5,1},{6,2},{7,3},{8,12},{9,13},{10,... | collective-permute-start | bytes 589832 | tf_op jit(solution)/shard_map/ppermute | solution.py:494
  8.5 1.5 %collective-permute-start.1 = (bf16[384,256]{1,0:T(8,128)(2,1)}, bf16[384,256]{1,0:T(8,128)(2,1)S(1)}, u32[]{:S(2)}, u32[]{:S(2)}) collective-permute-start(bf16[384,256]{1,0:T(8,128)(2,1)} %get-tuple-element.61), channel_id=1, source_target_pairs={{0,2},{1,3},{2,0},{3,1},{4,6},{5,7},{6,4},{7,5},{8,10},{9,11},{10,... | collective-permute-start | bytes 589832 | tf_op jit(solution)/shard_map/ppermute | solution.py:494
  11.4 7.2 %collective-permute-done = bf16[384,128]{1,0:T(8,128)(2,1)S(1)} collective-permute-done((bf16[384,128]{1,0:T(8,128)(2,1)}, bf16[384,128]{1,0:T(8,128)(2,1)S(1)}, u32[]{:S(2)}, u32[]{:S(2)}) %collective-permute-start) | collective-permute-done | bytes 98336 | tf_op jit(solution)/shard_map/ppermute | solution.py:494
  18.6 1.6 %collective-permute-start.7 = (bf16[384,256]{1,0:T(8,128)(2,1)S(1)}, bf16[384,256]{1,0:T(8,128)(2,1)S(1)}, u32[]{:S(2)}, u32[]{:S(2)}) collective-permute-start(bf16[384,256]{1,0:T(8,128)(2,1)S(1)} %collective-permute-done.3), channel_id=1, source_target_pairs={{0,4},{1,5},{2,6},{3,7},{4,0},{5,1},{6,2},{7,3},{8,12},{9,13},{10,... | collective-permute-start | bytes 589832 | tf_op jit(solution)/shard_map/ppermute | solution.py:494
  20.2 1.5 %collective-permute-start.5 = (bf16[384,256]{1,0:T(8,128)(2,1)S(1)}, bf16[384,256]{1,0:T(8,128)(2,1)S(1)}, u32[]{:S(2)}, u32[]{:S(2)}) collective-permute-start(bf16[384,256]{1,0:T(8,128)(2,1)S(1)} %collective-permute-done.3), channel_id=1, source_target_pairs={{0,2},{1,3},{2,0},{3,1},{4,6},{5,7},{6,4},{7,5},{8,10},{9,11},{10,... | collective-permute-start | bytes 589832 | tf_op jit(solution)/shard_map/ppermute | solution.py:494
  21.7 1.6 %collective-permute-start.4 = (bf16[384,128]{1,0:T(8,128)(2,1)}, bf16[384,128]{1,0:T(8,128)(2,1)S(1)}, u32[]{:S(2)}, u32[]{:S(2)}) collective-permute-start(bf16[384,128]{1,0:T(8,128)(2,1)} %get-tuple-element.70), channel_id=1, source_target_pairs={{0,8},{1,9},{2,10},{3,11},{4,12},{5,13},{6,14},{7,15},{8,0},{9,1},... | collective-permute-start | bytes 294920 | tf_op jit(solution)/shard_map/ppermute | solution.py:494
  23.9 4.6 %collective-permute-done.4 = bf16[384,128]{1,0:T(8,128)(2,1)S(1)} collective-permute-done((bf16[384,128]{1,0:T(8,128)(2,1)}, bf16[384,128]{1,0:T(8,128)(2,1)S(1)}, u32[]{:S(2)}, u32[]{:S(2)}) %collective-permute-start.4) | collective-permute-done | bytes 98336 | tf_op jit(solution)/shard_map/ppermute | solution.py:494
  28.5 1.5 %collective-permute-done.6 = bf16[384,256]{1,0:T(8,128)(2,1)S(1)} collective-permute-done((bf16[384,256]{1,0:T(8,128)(2,1)S(1)}, bf16[384,256]{1,0:T(8,128)(2,1)S(1)}, u32[]{:S(2)}, u32[]{:S(2)}) %collective-permute-start.6) | collective-permute-done | bytes 196640 | tf_op jit(solution)/shard_map/ppermute | solution.py:494
  30.2 1.5 %collective-permute-start.10 = (bf16[384,256]{1,0:T(8,128)(2,1)S(1)}, bf16[384,256]{1,0:T(8,128)(2,1)S(1)}, u32[]{:S(2)}, u32[]{:S(2)}) collective-permute-start(bf16[384,256]{1,0:T(8,128)(2,1)S(1)} %collective-permute-done.7), channel_id=1, source_target_pairs={{0,2},{1,3},{2,0},{3,1},{4,6},{5,7},{6,4},{7,5},{8,10},{9,11},{10,... | collective-permute-start | bytes 589832 | tf_op jit(solution)/shard_map/ppermute | solution.py:494
  33.1 5.4 %collective-permute-done.8 = bf16[384,128]{1,0:T(8,128)(2,1)S(1)} collective-permute-done((bf16[384,128]{1,0:T(8,128)(2,1)S(1)}, bf16[384,128]{1,0:T(8,128)(2,1)S(1)}, u32[]{:S(2)}, u32[]{:S(2)}) %collective-permute-start.8) | collective-permute-done | bytes 98336 | tf_op jit(solution)/shard_map/ppermute | solution.py:494
  40.0 22.7 %forward.1 = (bf16[4,1536,128]{2,1,0:T(8,128)(2,1)}, bf16[1472,128]{1,0:T(8,128)(2,1)S(1)}, f32[1472,128]{1,0:T(8,128)S(1)}, f32[1472,128]{1,0:T(8,128)}, f32[4,...) custom-call(bf16[7,384,256]{2,1,0:T(8,128)(2,1)} %copy-done.4, ...), custom_call_target="tpu_custom_call" | custom-call | flops 13891534848 | bytes 54263808 | tf_op jit(solution)/shard_map/forward/pallas_call | solution.py:33
  63.3 2.3 %collective-permute-done.15.other_odd = bf16[4,384,128]{2,1,0:T(8,128)(2,1)S(1)} collective-permute-done((bf16[4,384,128]{2,1,0:T(8,128)(2,1)S(1)}, bf16[4,384,128]{2,1,0:T(8,128)(2,1)S(1)}, u32[]{:S(2)}, u32[]{:S(2)}) %collective-permute-start.15) | collective-permute-done | bytes 393248 | tf_op jit(solution)/shard_map/ppermute | solution.py:494
  65.7 1.5 %add_convert_fusion = bf16[4,256,384]{2,1,0:T(8,128)(2,1)S(1)} fusion(bf16[4,256,384]{2,1,0:T(8,128)(2,1)S(1)} %collective-permute-done.14, bf16[4,256,384]{2,1,0:T(8,128)(2,1)} %get-tuple-element.86), kind=kLoop, calls=%fused_computation | loop fusion | flops 1572864 | bytes 2359296 | tf_op jit(solution)/shard_map/convert_element_type | solution.py:529
  68.5 22.7 %backward.1 = (bf16[4,1536,128]{2,1,0:T(8,128)(2,1)}, bf16[1472,128]{1,0:T(8,128)(2,1)S(1)}, bf16[1472,128]{1,0:T(8,128)(2,1)S(1)}, f32[8,128,384]{2,1,0:T(8,128)}, bf16[8,128,384]{2,1,0:T(8,128)(2,1)}) custom-call(bf16[4,384,128]{2,1,0:T(8,128)(2,1)S(1)} %pad_maximum_fusion.mine, bf16[4,384,128]{2,1,0:T(8,128)(2,1)S(1)} %collective-permute-done.12.mine_odd, ...), custom_call_target="tpu_custom_call" | custom-call | flops 6945767424 | bytes 54263808 | tf_op jit(solution)/shard_map/backward/pallas_call | solution.py:33
  92.2 1.8 %collective-permute-start.18 = (bf16[256,384]{1,0:T(8,128)(2,1)S(1)}, bf16[256,384]{1,0:T(8,128)(2,1)S(1)}, u32[]{:S(2)}, u32[]{:S(2)}) collective-permute-start(bf16[256,384]{1,0:T(8,128)(2,1)S(1)} %get-tuple-element.116), channel_id=1, source_target_pairs={{0,4},{1,5},{2,6},{3,7},{4,0},{5,1},{6,2},{7,3},{8,12},{9,13},{10,... | collective-permute-start | bytes 589832 | tf_op jit(solution)/shard_map/ppermute | solution.py:494
  94.0 8.5 %down_grad.1 = bf16[1472,6144]{1,0:T(8,128)(2,1)} custom-call(bf16[1472,128]{1,0:T(8,128)(2,1)S(1)} %get-tuple-element.92.hid_ref, bf16[4,1536,128]{2,1,0:T(8,128)(2,1)S(1)} %copy-done.1), custom_call_target="tpu_custom_call" | custom-call | flops 2315255808 | bytes 18087936 | tf_op jit(solution)/shard_map/down_grad/pallas_call | solution.py:33
  104.1 1.7 %collective-permute-start.23 = (bf16[256,384]{1,0:T(8,128)(2,1)S(1)}, bf16[256,384]{1,0:T(8,128)(2,1)S(1)}, u32[]{:S(2)}, u32[]{:S(2)}) collective-permute-start(bf16[256,384]{1,0:T(8,128)(2,1)S(1)} %fusion), channel_id=1, source_target_pairs={{0,8},{1,9},{2,10},{3,11},{4,12},{5,13},{6,14},{7,15},{8,0},{9,1},... | collective-permute-start | bytes 589832 | tf_op jit(solution)/shard_map/ppermute | solution.py:494
  105.8 8.5 %gate_grad.1 = bf16[1472,6144]{1,0:T(8,128)(2,1)} custom-call(bf16[1472,128]{1,0:T(8,128)(2,1)S(1)} %get-tuple-element.96.hid_ref, bf16[4,1536,128]{2,1,0:T(8,128)(2,1)S(1)} %copy-done), custom_call_target="tpu_custom_call" | custom-call | flops 2315255808 | bytes 18087936 | tf_op jit(solution)/shard_map/gate_grad/pallas_call | solution.py:33
  116.0 5.0 %up_grad_0.1.refs_0_ = bf16[1472,6144]{1,0:T(8,128)(2,1)} custom-call(bf16[1472,128]{1,0:T(8,128)(2,1)S(1)} %get-tuple-element.101.hid_ref, bf16[4,1536,128]{2,1,0:T(8,128)(2,1)S(1)} %copy-done), custom_call_target="tpu_custom_call" | custom-call | flops 1157627904 | bytes 9043968 | tf_op jit(solution)/shard_map/up_grad_0/pallas_call | solution.py:33
  121.1 1.6 %collective-permute-start.26 = (bf16[128,384]{1,0:T(8,128)(2,1)S(1)}, bf16[128,384]{1,0:T(8,128)(2,1)S(1)}, u32[]{:S(2)}, u32[]{:S(2)}) collective-permute-start(bf16[128,384]{1,0:T(8,128)(2,1)S(1)} %get-tuple-element.118), channel_id=1, source_target_pairs={{0,4},{1,5},{2,6},{3,7},{4,0},{5,1},{6,2},{7,3},{8,12},{9,13},{10,... | collective-permute-start | bytes 294920 | tf_op jit(solution)/shard_map/ppermute | solution.py:494
  122.7 1.5 %collective-permute-start.25 = (bf16[128,384]{1,0:T(8,128)(2,1)S(1)}, bf16[128,384]{1,0:T(8,128)(2,1)S(1)}, u32[]{:S(2)}, u32[]{:S(2)}) collective-permute-start(bf16[128,384]{1,0:T(8,128)(2,1)S(1)} %fusion.4), channel_id=1, source_target_pairs={{0,8},{1,9},{2,10},{3,11},{4,12},{5,13},{6,14},{7,15},{8,0},{9,1},... | collective-permute-start | bytes 294920 | tf_op jit(solution)/shard_map/ppermute | solution.py:494
  125.1 5.0 %up_grad_1.1 = bf16[1472,6144]{1,0:T(8,128)(2,1)} custom-call(bf16[1472,128]{1,0:T(8,128)(2,1)S(1)} %get-tuple-element.101.hid_ref, bf16[4,1536,128]{2,1,0:T(8,128)(2,1)S(1)} %copy-done, bf16[1472,6144]{1,0:T(8,128)(2,1)} %up_grad_0.1.refs_0_), custom_call_target="tpu_custom_call", output_to_operand_aliasing={{}: (2, {})} | custom-call | flops 1157627904 | bytes 9043968 | tf_op jit(solution)/shard_map/up_grad_1/pallas_call | solution.py:33
  (78 shorter events, 13.1 us)
Async XLA Ops:
  2.8 15.8 %collective-permute-start.3 = (bf16[384,256]{1,0:T(8,128)(2,1)}, bf16[384,256]{1,0:T(8,128)(2,1)S(1)}, u32[]{:S(2)}, u32[]{:S(2)}) collective-permute-start(bf16[384,256]{1,0:T(8,128)(2,1)} %get-tuple-element.61), channel_id=1, source_target_pairs={{0,8},{1,9},{2,10},{3,11},{4,12},{5,13},{6,14},{7,15},{8,0},{9,1},... | collective-permute-start | bytes 589832 | tf_op jit(solution)/shard_map/ppermute | solution.py:494
  6.9 11.7 %collective-permute-start.2 = (bf16[384,256]{1,0:T(8,128)(2,1)}, bf16[384,256]{1,0:T(8,128)(2,1)S(1)}, u32[]{:S(2)}, u32[]{:S(2)}) collective-permute-start(bf16[384,256]{1,0:T(8,128)(2,1)} %get-tuple-element.61), channel_id=1, source_target_pairs={{0,4},{1,5},{2,6},{3,7},{4,0},{5,1},{6,2},{7,3},{8,12},{9,13},{10,... | collective-permute-start | bytes 589832 | tf_op jit(solution)/shard_map/ppermute | solution.py:494
  8.5 10.2 %collective-permute-start.1 = (bf16[384,256]{1,0:T(8,128)(2,1)}, bf16[384,256]{1,0:T(8,128)(2,1)S(1)}, u32[]{:S(2)}, u32[]{:S(2)}) collective-permute-start(bf16[384,256]{1,0:T(8,128)(2,1)} %get-tuple-element.61), channel_id=1, source_target_pairs={{0,2},{1,3},{2,0},{3,1},{4,6},{5,7},{6,4},{7,5},{8,10},{9,11},{10,... | collective-permute-start | bytes 589832 | tf_op jit(solution)/shard_map/ppermute | solution.py:494
  10.0 8.6 %collective-permute-start = (bf16[384,128]{1,0:T(8,128)(2,1)}, bf16[384,128]{1,0:T(8,128)(2,1)S(1)}, u32[]{:S(2)}, u32[]{:S(2)}) collective-permute-start(bf16[384,128]{1,0:T(8,128)(2,1)} %get-tuple-element.70), channel_id=1, source_target_pairs={{0,4},{1,5},{2,6},{3,7},{4,0},{5,1},{6,2},{7,3},{8,12},{9,13},{10,... | collective-permute-start | bytes 294920 | tf_op jit(solution)/shard_map/ppermute | solution.py:494
  18.6 11.4 %collective-permute-start.7 = (bf16[384,256]{1,0:T(8,128)(2,1)S(1)}, bf16[384,256]{1,0:T(8,128)(2,1)S(1)}, u32[]{:S(2)}, u32[]{:S(2)}) collective-permute-start(bf16[384,256]{1,0:T(8,128)(2,1)S(1)} %collective-permute-done.3), channel_id=1, source_target_pairs={{0,4},{1,5},{2,6},{3,7},{4,0},{5,1},{6,2},{7,3},{8,12},{9,13},{10,... | collective-permute-start | bytes 589832 | tf_op jit(solution)/shard_map/ppermute | solution.py:494
  20.2 9.8 %collective-permute-start.5 = (bf16[384,256]{1,0:T(8,128)(2,1)S(1)}, bf16[384,256]{1,0:T(8,128)(2,1)S(1)}, u32[]{:S(2)}, u32[]{:S(2)}) collective-permute-start(bf16[384,256]{1,0:T(8,128)(2,1)S(1)} %collective-permute-done.3), channel_id=1, source_target_pairs={{0,2},{1,3},{2,0},{3,1},{4,6},{5,7},{6,4},{7,5},{8,10},{9,11},{10,... | collective-permute-start | bytes 589832 | tf_op jit(solution)/shard_map/ppermute | solution.py:494
  21.7 6.8 %collective-permute-start.4 = (bf16[384,128]{1,0:T(8,128)(2,1)}, bf16[384,128]{1,0:T(8,128)(2,1)S(1)}, u32[]{:S(2)}, u32[]{:S(2)}) collective-permute-start(bf16[384,128]{1,0:T(8,128)(2,1)} %get-tuple-element.70), channel_id=1, source_target_pairs={{0,8},{1,9},{2,10},{3,11},{4,12},{5,13},{6,14},{7,15},{8,0},{9,1},... | collective-permute-start | bytes 294920 | tf_op jit(solution)/shard_map/ppermute | solution.py:494
  23.3 6.7 %collective-permute-start.6 = (bf16[384,256]{1,0:T(8,128)(2,1)S(1)}, bf16[384,256]{1,0:T(8,128)(2,1)S(1)}, u32[]{:S(2)}, u32[]{:S(2)}) collective-permute-start(bf16[384,256]{1,0:T(8,128)(2,1)S(1)} %collective-permute-done.2), channel_id=1, source_target_pairs={{0,2},{1,3},{2,0},{3,1},{4,6},{5,7},{6,4},{7,5},{8,10},{9,11},{10,... | collective-permute-start | bytes 589832 | tf_op jit(solution)/shard_map/ppermute | solution.py:494
  30.1 8.3 %collective-permute-start.9 = (bf16[7,384,256]{2,1,0:T(8,128)(2,1)S(1)}, bf16[7,384,256]{2,1,0:T(8,128)(2,1)S(1)}, u32[]{:S(2)}, u32[]{:S(2)}) collective-permute-start(bf16[7,384,256]{2,1,0:T(8,128)(2,1)S(1)} %bitcast_dynamic-update-slice_fusion.mine), channel_id=1, source_target_pairs={{0,1},{1,0},{2,3},{3,2},{4,5},{5,4},{6,7},{7,6},{8,9},{9,8},{10,11... | collective-permute-start | bytes 4128776 | tf_op jit(solution)/shard_map/ppermute | solution.py:494
  30.2 8.3 %collective-permute-start.10 = (bf16[384,256]{1,0:T(8,128)(2,1)S(1)}, bf16[384,256]{1,0:T(8,128)(2,1)S(1)}, u32[]{:S(2)}, u32[]{:S(2)}) collective-permute-start(bf16[384,256]{1,0:T(8,128)(2,1)S(1)} %collective-permute-done.7), channel_id=1, source_target_pairs={{0,2},{1,3},{2,0},{3,1},{4,6},{5,7},{6,4},{7,5},{8,10},{9,11},{10,... | collective-permute-start | bytes 589832 | tf_op jit(solution)/shard_map/ppermute | solution.py:494
  31.7 6.8 %collective-permute-start.8 = (bf16[384,128]{1,0:T(8,128)(2,1)S(1)}, bf16[384,128]{1,0:T(8,128)(2,1)S(1)}, u32[]{:S(2)}, u32[]{:S(2)}) collective-permute-start(bf16[384,128]{1,0:T(8,128)(2,1)S(1)} %copy-done.9), channel_id=1, source_target_pairs={{0,12},{1,13},{2,14},{3,15},{4,8},{5,9},{6,10},{7,11},{8,4},{9,5},... | collective-permute-start | bytes 294920 | tf_op jit(solution)/shard_map/ppermute | solution.py:494
  38.6 24.1 %collective-permute-start.13 = (bf16[4,384,128]{2,1,0:T(8,128)(2,1)S(1)}, bf16[4,384,128]{2,1,0:T(8,128)(2,1)S(1)}, u32[]{:S(2)}, u32[]{:S(2)}) collective-permute-start(bf16[4,384,128]{2,1,0:T(8,128)(2,1)S(1)} %pad_maximum_fusion.mine), channel_id=1, source_target_pairs={{0,1},{1,0},{2,3},{3,2},{4,5},{5,4},{6,7},{7,6},{8,9},{9,8},{10,11... | collective-permute-start | bytes 1179656 | tf_op jit(solution)/shard_map/ppermute | solution.py:494
  39.1 23.6 %collective-permute-start.12 = (bf16[4,384,128]{2,1,0:T(8,128)(2,1)S(1)}, bf16[4,384,128]{2,1,0:T(8,128)(2,1)S(1)}, u32[]{:S(2)}, u32[]{:S(2)}) collective-permute-start(bf16[4,384,128]{2,1,0:T(8,128)(2,1)S(1)} %pad_maximum_fusion.mine), channel_id=1, source_target_pairs={{0,2},{1,3},{2,0},{3,1},{4,6},{5,7},{6,4},{7,5},{8,10},{9,11},{10,... | collective-permute-start | bytes 1179656 | tf_op jit(solution)/shard_map/ppermute | solution.py:494
  67.1 24.0 %collective-permute-start.16 = (bf16[4,256,384]{2,1,0:T(8,128)(2,1)S(1)}, bf16[4,256,384]{2,1,0:T(8,128)(2,1)S(1)}, u32[]{:S(2)}, u32[]{:S(2)}) collective-permute-start(bf16[4,256,384]{2,1,0:T(8,128)(2,1)S(1)} %add_convert_fusion), channel_id=1, source_target_pairs={{0,2},{1,3},{2,0},{3,1},{4,6},{5,7},{6,4},{7,5},{8,10},{9,11},{10,... | collective-permute-start | bytes 2359304 | tf_op jit(solution)/shard_map/ppermute | solution.py:494
  68.4 22.7 %collective-permute-start.17 = (bf16[4,256,384]{2,1,0:T(8,128)(2,1)S(1)}, bf16[4,256,384]{2,1,0:T(8,128)(2,1)S(1)}, u32[]{:S(2)}, u32[]{:S(2)}) collective-permute-start(bf16[4,256,384]{2,1,0:T(8,128)(2,1)S(1)} %copy-done.10), channel_id=1, source_target_pairs={{0,1},{1,0},{2,3},{3,2},{4,5},{5,4},{6,7},{7,6},{8,9},{9,8},{10,11... | collective-permute-start | bytes 2359304 | tf_op jit(solution)/shard_map/ppermute | solution.py:494
  91.2 11.9 %collective-permute-start.19 = (bf16[8,128,384]{2,1,0:T(8,128)(2,1)}, bf16[8,128,384]{2,1,0:T(8,128)(2,1)S(1)}, u32[]{:S(2)}, u32[]{:S(2)}) collective-permute-start(bf16[8,128,384]{2,1,0:T(8,128)(2,1)} %get-tuple-element.94), channel_id=1, source_target_pairs={{0,1},{1,0},{2,3},{3,2},{4,5},{5,4},{6,7},{7,6},{8,9},{9,8},{10,11... | collective-permute-start | bytes 2359304 | tf_op jit(solution)/shard_map/ppermute | solution.py:494
  91.9 29.0 %collective-permute-start.24 = (bf16[256,384]{1,0:T(8,128)(2,1)S(1)}, bf16[256,384]{1,0:T(8,128)(2,1)S(1)}, u32[]{:S(2)}, u32[]{:S(2)}) collective-permute-start(bf16[256,384]{1,0:T(8,128)(2,1)S(1)} %get-tuple-element.115), channel_id=1, source_target_pairs={{0,4},{1,5},{2,6},{3,7},{4,0},{5,1},{6,2},{7,3},{8,12},{9,13},{10,... | collective-permute-start | bytes 589832 | tf_op jit(solution)/shard_map/ppermute | solution.py:494
  92.2 10.9 %collective-permute-start.18 = (bf16[256,384]{1,0:T(8,128)(2,1)S(1)}, bf16[256,384]{1,0:T(8,128)(2,1)S(1)}, u32[]{:S(2)}, u32[]{:S(2)}) collective-permute-start(bf16[256,384]{1,0:T(8,128)(2,1)S(1)} %get-tuple-element.116), channel_id=1, source_target_pairs={{0,4},{1,5},{2,6},{3,7},{4,0},{5,1},{6,2},{7,3},{8,12},{9,13},{10,... | collective-permute-start | bytes 589832 | tf_op jit(solution)/shard_map/ppermute | solution.py:494
  103.2 11.0 %collective-permute-start.20 = (bf16[2,128,384]{2,1,0:T(8,128)(2,1)S(1)}, bf16[2,128,384]{2,1,0:T(8,128)(2,1)S(1)}, u32[]{:S(2)}, u32[]{:S(2)}) collective-permute-start(bf16[2,128,384]{2,1,0:T(8,128)(2,1)S(1)} %add_convert_fusion.3), channel_id=1, source_target_pairs={{0,2},{1,3},{2,0},{3,1},{4,6},{5,7},{6,4},{7,5},{8,10},{9,11},{10,... | collective-permute-start | bytes 589832 | tf_op jit(solution)/shard_map/ppermute | solution.py:494
  104.1 16.9 %collective-permute-start.23 = (bf16[256,384]{1,0:T(8,128)(2,1)S(1)}, bf16[256,384]{1,0:T(8,128)(2,1)S(1)}, u32[]{:S(2)}, u32[]{:S(2)}) collective-permute-start(bf16[256,384]{1,0:T(8,128)(2,1)S(1)} %fusion), channel_id=1, source_target_pairs={{0,8},{1,9},{2,10},{3,11},{4,12},{5,13},{6,14},{7,15},{8,0},{9,1},... | collective-permute-start | bytes 589832 | tf_op jit(solution)/shard_map/ppermute | solution.py:494
  114.3 6.7 %collective-permute-start.22 = (bf16[2,128,384]{2,1,0:T(8,128)(2,1)S(1)}, bf16[2,128,384]{2,1,0:T(8,128)(2,1)S(1)}, u32[]{:S(2)}, u32[]{:S(2)}) collective-permute-start(bf16[2,128,384]{2,1,0:T(8,128)(2,1)S(1)} %add_convert_fusion.2), channel_id=1, source_target_pairs={{0,2},{1,3},{2,0},{3,1},{4,6},{5,7},{6,4},{7,5},{8,10},{9,11},{10,... | collective-permute-start | bytes 589832 | tf_op jit(solution)/shard_map/ppermute | solution.py:494
  115.4 5.6 %collective-permute-start.21 = (bf16[128,384]{1,0:T(8,128)(2,1)S(1)}, bf16[128,384]{1,0:T(8,128)(2,1)S(1)}, u32[]{:S(2)}, u32[]{:S(2)}) collective-permute-start(bf16[128,384]{1,0:T(8,128)(2,1)S(1)} %fusion.5), channel_id=1, source_target_pairs={{0,4},{1,5},{2,6},{3,7},{4,0},{5,1},{6,2},{7,3},{8,12},{9,13},{10,... | collective-permute-start | bytes 294920 | tf_op jit(solution)/shard_map/ppermute | solution.py:494
  121.1 9.0 %collective-permute-start.26 = (bf16[128,384]{1,0:T(8,128)(2,1)S(1)}, bf16[128,384]{1,0:T(8,128)(2,1)S(1)}, u32[]{:S(2)}, u32[]{:S(2)}) collective-permute-start(bf16[128,384]{1,0:T(8,128)(2,1)S(1)} %get-tuple-element.118), channel_id=1, source_target_pairs={{0,4},{1,5},{2,6},{3,7},{4,0},{5,1},{6,2},{7,3},{8,12},{9,13},{10,... | collective-permute-start | bytes 294920 | tf_op jit(solution)/shard_map/ppermute | solution.py:494
  122.7 7.5 %collective-permute-start.25 = (bf16[128,384]{1,0:T(8,128)(2,1)S(1)}, bf16[128,384]{1,0:T(8,128)(2,1)S(1)}, u32[]{:S(2)}, u32[]{:S(2)}) collective-permute-start(bf16[128,384]{1,0:T(8,128)(2,1)S(1)} %fusion.4), channel_id=1, source_target_pairs={{0,8},{1,9},{2,10},{3,11},{4,12},{5,13},{6,14},{7,15},{8,0},{9,1},... | collective-permute-start | bytes 294920 | tf_op jit(solution)/shard_map/ppermute | solution.py:494
  (14 other events, 115.7 us)

commit v4 on v3

--- a/solution.py
+++ b/solution.py
@@ -29,14 +29,13 @@
     return pl.ds(pl.multiple_of(chip * (2 * width), 2 * width), 2 * width)
 
 
-def call(kernel, name, operands, outs, scratch, flops, nbytes, alias=None, vmem=VMEM_BYTES):
+def call(kernel, name, operands, outs, scratch, flops, nbytes, vmem=VMEM_BYTES):
     return pl.pallas_call(
         kernel,
         in_specs=[pl.BlockSpec(memory_space=pl.ANY)] * len(operands),
         out_specs=[pl.BlockSpec(memory_space=pl.ANY)] * len(outs),
         out_shape=[jax.ShapeDtypeStruct(shape, kind) for shape, kind in outs],
         scratch_shapes=scratch,
-        input_output_aliases={} if alias is None else {alias: 0},
         compiler_params=pltpu.CompilerParams(vmem_limit_bytes=vmem),
         cost_estimate=pl.CostEstimate(flops=flops, bytes_accessed=nbytes, transcendentals=0),
         name=name,
@@ -168,17 +167,19 @@
     return [(even, odd)[k % 2].at[k // 2] for k in range(2 * even.shape[0])]
 
 
-def piece_copies(sems, total, rounded, keep_ref, send_ref):
-    rows, _, wide = total.shape
-    width = wide // 4
+def part_copies(j, total, rounded, outs, sems):
+    width = total.shape[2] // 4
     in_row = lax.axis_index("hid") % 4
-    pairs = []
-    for row in range(rows):
-        for side in range(2):
-            at = [pl.ds(pl.multiple_of((in_row ^ (2 * side + i)) * width, width), width) for i in range(2)]
-            pairs.append((total.at[row, :, at[0]], keep_ref.at[2 * row + side]))
-            pairs.append((rounded.at[row, :, at[1]], send_ref.at[2 * row + side]))
-    return copies(sems, *pairs)
+    keep_even, keep_odd, send_even, send_odd = outs
+    made = []
+    for i, (src, dst) in enumerate(((total, keep_even), (rounded, send_even), (rounded, keep_odd), (rounded, send_odd))):
+        at = pl.ds(pl.multiple_of((in_row ^ i) * width, width), width)
+        made.append(pltpu.make_async_copy(src.at[j, :, at], dst.at[j], sems.at[4 * j + i]))
+    return made
+
+
+def part_outs(rows, tok, width):
+    return [((rows, tok, width), F32)] + 3 * [((rows, tok, width), BF16)]
 
 
 def start_gate_up(gate_w, up_w, base, j, buffer, sem):
@@ -201,7 +202,7 @@
 def forward_kernel(
     mine, mine_last, other, other_last, gate_w, up_w, down_w, x_ref, hidden_t_ref, act_ref, slope_ref, *rest
 ):
-    keep_even, keep_odd, send_even, send_odd = rest[:4]
+    parts = rest[:4]
     x, w, acc, hidden_v, hidden_t_v, act_v, slope_v, total, rounded, sems, x_sems, w_sems, out_sems = rest[4:]
     slots = w.shape[0]
     rows = x.shape[0]
@@ -255,20 +256,6 @@
     hidden_v[...] = hidden.T
     out += copies(sems.at[pl.ds(1, 3)], (hidden_t_v, hidden_t_ref), (act_v, act_ref), (slope_v, slope_ref))
 
-    wide = x.shape[1]
-    width = wide // 4
-    in_row = lax.axis_index("hid") % 4
-    at = [pl.ds(pl.multiple_of((in_row ^ i) * width, width), width) for i in range(4)]
-
-    def out_copies(j):
-        pairs = (
-            (rounded.at[j, :, at[3]], send_odd.at[j]),
-            (rounded.at[j, :, at[2]], keep_odd.at[j]),
-            (rounded.at[j, :, at[1]], send_even.at[j]),
-            (total.at[j, :, at[0]], keep_even.at[j]),
-        )
-        return [pltpu.make_async_copy(src, dst, out_sems.at[4 * j + i]) for i, (src, dst) in enumerate(pairs)]
-
     def two(j):
         slot = j % slots
         wait_block(down_w, w.at[slot], w_sems.at[slot])
@@ -280,12 +267,12 @@
         part = dot(hidden_v[...], w[slot], 1, 0)
         total[j] = part
         rounded[j] = part.astype(BF16)
-        for c in out_copies(j):
+        for c in part_copies(j, total, rounded, parts, out_sems):
             c.start()
 
     each(rows, two)
     for j in range(rows):
-        wait_all(out_copies(j))
+        wait_all(part_copies(j, total, rounded, parts, out_sems))
     wait_all(out)
 
 
@@ -303,10 +290,7 @@
             ((ff, live), BF16),
             ((ff, live), F32),
             ((ff, live), F32),
-            ((rows, tok, width), F32),
-            ((rows, tok, width), BF16),
-            ((rows, tok, width), BF16),
-            ((rows, tok, width), BF16),
+            *part_outs(rows, tok, width),
         ],
         [
             pltpu.VMEM((rows, 4 * width, tok), BF16),
@@ -325,13 +309,15 @@
         ],
         12 * chips * width * ff * tok,
         12 * chips * width * ff,
+        vmem=48 * 1024 * 1024,
     )
 
 
 def backward_kernel(
     mine, mine_odd, other, other_odd, act_ref, slope_ref, gate_w, up_w, down_w, g_ref, d_gate_ref, d_up_ref, *rest
 ):
-    keep_ref, send_ref, g, act, slope, w, acc, *rest = rest
+    parts = rest[:4]
+    g, act, slope, w, acc, *rest = rest[4:]
     d_hid, d_hid_t, total, rounded, sems, g_sems, w_sems, out_sems = rest
     slots = w.shape[0]
     rows = g.shape[0]
@@ -388,8 +374,15 @@
         total[j // 2] = part
         rounded[j // 2] = part.astype(BF16)
 
+        @pl.when(j % 2 == 1)
+        def _():
+            for c in part_copies(j // 2, total, rounded, parts, out_sems):
+                c.start()
+
     each(steps, two)
-    wait_all(out + piece_copies(out_sems, total, rounded, keep_ref, send_ref))
+    for j in range(rows):
+        wait_all(part_copies(j, total, rounded, parts, out_sems))
+    wait_all(out)
 
 
 def backward(mine, other, act, slope, gate_w, up_w, down_w):
@@ -402,7 +395,7 @@
         backward_kernel,
         "backward",
         (*mine, *other, act, slope, gate_w, up_w, down_w),
-        [((rows, 4 * width, live), BF16), d_hid_t, d_hid_t, ((chips, live, width), F32), ((chips, live, width), BF16)],
+        [((rows, 4 * width, live), BF16), d_hid_t, d_hid_t, *part_outs(rows, live, width)],
         [
             pltpu.VMEM((rows, 4 * width, live), BF16),
             pltpu.VMEM((ff, live), F32),
@@ -420,18 +413,18 @@
         ],
         6 * live * down_w.size,
         6 * down_w.size,
+        vmem=32 * 1024 * 1024,
     )
 
 
-def weight_grad_kernel(base, hid_ref, x_ref, *refs):
-    out_ref, hid, x, out_v, sems, out_sems = refs[-6:]
+def weight_grad_kernel(hid_ref, x_ref, out_ref, hid, x, out_v, sems, out_sems):
     steps = out_v.shape[0]
     rows, wide, _ = x.shape
     half = wide // 2
-    ready = copies(sems, (hid_ref, hid), *[(x_ref.at[base + row], x.at[row]) for row in range(rows)])
+    ready = copies(sems, (hid_ref, hid), *[(x_ref.at[row], x.at[row]) for row in range(rows)])
 
     def out_copy(j):
-        row = (lax.axis_index("hid") // 4) ^ (base + j // 2)
+        row = (lax.axis_index("hid") // 4) ^ (j // 2)
         at = pl.ds(pl.multiple_of(row * wide + (j % 2) * half, half), half)
         return pltpu.make_async_copy(out_v.at[j], out_ref.at[:, at], out_sems.at[j])
 
@@ -451,15 +444,15 @@
     wait_each(steps, out_copy)
 
 
-def weight_grad(hid, x, name, base=0, rows=4, before=None):
-    all_rows, wide, live = x.shape
+def weight_grad(hid, x, name):
+    rows, wide, live = x.shape
     ff = hid.shape[-2]
     steps = 2 * rows
     return call(
-        functools.partial(weight_grad_kernel, base),
+        weight_grad_kernel,
         name,
-        (hid, x) if before is None else (hid, x, before),
-        [((ff, all_rows * wide), BF16)],
+        (hid, x),
+        [((ff, rows * wide), BF16)],
         [
             pltpu.VMEM((ff, live), BF16),
             pltpu.VMEM((rows, wide, live), BF16),
@@ -469,25 +462,29 @@
         ],
         2 * live * ff * rows * wide,
         2 * ff * rows * wide,
-        None if before is None else 2,
-        24 * 1024 * 1024,
+        vmem=24 * 1024 * 1024,
     )[0]
 
 
-def last_kernel(one_hot, *refs):
-    total = refs[0][...].astype(F32)
-    for part in refs[1:-1]:
-        total = total + part[...].astype(F32)
-    refs[-1][...] = dot(one_hot[...], total.astype(BF16), 0, 0).astype(BF16)
-
-
-def last_sum(one_hot, parts, name):
+def last_kernel(count, *refs):
+    one_hot = refs[0][...]
+    for i, out in enumerate(refs[-2:]):
+        parts = refs[1 + i * count : 1 + (i + 1) * count]
+        total = parts[0][...].astype(F32)
+        for part in parts[1:]:
+            total = total + part[...].astype(F32)
+        out[...] = dot(one_hot[: total.shape[0]], total.astype(BF16), 0, 0).astype(BF16)
+
+
+def last_sums(one_hot, first, second):
+    tok = one_hot.shape[1]
+    out = jax.ShapeDtypeStruct((tok, first[0].shape[1]), BF16)
     return pl.pallas_call(
-        last_kernel,
-        out_shape=jax.ShapeDtypeStruct((one_hot.shape[1], parts[0].shape[1]), BF16),
+        functools.partial(last_kernel, len(first)),
+        out_shape=[out, out],
         compiler_params=params(),
-        name=name,
-    )(one_hot, *parts)
+        name="last_sums",
+    )(one_hot, *first, *second)
 
 
 def flip(x, bits):
@@ -507,15 +504,16 @@
     live = tok // 2
     gate_w, up_w = gate_weight.T, up_weight.T
     one_hot, x, g = order_tokens(tokens, upstream, loss_mask)
-    z2, z1, y, gz1 = flip(x, 8), flip(x, 4), flip(x, 2), flip(g, 4)
-    gz1, y, z1, z2, g = join(gz1, y, z1, z2, g)
-    z3, yz1, yz2, gz2 = flip(z2, 4), flip(z1, 2), flip(z2, 2), flip(g, 8)
-    gz2, yz2, yz1, z3, g = join(gz2, yz2, yz1, z3, g)
+    z2, z1, y = flip(x, 8), flip(x, 4), flip(x, 2)
+    yz1 = flip(z1, 2)
+    yz1, y, z1, z2, g = join(yz1, y, z1, z2, g)
+    z3, yz2, gz2 = flip(z2, 4), flip(z2, 2), flip(g, 8)
+    gz2, yz2, z3, g = join(gz2, yz2, z3, g)
     yz3 = flip(z3, 2)
     most = jnp.stack([x, y, z1, yz1, z2, yz2, z3])
     most_other = flip(most, 1)
-    gz3 = flip(g, 12)
-    gz3, most_other, yz3 = join(gz3, most_other, yz3)
+    gz3, gz1 = flip(g, 12), flip(g, 4)
+    gz1, gz3, most_other, yz3 = join(gz1, gz3, most_other, yz3)
     g_even = jnp.stack([g, gz1, gz2, gz3])
     g_odd, g_even_other = flip(g_even, 2), flip(g_even, 1)
     x_mine, x_other = (most, yz3[None]), (most_other, flip(yz3, 1)[None])
@@ -527,30 +525,33 @@
     recv_odd, g_odd_other, send_even = join(recv_odd, g_odd_other, send_even)
     recv_even = flip(send_even, 1)
     out_y = flip(plus(keep_odd, recv_odd).astype(BF16), 2)
-    g_rows, d_gate_t, d_up_t, tk, ts = backward(
+    g_rows, d_gate_t, d_up_t, t_keep_even, t_keep_odd, t_send_even, t_send_odd = backward(
         (g_even, g_odd), (g_even_other, g_odd_other), act, slope, gate_w, up_w, down_weight
     )
-    ts, out_y, recv_even, hidden_t = join(ts, out_y, recv_even, hidden_t)
+    t_send_odd, out_y, recv_even = join(t_send_odd, out_y, recv_even)
+    t_recv_odd = flip(t_send_odd, 1)
     rows = [plus(keep_even[k], recv_even[k]) + out_y[k].astype(F32) for k in range(4)]
-    t_recv = flip(ts, 1)
     z13 = flip(rows[3].astype(BF16), 4)
+    t_recv_odd, t_send_even, hidden_t = join(t_recv_odd, t_send_even, hidden_t)
+    t_recv_even = flip(t_send_even, 1)
+    t_y23 = flip(plus(t_keep_odd[2:], t_recv_odd[2:]).astype(BF16), 2)
     down_grad = weight_grad(hidden_t, g_rows, "down_grad")
-    down_grad, z13, t_recv, d_gate_t = join(down_grad, z13, t_recv, d_gate_t)
+    down_grad, z13, t_y23, t_recv_odd, t_recv_even, d_gate_t = join(
+        down_grad, z13, t_y23, t_recv_odd, t_recv_even, d_gate_t
+    )
+    t_even = plus(t_keep_even, t_recv_even)
     z2 = flip((rows[2] + z13.astype(F32)).astype(BF16), 8)
     z1 = flip(rows[1].astype(BF16), 4)
-    t_y23 = flip(plus(tk[5::2], t_recv[5::2]).astype(BF16), 2)
+    t_y01 = flip(plus(t_keep_odd[:2], t_recv_odd[:2]).astype(BF16), 2)
+    tz13 = flip((t_even[3] + t_y23[1].astype(F32)).astype(BF16), 4)
     gate_grad = weight_grad(d_gate_t, x_rows, "gate_grad")
-    gate_grad, d_up_t, t_y23, t_recv = join(gate_grad, d_up_t, t_y23, t_recv)
-    tz13 = flip((plus(tk[6], t_recv[6]) + t_y23[1].astype(F32)).astype(BF16), 4)
-    t_y01 = flip(plus(tk[1:4:2], t_recv[1:4:2]).astype(BF16), 2)
-    up_grad = weight_grad(d_up_t, x_rows, "up_grad_0", 0, 2)
-    up_grad, tz13, t_y01, z2, z1 = join(up_grad, tz13, t_y01, z2, z1)
-    tz2 = flip((plus(tk[4], t_recv[4]) + plus(t_y23[0], tz13)).astype(BF16), 8)
-    tz1 = flip((plus(tk[2], t_recv[2]) + t_y01[1].astype(F32)).astype(BF16), 4)
-    ffn_output = last_sum(one_hot, (rows[0], z2, z1), "ffn_output")
-    up_grad = weight_grad(d_up_t, x_rows, "up_grad_1", 2, 2, up_grad)
+    gate_grad, d_up_t, tz13, t_y01, z2, z1 = join(gate_grad, d_up_t, tz13, t_y01, z2, z1)
+    tz1 = flip((t_even[1] + t_y01[1].astype(F32)).astype(BF16), 4)
+    tz2 = flip((t_even[2] + plus(t_y23[0], tz13)).astype(BF16), 8)
+    up_grad = weight_grad(d_up_t, x_rows, "up_grad")
     up_grad, tz2, tz1 = join(up_grad, tz2, tz1)
-    token_grad = last_sum(one_hot[:live], (plus(tk[0], t_recv[0]) + t_y01[0].astype(F32), tz2, tz1), "token_grad")
+    t_row = t_even[0] + t_y01[0].astype(F32)
+    ffn_output, token_grad = last_sums(one_hot, (rows[0], z2, z1), (t_row, tz2, tz1))
     return ffn_output, token_grad, gate_grad.T, up_grad.T, down_grad
 
 

time: 131 us -> 126 us (0.962)
  Pallas kernels: 76.3 us -> 72.1 us
  starting transfers between devices: 28.8 us -> 30.3 us
    pallas_call x7 -> x6, Pallas kernels: 74.5 us -> 71.1 us  [call(): pl.pallas_call(kernel, in_specs=[pl.BlockSpec(memory_space=pl.ANY)] * len...]
    ppermute x27 -> x28, starting transfers between devices: 28.8 us -> 30.3 us  [flip(): return lax.ppermute(x, 'hid', [(i, i ^ bits) for i in range(16)])]
    ppermute x27 -> x28, waiting for transfers between devices: 21.9 us -> 20.8 us  [flip(): return lax.ppermute(x, 'hid', [(i, i ^ bits) for i in range(16)])]
  transfers between devices with their start and end apart: 27 -> 28, of which waited for: 7 -> 7; matrix products, arithmetic and copies ran while one was open for 1% -> 1% of each run, Pallas kernels for 56% -> 55%
where the time goes in v4:
time: 126 us
  Pallas kernels  72.1 us (57%)
  starting transfers between devices  30.3 us (24%)
  waiting for transfers between devices  20.8 us (17%)
    pallas_call x6, Pallas kernels, call(): pl.pallas_call(kernel, in_specs=[pl.BlockSpec(memory_space=pl.ANY)] * len...  71.1 us
    ppermute x28, starting transfers between devices, flip(): return lax.ppermute(x, 'hid', [(i, i ^ bits) for i in range(16)])  30.3 us
    ppermute x28, waiting for transfers between devices, flip(): return lax.ppermute(x, 'hid', [(i, i ^ bits) for i in range(16)])  20.8 us
  transfers between devices with their start and end apart: 28, of which 7 were waited for; matrix products, arithmetic and copies ran while one was open for 1% of the time, Pallas kernels for 55%

profile of v4, /device:TPU:0, one launch (start us, length us, event | category | flops | bytes accessed | tf_op | source)
XLA Modules:
  0.0 125.9 jit_solution(16233207297173780205)
XLA Ops:
  0.6 2.2 %order_tokens.1 = (bf16[256,256]{1,0:T(8,128)(2,1)}, bf16[384,256]{1,0:T(8,128)(2,1)}, bf16[384,128]{1,0:T(8,128)(2,1)}) custom-call(s32[1,256]{1,0:T(1,128)} %bitcast.62, bf16[256,384]{1,0:T(8,128)(2,1)} %tokens_ref.1, bf16[256,384]{1,0:T(8,128)(2,1)} %upstream_ref.1), custom_call_target="tpu_custom_call" | custom-call | flops 75497472 | bytes 786432 | tf_op jit(solution)/shard_map/order_tokens/pallas_call | solution.py:33
  2.8 3.1 %collective-permute-start = (bf16[384,256]{1,0:T(8,128)(2,1)}, bf16[384,256]{1,0:T(8,128)(2,1)S(1)}, u32[]{:S(2)}, u32[]{:S(2)}) collective-permute-start(bf16[384,256]{1,0:T(8,128)(2,1)} %get-tuple-element.66), channel_id=1, source_target_pairs={{0,4},{1,5},{2,6},{3,7},{4,0},{5,1},{6,2},{7,3},{8,12},{9,13},{10,... | collective-permute-start | bytes 589832 | tf_op jit(solution)/shard_map/ppermute | solution.py:491
  5.9 2.6 %collective-permute-start.3 = (bf16[384,256]{1,0:T(8,128)(2,1)}, bf16[384,256]{1,0:T(8,128)(2,1)S(1)}, u32[]{:S(2)}, u32[]{:S(2)}) collective-permute-start(bf16[384,256]{1,0:T(8,128)(2,1)} %get-tuple-element.66), channel_id=1, source_target_pairs={{0,8},{1,9},{2,10},{3,11},{4,12},{5,13},{6,14},{7,15},{8,0},{9,1},... | collective-permute-start | bytes 589832 | tf_op jit(solution)/shard_map/ppermute | solution.py:491
  8.5 1.5 %collective-permute-start.2 = (bf16[384,256]{1,0:T(8,128)(2,1)}, bf16[384,256]{1,0:T(8,128)(2,1)S(1)}, u32[]{:S(2)}, u32[]{:S(2)}) collective-permute-start(bf16[384,256]{1,0:T(8,128)(2,1)} %get-tuple-element.66), channel_id=1, source_target_pairs={{0,2},{1,3},{2,0},{3,1},{4,6},{5,7},{6,4},{7,5},{8,10},{9,11},{10,... | collective-permute-start | bytes 589832 | tf_op jit(solution)/shard_map/ppermute | solution.py:491
  10.0 5.1 %collective-permute-done = bf16[384,256]{1,0:T(8,128)(2,1)S(1)} collective-permute-done((bf16[384,256]{1,0:T(8,128)(2,1)}, bf16[384,256]{1,0:T(8,128)(2,1)S(1)}, u32[]{:S(2)}, u32[]{:S(2)}) %collective-permute-start) | collective-permute-done | bytes 196640 | tf_op jit(solution)/shard_map/ppermute | solution.py:491
  15.1 1.7 %collective-permute-start.1 = (bf16[384,256]{1,0:T(8,128)(2,1)S(1)}, bf16[384,256]{1,0:T(8,128)(2,1)S(1)}, u32[]{:S(2)}, u32[]{:S(2)}) collective-permute-start(bf16[384,256]{1,0:T(8,128)(2,1)S(1)} %collective-permute-done), channel_id=1, source_target_pairs={{0,2},{1,3},{2,0},{3,1},{4,6},{5,7},{6,4},{7,5},{8,10},{9,11},{10,... | collective-permute-start | bytes 589832 | tf_op jit(solution)/shard_map/ppermute | solution.py:491
  17.7 3.1 %collective-permute-done.1 = bf16[384,256]{1,0:T(8,128)(2,1)S(1)} collective-permute-done((bf16[384,256]{1,0:T(8,128)(2,1)S(1)}, bf16[384,256]{1,0:T(8,128)(2,1)S(1)}, u32[]{:S(2)}, u32[]{:S(2)}) %collective-permute-start.1) | collective-permute-done | bytes 196640 | tf_op jit(solution)/shard_map/ppermute | solution.py:491
  20.9 1.6 %collective-permute-start.5 = (bf16[384,256]{1,0:T(8,128)(2,1)S(1)}, bf16[384,256]{1,0:T(8,128)(2,1)S(1)}, u32[]{:S(2)}, u32[]{:S(2)}) collective-permute-start(bf16[384,256]{1,0:T(8,128)(2,1)S(1)} %collective-permute-done.3), channel_id=1, source_target_pairs={{0,2},{1,3},{2,0},{3,1},{4,6},{5,7},{6,4},{7,5},{8,10},{9,11},{10,... | collective-permute-start | bytes 589832 | tf_op jit(solution)/shard_map/ppermute | solution.py:491
  22.5 3.2 %collective-permute-start.4 = (bf16[384,128]{1,0:T(8,128)(2,1)}, bf16[384,128]{1,0:T(8,128)(2,1)S(1)}, u32[]{:S(2)}, u32[]{:S(2)}) collective-permute-start(bf16[384,128]{1,0:T(8,128)(2,1)} %get-tuple-element.75), channel_id=1, source_target_pairs={{0,8},{1,9},{2,10},{3,11},{4,12},{5,13},{6,14},{7,15},{8,0},{9,1},... | collective-permute-start | bytes 294920 | tf_op jit(solution)/shard_map/ppermute | solution.py:491
  25.7 2.7 %collective-permute-done.4 = bf16[384,128]{1,0:T(8,128)(2,1)S(1)} collective-permute-done((bf16[384,128]{1,0:T(8,128)(2,1)}, bf16[384,128]{1,0:T(8,128)(2,1)S(1)}, u32[]{:S(2)}, u32[]{:S(2)}) %collective-permute-start.4) | collective-permute-done | bytes 98336 | tf_op jit(solution)/shard_map/ppermute | solution.py:491
  29.4 2.8 %collective-permute-start.8 = (bf16[384,128]{1,0:T(8,128)(2,1)S(1)}, bf16[384,128]{1,0:T(8,128)(2,1)S(1)}, u32[]{:S(2)}, u32[]{:S(2)}) collective-permute-start(bf16[384,128]{1,0:T(8,128)(2,1)S(1)} %copy-done.4), channel_id=1, source_target_pairs={{0,12},{1,13},{2,14},{3,15},{4,8},{5,9},{6,10},{7,11},{8,4},{9,5},... | collective-permute-start | bytes 294920 | tf_op jit(solution)/shard_map/ppermute | solution.py:491
  32.6 4.2 %collective-permute-done.8 = bf16[384,128]{1,0:T(8,128)(2,1)S(1)} collective-permute-done((bf16[384,128]{1,0:T(8,128)(2,1)S(1)}, bf16[384,128]{1,0:T(8,128)(2,1)S(1)}, u32[]{:S(2)}, u32[]{:S(2)}) %collective-permute-start.8) | collective-permute-done | bytes 98336 | tf_op jit(solution)/shard_map/ppermute | solution.py:491
  36.8 1.4 %collective-permute-done.7 = bf16[384,128]{1,0:T(8,128)(2,1)S(1)} collective-permute-done((bf16[384,128]{1,0:T(8,128)(2,1)S(1)}, bf16[384,128]{1,0:T(8,128)(2,1)S(1)}, u32[]{:S(2)}, u32[]{:S(2)}) %collective-permute-start.7) | collective-permute-done | bytes 98336 | tf_op jit(solution)/shard_map/ppermute | solution.py:491
  38.9 1.3 %collective-permute-start.12 = (bf16[4,384,128]{2,1,0:T(8,128)(2,1)S(1)}, bf16[4,384,128]{2,1,0:T(8,128)(2,1)S(1)}, u32[]{:S(2)}, u32[]{:S(2)}) collective-permute-start(bf16[4,384,128]{2,1,0:T(8,128)(2,1)S(1)} %pad_maximum_fusion.mine), channel_id=1, source_target_pairs={{0,2},{1,3},{2,0},{3,1},{4,6},{5,7},{6,4},{7,5},{8,10},{9,11},{10,... | collective-permute-start | bytes 1179656 | tf_op jit(solution)/shard_map/ppermute | solution.py:491
  40.2 22.6 %forward.1 = (bf16[4,1536,128]{2,1,0:T(8,128)(2,1)}, bf16[1472,128]{1,0:T(8,128)(2,1)S(1)}, f32[1472,128]{1,0:T(8,128)S(1)}, f32[1472,128]{1,0:T(8,128)S(1)}, f3...) custom-call(bf16[7,384,256]{2,1,0:T(8,128)(2,1)S(1)} %bitcast_dynami, ...), custom_call_target="tpu_custom_call" | custom-call | flops 13891534848 | bytes 54263808 | tf_op jit(solution)/shard_map/forward/pallas_call | solution.py:33
  63.5 2.3 %collective-permute-done.15.other_odd = bf16[4,384,128]{2,1,0:T(8,128)(2,1)S(1)} collective-permute-done((bf16[4,384,128]{2,1,0:T(8,128)(2,1)S(1)}, bf16[4,384,128]{2,1,0:T(8,128)(2,1)S(1)}, u32[]{:S(2)}, u32[]{:S(2)}) %collective-permute-start.15) | collective-permute-done | bytes 393248 | tf_op jit(solution)/shard_map/ppermute | solution.py:491
  66.9 20.9 %backward.1 = (bf16[4,1536,128]{2,1,0:T(8,128)(2,1)S(1)}, bf16[1472,128]{1,0:T(8,128)(2,1)S(1)}, bf16[1472,128]{1,0:T(8,128)(2,1)S(1)}, f32[4,128,384]{2,1,0:T(8...) custom-call(bf16[4,384,128]{2,1,0:T(8,128)(2,1)S(1)} %pad_maximum_fu, ...), custom_call_target="tpu_custom_call" | custom-call | flops 6945767424 | bytes 54263808 | tf_op jit(solution)/shard_map/backward/pallas_call | solution.py:33
  90.7 1.3 %collective-permute-start.20 = (bf16[2,128,384]{2,1,0:T(8,128)(2,1)S(1)}, bf16[2,128,384]{2,1,0:T(8,128)(2,1)S(1)}, u32[]{:S(2)}, u32[]{:S(2)}) collective-permute-start(bf16[2,128,384]{2,1,0:T(8,128)(2,1)S(1)} %add_convert_fusion.3), channel_id=1, source_target_pairs={{0,2},{1,3},{2,0},{3,1},{4,6},{5,7},{6,4},{7,5},{8,10},{9,11},{10,... | collective-permute-start | bytes 589832 | tf_op jit(solution)/shard_map/ppermute | solution.py:491
  92.0 8.5 %down_grad.1 = bf16[1472,6144]{1,0:T(8,128)(2,1)} custom-call(bf16[1472,128]{1,0:T(8,128)(2,1)S(1)} %get-tuple-element.99.hid_ref, bf16[4,1536,128]{2,1,0:T(8,128)(2,1)S(1)} %get-tuple-element.100.x_ref), custom_call_target="tpu_custom_call" | custom-call | flops 2315255808 | bytes 18087936 | tf_op jit(solution)/shard_map/down_grad/pallas_call | solution.py:33
  102.6 1.3 %collective-permute-start.24 = (bf16[256,384]{1,0:T(8,128)(2,1)S(1)}, bf16[256,384]{1,0:T(8,128)(2,1)S(1)}, u32[]{:S(2)}, u32[]{:S(2)}) collective-permute-start(bf16[256,384]{1,0:T(8,128)(2,1)S(1)} %fusion), channel_id=1, source_target_pairs={{0,8},{1,9},{2,10},{3,11},{4,12},{5,13},{6,14},{7,15},{8,0},{9,1},... | collective-permute-start | bytes 589832 | tf_op jit(solution)/shard_map/ppermute | solution.py:491
  103.8 8.5 %gate_grad.1 = bf16[1472,6144]{1,0:T(8,128)(2,1)} custom-call(bf16[1472,128]{1,0:T(8,128)(2,1)S(1)} %get-tuple-element.105.hid_ref, bf16[4,1536,128]{2,1,0:T(8,128)(2,1)S(1)} %copy-done), custom_call_target="tpu_custom_call" | custom-call | flops 2315255808 | bytes 18087936 | tf_op jit(solution)/shard_map/gate_grad/pallas_call | solution.py:33
  112.3 1.8 %collective-permute-done.24.refs_2_ = bf16[256,384]{1,0:T(8,128)(2,1)S(1)} collective-permute-done((bf16[256,384]{1,0:T(8,128)(2,1)S(1)}, bf16[256,384]{1,0:T(8,128)(2,1)S(1)}, u32[]{:S(2)}, u32[]{:S(2)}) %collective-permute-start.24) | collective-permute-done | bytes 196640 | tf_op jit(solution)/shard_map/ppermute | solution.py:491
  114.3 2.1 %collective-permute-start.26 = (bf16[128,384]{1,0:T(8,128)(2,1)S(1)}, bf16[128,384]{1,0:T(8,128)(2,1)S(1)}, u32[]{:S(2)}, u32[]{:S(2)}) collective-permute-start(bf16[128,384]{1,0:T(8,128)(2,1)S(1)} %fusion.5), channel_id=1, source_target_pairs={{0,8},{1,9},{2,10},{3,11},{4,12},{5,13},{6,14},{7,15},{8,0},{9,1},... | collective-permute-start | bytes 294920 | tf_op jit(solution)/shard_map/ppermute | solution.py:491
  116.4 8.5 %up_grad.1 = bf16[1472,6144]{1,0:T(8,128)(2,1)} custom-call(bf16[1472,128]{1,0:T(8,128)(2,1)S(1)} %get-tuple-element.116.hid_ref, bf16[4,1536,128]{2,1,0:T(8,128)(2,1)S(1)} %copy-done), custom_call_target="tpu_custom_call" | custom-call | flops 2315255808 | bytes 18087936 | tf_op jit(solution)/shard_map/up_grad/pallas_call | solution.py:33
  (66 shorter events, 10.8 us)
Async XLA Ops:
  2.8 12.3 %collective-permute-start = (bf16[384,256]{1,0:T(8,128)(2,1)}, bf16[384,256]{1,0:T(8,128)(2,1)S(1)}, u32[]{:S(2)}, u32[]{:S(2)}) collective-permute-start(bf16[384,256]{1,0:T(8,128)(2,1)} %get-tuple-element.66), channel_id=1, source_target_pairs={{0,4},{1,5},{2,6},{3,7},{4,0},{5,1},{6,2},{7,3},{8,12},{9,13},{10,... | collective-permute-start | bytes 589832 | tf_op jit(solution)/shard_map/ppermute | solution.py:491
  5.9 11.8 %collective-permute-start.3 = (bf16[384,256]{1,0:T(8,128)(2,1)}, bf16[384,256]{1,0:T(8,128)(2,1)S(1)}, u32[]{:S(2)}, u32[]{:S(2)}) collective-permute-start(bf16[384,256]{1,0:T(8,128)(2,1)} %get-tuple-element.66), channel_id=1, source_target_pairs={{0,8},{1,9},{2,10},{3,11},{4,12},{5,13},{6,14},{7,15},{8,0},{9,1},... | collective-permute-start | bytes 589832 | tf_op jit(solution)/shard_map/ppermute | solution.py:491
  8.5 9.2 %collective-permute-start.2 = (bf16[384,256]{1,0:T(8,128)(2,1)}, bf16[384,256]{1,0:T(8,128)(2,1)S(1)}, u32[]{:S(2)}, u32[]{:S(2)}) collective-permute-start(bf16[384,256]{1,0:T(8,128)(2,1)} %get-tuple-element.66), channel_id=1, source_target_pairs={{0,2},{1,3},{2,0},{3,1},{4,6},{5,7},{6,4},{7,5},{8,10},{9,11},{10,... | collective-permute-start | bytes 589832 | tf_op jit(solution)/shard_map/ppermute | solution.py:491
  15.1 5.8 %collective-permute-start.1 = (bf16[384,256]{1,0:T(8,128)(2,1)S(1)}, bf16[384,256]{1,0:T(8,128)(2,1)S(1)}, u32[]{:S(2)}, u32[]{:S(2)}) collective-permute-start(bf16[384,256]{1,0:T(8,128)(2,1)S(1)} %collective-permute-done), channel_id=1, source_target_pairs={{0,2},{1,3},{2,0},{3,1},{4,6},{5,7},{6,4},{7,5},{8,10},{9,11},{10,... | collective-permute-start | bytes 589832 | tf_op jit(solution)/shard_map/ppermute | solution.py:491
  20.9 7.5 %collective-permute-start.6 = (bf16[384,256]{1,0:T(8,128)(2,1)S(1)}, bf16[384,256]{1,0:T(8,128)(2,1)S(1)}, u32[]{:S(2)}, u32[]{:S(2)}) collective-permute-start(bf16[384,256]{1,0:T(8,128)(2,1)S(1)} %collective-permute-done.3), channel_id=1, source_target_pairs={{0,4},{1,5},{2,6},{3,7},{4,0},{5,1},{6,2},{7,3},{8,12},{9,13},{10,... | collective-permute-start | bytes 589832 | tf_op jit(solution)/shard_map/ppermute | solution.py:491
  20.9 7.5 %collective-permute-start.5 = (bf16[384,256]{1,0:T(8,128)(2,1)S(1)}, bf16[384,256]{1,0:T(8,128)(2,1)S(1)}, u32[]{:S(2)}, u32[]{:S(2)}) collective-permute-start(bf16[384,256]{1,0:T(8,128)(2,1)S(1)} %collective-permute-done.3), channel_id=1, source_target_pairs={{0,2},{1,3},{2,0},{3,1},{4,6},{5,7},{6,4},{7,5},{8,10},{9,11},{10,... | collective-permute-start | bytes 589832 | tf_op jit(solution)/shard_map/ppermute | solution.py:491
  22.5 6.0 %collective-permute-start.4 = (bf16[384,128]{1,0:T(8,128)(2,1)}, bf16[384,128]{1,0:T(8,128)(2,1)S(1)}, u32[]{:S(2)}, u32[]{:S(2)}) collective-permute-start(bf16[384,128]{1,0:T(8,128)(2,1)} %get-tuple-element.75), channel_id=1, source_target_pairs={{0,8},{1,9},{2,10},{3,11},{4,12},{5,13},{6,14},{7,15},{8,0},{9,1},... | collective-permute-start | bytes 294920 | tf_op jit(solution)/shard_map/ppermute | solution.py:491
  28.5 9.8 %collective-permute-start.9 = (bf16[7,384,256]{2,1,0:T(8,128)(2,1)S(1)}, bf16[7,384,256]{2,1,0:T(8,128)(2,1)S(1)}, u32[]{:S(2)}, u32[]{:S(2)}) collective-permute-start(bf16[7,384,256]{2,1,0:T(8,128)(2,1)S(1)} %bitcast_dynamic-update-slice_fusion.mine), channel_id=1, source_target_pairs={{0,1},{1,0},{2,3},{3,2},{4,5},{5,4},{6,7},{7,6},{8,9},{9,8},{10,11... | collective-permute-start | bytes 4128776 | tf_op jit(solution)/shard_map/ppermute | solution.py:491
  28.5 9.7 %collective-permute-start.10 = (bf16[384,256]{1,0:T(8,128)(2,1)S(1)}, bf16[384,256]{1,0:T(8,128)(2,1)S(1)}, u32[]{:S(2)}, u32[]{:S(2)}) collective-permute-start(bf16[384,256]{1,0:T(8,128)(2,1)S(1)} %collective-permute-done.6), channel_id=1, source_target_pairs={{0,2},{1,3},{2,0},{3,1},{4,6},{5,7},{6,4},{7,5},{8,10},{9,11},{10,... | collective-permute-start | bytes 589832 | tf_op jit(solution)/shard_map/ppermute | solution.py:491
  29.4 7.5 %collective-permute-start.8 = (bf16[384,128]{1,0:T(8,128)(2,1)S(1)}, bf16[384,128]{1,0:T(8,128)(2,1)S(1)}, u32[]{:S(2)}, u32[]{:S(2)}) collective-permute-start(bf16[384,128]{1,0:T(8,128)(2,1)S(1)} %copy-done.4), channel_id=1, source_target_pairs={{0,12},{1,13},{2,14},{3,15},{4,8},{5,9},{6,10},{7,11},{8,4},{9,5},... | collective-permute-start | bytes 294920 | tf_op jit(solution)/shard_map/ppermute | solution.py:491
  32.2 6.0 %collective-permute-start.7 = (bf16[384,128]{1,0:T(8,128)(2,1)S(1)}, bf16[384,128]{1,0:T(8,128)(2,1)S(1)}, u32[]{:S(2)}, u32[]{:S(2)}) collective-permute-start(bf16[384,128]{1,0:T(8,128)(2,1)S(1)} %copy-done.4), channel_id=1, source_target_pairs={{0,4},{1,5},{2,6},{3,7},{4,0},{5,1},{6,2},{7,3},{8,12},{9,13},{10,... | collective-permute-start | bytes 294920 | tf_op jit(solution)/shard_map/ppermute | solution.py:491
  38.4 24.5 %collective-permute-start.13 = (bf16[4,384,128]{2,1,0:T(8,128)(2,1)S(1)}, bf16[4,384,128]{2,1,0:T(8,128)(2,1)S(1)}, u32[]{:S(2)}, u32[]{:S(2)}) collective-permute-start(bf16[4,384,128]{2,1,0:T(8,128)(2,1)S(1)} %pad_maximum_fusion.mine), channel_id=1, source_target_pairs={{0,1},{1,0},{2,3},{3,2},{4,5},{5,4},{6,7},{7,6},{8,9},{9,8},{10,11... | collective-permute-start | bytes 1179656 | tf_op jit(solution)/shard_map/ppermute | solution.py:491
  38.9 23.9 %collective-permute-start.12 = (bf16[4,384,128]{2,1,0:T(8,128)(2,1)S(1)}, bf16[4,384,128]{2,1,0:T(8,128)(2,1)S(1)}, u32[]{:S(2)}, u32[]{:S(2)}) collective-permute-start(bf16[4,384,128]{2,1,0:T(8,128)(2,1)S(1)} %pad_maximum_fusion.mine), channel_id=1, source_target_pairs={{0,2},{1,3},{2,0},{3,1},{4,6},{5,7},{6,4},{7,5},{8,10},{9,11},{10,... | collective-permute-start | bytes 1179656 | tf_op jit(solution)/shard_map/ppermute | solution.py:491
  66.0 21.8 %collective-permute-start.16 = (bf16[4,256,384]{2,1,0:T(8,128)(2,1)S(1)}, bf16[4,256,384]{2,1,0:T(8,128)(2,1)S(1)}, u32[]{:S(2)}, u32[]{:S(2)}) collective-permute-start(bf16[4,256,384]{2,1,0:T(8,128)(2,1)S(1)} %add_convert_fusion), channel_id=1, source_target_pairs={{0,2},{1,3},{2,0},{3,1},{4,6},{5,7},{6,4},{7,5},{8,10},{9,11},{10,... | collective-permute-start | bytes 2359304 | tf_op jit(solution)/shard_map/ppermute | solution.py:491
  66.9 20.9 %collective-permute-start.17 = (bf16[4,256,384]{2,1,0:T(8,128)(2,1)S(1)}, bf16[4,256,384]{2,1,0:T(8,128)(2,1)S(1)}, u32[]{:S(2)}, u32[]{:S(2)}) collective-permute-start(bf16[4,256,384]{2,1,0:T(8,128)(2,1)S(1)} %get-tuple-element.93), channel_id=1, source_target_pairs={{0,1},{1,0},{2,3},{3,2},{4,5},{5,4},{6,7},{7,6},{8,9},{9,8},{10,11... | collective-permute-start | bytes 2359304 | tf_op jit(solution)/shard_map/ppermute | solution.py:491
  88.5 23.8 %collective-permute-start.25 = (bf16[256,384]{1,0:T(8,128)(2,1)S(1)}, bf16[256,384]{1,0:T(8,128)(2,1)S(1)}, u32[]{:S(2)}, u32[]{:S(2)}) collective-permute-start(bf16[256,384]{1,0:T(8,128)(2,1)S(1)} %get-tuple-element.125), channel_id=1, source_target_pairs={{0,4},{1,5},{2,6},{3,7},{4,0},{5,1},{6,2},{7,3},{8,12},{9,13},{10,... | collective-permute-start | bytes 589832 | tf_op jit(solution)/shard_map/ppermute | solution.py:491
  89.5 10.9 %collective-permute-start.19 = (bf16[256,384]{1,0:T(8,128)(2,1)S(1)}, bf16[256,384]{1,0:T(8,128)(2,1)S(1)}, u32[]{:S(2)}, u32[]{:S(2)}) collective-permute-start(bf16[256,384]{1,0:T(8,128)(2,1)S(1)} %get-tuple-element.126), channel_id=1, source_target_pairs={{0,4},{1,5},{2,6},{3,7},{4,0},{5,1},{6,2},{7,3},{8,12},{9,13},{10,... | collective-permute-start | bytes 589832 | tf_op jit(solution)/shard_map/ppermute | solution.py:491
  90.6 9.8 %collective-permute-start.21 = (bf16[4,128,384]{2,1,0:T(8,128)(2,1)S(1)}, bf16[4,128,384]{2,1,0:T(8,128)(2,1)S(1)}, u32[]{:S(2)}, u32[]{:S(2)}) collective-permute-start(bf16[4,128,384]{2,1,0:T(8,128)(2,1)S(1)} %get-tuple-element.103), channel_id=1, source_target_pairs={{0,1},{1,0},{2,3},{3,2},{4,5},{5,4},{6,7},{7,6},{8,9},{9,8},{10,11... | collective-permute-start | bytes 1179656 | tf_op jit(solution)/shard_map/ppermute | solution.py:491
  90.7 9.8 %collective-permute-start.20 = (bf16[2,128,384]{2,1,0:T(8,128)(2,1)S(1)}, bf16[2,128,384]{2,1,0:T(8,128)(2,1)S(1)}, u32[]{:S(2)}, u32[]{:S(2)}) collective-permute-start(bf16[2,128,384]{2,1,0:T(8,128)(2,1)S(1)} %add_convert_fusion.3), channel_id=1, source_target_pairs={{0,2},{1,3},{2,0},{3,1},{4,6},{5,7},{6,4},{7,5},{8,10},{9,11},{10,... | collective-permute-start | bytes 589832 | tf_op jit(solution)/shard_map/ppermute | solution.py:491
  100.8 11.5 %collective-permute-start.22 = (bf16[128,384]{1,0:T(8,128)(2,1)S(1)}, bf16[128,384]{1,0:T(8,128)(2,1)S(1)}, u32[]{:S(2)}, u32[]{:S(2)}) collective-permute-start(bf16[128,384]{1,0:T(8,128)(2,1)S(1)} %fusion.8), channel_id=1, source_target_pairs={{0,4},{1,5},{2,6},{3,7},{4,0},{5,1},{6,2},{7,3},{8,12},{9,13},{10,... | collective-permute-start | bytes 294920 | tf_op jit(solution)/shard_map/ppermute | solution.py:491
  101.3 11.0 %collective-permute-start.23 = (bf16[2,128,384]{2,1,0:T(8,128)(2,1)S(1)}, bf16[2,128,384]{2,1,0:T(8,128)(2,1)S(1)}, u32[]{:S(2)}, u32[]{:S(2)}) collective-permute-start(bf16[2,128,384]{2,1,0:T(8,128)(2,1)S(1)} %add_convert_fusion.2), channel_id=1, source_target_pairs={{0,2},{1,3},{2,0},{3,1},{4,6},{5,7},{6,4},{7,5},{8,10},{9,11},{10,... | collective-permute-start | bytes 589832 | tf_op jit(solution)/shard_map/ppermute | solution.py:491
  102.6 11.6 %collective-permute-start.24 = (bf16[256,384]{1,0:T(8,128)(2,1)S(1)}, bf16[256,384]{1,0:T(8,128)(2,1)S(1)}, u32[]{:S(2)}, u32[]{:S(2)}) collective-permute-start(bf16[256,384]{1,0:T(8,128)(2,1)S(1)} %fusion), channel_id=1, source_target_pairs={{0,8},{1,9},{2,10},{3,11},{4,12},{5,13},{6,14},{7,15},{8,0},{9,1},... | collective-permute-start | bytes 589832 | tf_op jit(solution)/shard_map/ppermute | solution.py:491
  114.2 10.7 %collective-permute-start.27 = (bf16[128,384]{1,0:T(8,128)(2,1)S(1)}, bf16[128,384]{1,0:T(8,128)(2,1)S(1)}, u32[]{:S(2)}, u32[]{:S(2)}) collective-permute-start(bf16[128,384]{1,0:T(8,128)(2,1)S(1)} %get-tuple-element.128), channel_id=1, source_target_pairs={{0,4},{1,5},{2,6},{3,7},{4,0},{5,1},{6,2},{7,3},{8,12},{9,13},{10,... | collective-permute-start | bytes 294920 | tf_op jit(solution)/shard_map/ppermute | solution.py:491
  114.3 10.6 %collective-permute-start.26 = (bf16[128,384]{1,0:T(8,128)(2,1)S(1)}, bf16[128,384]{1,0:T(8,128)(2,1)S(1)}, u32[]{:S(2)}, u32[]{:S(2)}) collective-permute-start(bf16[128,384]{1,0:T(8,128)(2,1)S(1)} %fusion.5), channel_id=1, source_target_pairs={{0,8},{1,9},{2,10},{3,11},{4,12},{5,13},{6,14},{7,15},{8,0},{9,1},... | collective-permute-start | bytes 294920 | tf_op jit(solution)/shard_map/ppermute | solution.py:491
  (9 other events, 74.6 us)

commit v5 on v4

--- a/solution.py
+++ b/solution.py
@@ -147,35 +147,17 @@
     return pl.ds(pl.multiple_of(row * wide, wide), wide)
 
 
-def row_copies(mine, other, dst):
-    rows, wide, _ = dst.shape
-    width = wide // 4
-    in_row = lax.axis_index("hid") % 4
+def place(side, flipped):
+    return (lax.axis_index("hid") % 4) ^ (2 * side + flipped)
+
+
+def part_copies(total, rounded, outs, sems):
+    width = total.shape[2] // 4
+    keep_even, keep_odd, send_even, send_odd = outs
     pairs = []
-    for chip in range(2 * rows):
-        for flipped, part in enumerate((mine, other)):
-            at = pl.ds(pl.multiple_of((in_row ^ (2 * (chip % 2) + flipped)) * width, width), width)
-            pairs.append((part[chip], dst.at[chip // 2, at]))
-    return pairs
-
-
-def with_last(most, last):
-    return [most.at[k] for k in range(most.shape[0])] + [last.at[0]]
-
-
-def even_odd(even, odd):
-    return [(even, odd)[k % 2].at[k // 2] for k in range(2 * even.shape[0])]
-
-
-def part_copies(j, total, rounded, outs, sems):
-    width = total.shape[2] // 4
-    in_row = lax.axis_index("hid") % 4
-    keep_even, keep_odd, send_even, send_odd = outs
-    made = []
     for i, (src, dst) in enumerate(((total, keep_even), (rounded, send_even), (rounded, keep_odd), (rounded, send_odd))):
-        at = pl.ds(pl.multiple_of((in_row ^ i) * width, width), width)
-        made.append(pltpu.make_async_copy(src.at[j, :, at], dst.at[j], sems.at[4 * j + i]))
-    return made
+        pairs.append((src.at[:, :, pl.ds(pl.multiple_of(place(i // 2, i % 2) * width, width), width)], dst))
+    return copies(sems, *pairs)
 
 
 def part_outs(rows, tok, width):
@@ -215,20 +197,27 @@
     def start_last(j):
         start_down(down_w, j, w.at[j % slots], w_sems.at[j % slots])
 
-    x_pairs = row_copies(with_last(mine, mine_last), with_last(other, other_last), x)
-    x_in = copies(x_sems, *x_pairs[:4])
+    most = mine.shape[0]
+    x_pairs = []
+    for at, pieces in ((pl.ds(0, most), (mine, other)), (pl.ds(most, rows - most), (mine_last, other_last))):
+        for side in range(2):
+            for flipped, part in enumerate(pieces):
+                x_pairs.append((part.at[:, side], x.at[at, place(side, flipped)]))
+    x_in = copies(x_sems, *x_pairs)
     start(0)
-    x_in += copies(x_sems.at[pl.ds(4, 4 * rows - 4)], *x_pairs[4:])
     start(1)
     acc[...] = jnp.zeros_like(acc)
 
     def one(j):
         slot = j % slots
-        for row in range(rows):
-
-            @pl.when(j == 2 * row)
-            def _():
-                wait_all(x_in[4 * row : 4 * row + 4])
+
+        @pl.when(j == 0)
+        def _():
+            wait_all(x_in[:4])
+
+        @pl.when(j == 2 * most)
+        def _():
+            wait_all(x_in[4:])
 
         wait_block(gate_w, w.at[slot], w_sems.at[slot])
 
@@ -240,11 +229,11 @@
         def _():
             start_last(j + 2 - steps)
 
-        acc[j % 2] += dot(w[slot], x[j // 2], 1, 0)
+        acc[j % 2] += dot(w[slot], x[j // 2].reshape(-1, x.shape[-1]), 1, 0)
 
     each(steps, one)
     live = act_v.shape[1]
-    out = copies(sems, (x.at[:, :, pl.ds(0, live)], x_ref))
+    out = copies(sems, (x.at[:, :, :, pl.ds(0, live)], x_ref))
     gate_lin = acc[0]
     up_lin = acc[1]
     sig = jax.nn.sigmoid(gate_lin)
@@ -267,17 +256,13 @@
         part = dot(hidden_v[...], w[slot], 1, 0)
         total[j] = part
         rounded[j] = part.astype(BF16)
-        for c in part_copies(j, total, rounded, parts, out_sems):
-            c.start()
 
     each(rows, two)
-    for j in range(rows):
-        wait_all(part_copies(j, total, rounded, parts, out_sems))
-    wait_all(out)
+    wait_all(out + part_copies(total, rounded, parts, out_sems))
 
 
 def forward(mine, other, gate_w, up_w, down_w, live):
-    _, width, tok = mine[0].shape
+    _, _, width, tok = mine[0].shape
     ff, features = gate_w.shape
     chips = features // (2 * width)
     rows, slots = chips // 2, 4
@@ -286,14 +271,14 @@
         "forward",
         (*mine, *other, gate_w, up_w, down_w),
         [
-            ((rows, 4 * width, live), BF16),
+            ((rows, 4, width, live), BF16),
             ((ff, live), BF16),
             ((ff, live), F32),
             ((ff, live), F32),
             *part_outs(rows, tok, width),
         ],
         [
-            pltpu.VMEM((rows, 4 * width, tok), BF16),
+            pltpu.VMEM((rows, 4, width, tok), BF16),
             pltpu.VMEM((slots, ff, 4 * width), BF16),
             pltpu.VMEM((2, ff, tok), F32),
             pltpu.VMEM((tok, ff), BF16),
@@ -330,7 +315,8 @@
         slot = j % slots
         start_gate_up(gate_w, up_w, 0, j, w.at[slot], w_sems.at[slot])
 
-    first = copies(g_sems, *row_copies(even_odd(mine, mine_odd), even_odd(other, other_odd), g))
+    stacks = (mine, other, mine_odd, other_odd)
+    first = copies(g_sems, *[(part, g.at[:, place(i // 2, i % 2)]) for i, part in enumerate(stacks)])
     start_first(0)
     start_first(1)
     late = copies(sems, (act_ref, act), (slope_ref, slope))
@@ -350,7 +336,7 @@
         def _():
             start(j + 2 - rows)
 
-        acc[...] += dot(w[slot], g[j], 1, 0)
+        acc[...] += dot(w[slot], g[j].reshape(-1, g.shape[-1]), 1, 0)
 
     each(rows, one)
     wait_all(late)
@@ -374,15 +360,8 @@
         total[j // 2] = part
         rounded[j // 2] = part.astype(BF16)
 
-        @pl.when(j % 2 == 1)
-        def _():
-            for c in part_copies(j // 2, total, rounded, parts, out_sems):
-                c.start()
-
     each(steps, two)
-    for j in range(rows):
-        wait_all(part_copies(j, total, rounded, parts, out_sems))
-    wait_all(out)
+    wait_all(out + part_copies(total, rounded, parts, out_sems))
 
 
 def backward(mine, other, act, slope, gate_w, up_w, down_w):
@@ -395,9 +374,9 @@
         backward_kernel,
         "backward",
         (*mine, *other, act, slope, gate_w, up_w, down_w),
-        [((rows, 4 * width, live), BF16), d_hid_t, d_hid_t, *part_outs(rows, live, width)],
+        [((rows, 4, width, live), BF16), d_hid_t, d_hid_t, *part_outs(rows, live, width)],
         [
-            pltpu.VMEM((rows, 4 * width, live), BF16),
+            pltpu.VMEM((rows, 4, width, live), BF16),
             pltpu.VMEM((ff, live), F32),
             pltpu.VMEM((ff, live), F32),
             pltpu.VMEM((slots, ff, 4 * width), BF16),
@@ -421,22 +400,16 @@
     steps = out_v.shape[0]
     rows, wide, _ = x.shape
     half = wide // 2
-    ready = copies(sems, (hid_ref, hid), *[(x_ref.at[row], x.at[row]) for row in range(rows)])
+    ready = copies(sems, (hid_ref, hid), (x_ref, x))
 
     def out_copy(j):
         row = (lax.axis_index("hid") // 4) ^ (j // 2)
         at = pl.ds(pl.multiple_of(row * wide + (j % 2) * half, half), half)
         return pltpu.make_async_copy(out_v.at[j], out_ref.at[:, at], out_sems.at[j])
 
-    ready[0].wait()
+    wait_all(ready)
 
     def step(j):
-        for row in range(rows):
-
-            @pl.when(j == 2 * row)
-            def _():
-                ready[1 + row].wait()
-
         out_v[j] = dot(hid[...], x[j // 2, pl.ds(pl.multiple_of((j % 2) * half, half), half), :], 1, 1).astype(BF16)
         out_copy(j).start()
 
@@ -457,7 +430,7 @@
             pltpu.VMEM((ff, live), BF16),
             pltpu.VMEM((rows, wide, live), BF16),
             pltpu.VMEM((steps, ff, wide // 2), BF16),
-            dma(1 + rows),
+            dma(2),
             dma(steps),
         ],
         2 * live * ff * rows * wide,
@@ -510,13 +483,14 @@
     z3, yz2, gz2 = flip(z2, 4), flip(z2, 2), flip(g, 8)
     gz2, yz2, z3, g = join(gz2, yz2, z3, g)
     yz3 = flip(z3, 2)
-    most = jnp.stack([x, y, z1, yz1, z2, yz2, z3])
+    most = jnp.stack([x, y, z1, yz1, z2, yz2]).reshape(3, 2, width, tok)
     most_other = flip(most, 1)
     gz3, gz1 = flip(g, 12), flip(g, 4)
     gz1, gz3, most_other, yz3 = join(gz1, gz3, most_other, yz3)
     g_even = jnp.stack([g, gz1, gz2, gz3])
     g_odd, g_even_other = flip(g_even, 2), flip(g_even, 1)
-    x_mine, x_other = (most, yz3[None]), (most_other, flip(yz3, 1)[None])
+    last = jnp.stack([z3, yz3]).reshape(1, 2, width, tok)
+    x_mine, x_other = (most, last), (most_other, flip(last, 1))
     x_rows, hidden_t, act, slope, keep_even, keep_odd, send_even, send_odd = forward(
         x_mine, x_other, gate_w, up_w, down_weight, live
     )
@@ -535,7 +509,7 @@
     t_recv_odd, t_send_even, hidden_t = join(t_recv_odd, t_send_even, hidden_t)
     t_recv_even = flip(t_send_even, 1)
     t_y23 = flip(plus(t_keep_odd[2:], t_recv_odd[2:]).astype(BF16), 2)
-    down_grad = weight_grad(hidden_t, g_rows, "down_grad")
+    down_grad = weight_grad(hidden_t, g_rows.reshape(4, 4 * width, live), "down_grad")
     down_grad, z13, t_y23, t_recv_odd, t_recv_even, d_gate_t = join(
         down_grad, z13, t_y23, t_recv_odd, t_recv_even, d_gate_t
     )
@@ -544,6 +518,7 @@
     z1 = flip(rows[1].astype(BF16), 4)
     t_y01 = flip(plus(t_keep_odd[:2], t_recv_odd[:2]).astype(BF16), 2)
     tz13 = flip((t_even[3] + t_y23[1].astype(F32)).astype(BF16), 4)
+    x_rows = x_rows.reshape(4, 4 * width, live)
     gate_grad = weight_grad(d_gate_t, x_rows, "gate_grad")
     gate_grad, d_up_t, tz13, t_y01, z2, z1 = join(gate_grad, d_up_t, tz13, t_y01, z2, z1)
     tz1 = flip((t_even[1] + t_y01[1].astype(F32)).astype(BF16), 4)

time: 126 us -> 124 us (0.984)
  Pallas kernels: 72.1 us -> 68.8 us
    pallas_call x6, Pallas kernels: 71.1 us -> 67.8 us  [call(): pl.pallas_call(kernel, in_specs=[pl.BlockSpec(memory_space=pl.ANY)] * len...]
  transfers between devices with their start and end apart: 28 -> 28, of which waited for: 7 -> 8; matrix products, arithmetic and copies ran while one was open for 1% -> 1% of each run, Pallas kernels for 55% -> 53%
where the time goes in v5:
time: 124 us
  Pallas kernels  68.8 us (55%)
  starting transfers between devices  30.7 us (25%)
  waiting for transfers between devices  21.3 us (17%)
    pallas_call x6, Pallas kernels, call(): pl.pallas_call(kernel, in_specs=[pl.BlockSpec(memory_space=pl.ANY)] * len...  67.8 us
    ppermute x28, starting transfers between devices, flip(): return lax.ppermute(x, 'hid', [(i, i ^ bits) for i in range(16)])  30.7 us
    ppermute x28, waiting for transfers between devices, flip(): return lax.ppermute(x, 'hid', [(i, i ^ bits) for i in range(16)])  21.3 us
  transfers between devices with their start and end apart: 28, of which 8 were waited for; matrix products, arithmetic and copies ran while one was open for 1% of the time, Pallas kernels for 53%

profile of v5, /device:TPU:0, one launch (start us, length us, event | category | flops | bytes accessed | tf_op | source)
XLA Modules:
  0.0 123.6 jit_solution(1150174075099798717)
XLA Ops:
  0.6 2.2 %order_tokens.1 = (bf16[256,256]{1,0:T(8,128)(2,1)}, bf16[384,256]{1,0:T(8,128)(2,1)}, bf16[384,128]{1,0:T(8,128)(2,1)}) custom-call(s32[1,256]{1,0:T(1,128)} %bitcast.70, bf16[256,384]{1,0:T(8,128)(2,1)} %tokens_ref.1, bf16[256,384]{1,0:T(8,128)(2,1)} %upstream_ref.1), custom_call_target="tpu_custom_call" | custom-call | flops 75497472 | bytes 786432 | tf_op jit(solution)/shard_map/order_tokens/pallas_call | solution.py:33
  2.8 3.1 %collective-permute-start = (bf16[384,256]{1,0:T(8,128)(2,1)}, bf16[384,256]{1,0:T(8,128)(2,1)S(1)}, u32[]{:S(2)}, u32[]{:S(2)}) collective-permute-start(bf16[384,256]{1,0:T(8,128)(2,1)} %get-tuple-element.66), channel_id=1, source_target_pairs={{0,4},{1,5},{2,6},{3,7},{4,0},{5,1},{6,2},{7,3},{8,12},{9,13},{10,... | collective-permute-start | bytes 589832 | tf_op jit(solution)/shard_map/ppermute | solution.py:464
  5.9 2.6 %collective-permute-start.3 = (bf16[384,256]{1,0:T(8,128)(2,1)}, bf16[384,256]{1,0:T(8,128)(2,1)S(1)}, u32[]{:S(2)}, u32[]{:S(2)}) collective-permute-start(bf16[384,256]{1,0:T(8,128)(2,1)} %get-tuple-element.66), channel_id=1, source_target_pairs={{0,8},{1,9},{2,10},{3,11},{4,12},{5,13},{6,14},{7,15},{8,0},{9,1},... | collective-permute-start | bytes 589832 | tf_op jit(solution)/shard_map/ppermute | solution.py:464
  8.5 1.5 %collective-permute-start.2 = (bf16[384,256]{1,0:T(8,128)(2,1)}, bf16[384,256]{1,0:T(8,128)(2,1)S(1)}, u32[]{:S(2)}, u32[]{:S(2)}) collective-permute-start(bf16[384,256]{1,0:T(8,128)(2,1)} %get-tuple-element.66), channel_id=1, source_target_pairs={{0,2},{1,3},{2,0},{3,1},{4,6},{5,7},{6,4},{7,5},{8,10},{9,11},{10,... | collective-permute-start | bytes 589832 | tf_op jit(solution)/shard_map/ppermute | solution.py:464
  10.0 5.1 %collective-permute-done = bf16[384,256]{1,0:T(8,128)(2,1)S(1)} collective-permute-done((bf16[384,256]{1,0:T(8,128)(2,1)}, bf16[384,256]{1,0:T(8,128)(2,1)S(1)}, u32[]{:S(2)}, u32[]{:S(2)}) %collective-permute-start) | collective-permute-done | bytes 196640 | tf_op jit(solution)/shard_map/ppermute | solution.py:464
  15.1 1.7 %collective-permute-start.1 = (bf16[384,256]{1,0:T(8,128)(2,1)S(1)}, bf16[384,256]{1,0:T(8,128)(2,1)S(1)}, u32[]{:S(2)}, u32[]{:S(2)}) collective-permute-start(bf16[384,256]{1,0:T(8,128)(2,1)S(1)} %collective-permute-done), channel_id=1, source_target_pairs={{0,2},{1,3},{2,0},{3,1},{4,6},{5,7},{6,4},{7,5},{8,10},{9,11},{10,... | collective-permute-start | bytes 589832 | tf_op jit(solution)/shard_map/ppermute | solution.py:464
  17.7 3.1 %collective-permute-done.1 = bf16[384,256]{1,0:T(8,128)(2,1)S(1)} collective-permute-done((bf16[384,256]{1,0:T(8,128)(2,1)S(1)}, bf16[384,256]{1,0:T(8,128)(2,1)S(1)}, u32[]{:S(2)}, u32[]{:S(2)}) %collective-permute-start.1) | collective-permute-done | bytes 196640 | tf_op jit(solution)/shard_map/ppermute | solution.py:464
  20.9 1.6 %collective-permute-start.5 = (bf16[384,256]{1,0:T(8,128)(2,1)S(1)}, bf16[384,256]{1,0:T(8,128)(2,1)S(1)}, u32[]{:S(2)}, u32[]{:S(2)}) collective-permute-start(bf16[384,256]{1,0:T(8,128)(2,1)S(1)} %collective-permute-done.3), channel_id=1, source_target_pairs={{0,2},{1,3},{2,0},{3,1},{4,6},{5,7},{6,4},{7,5},{8,10},{9,11},{10,... | collective-permute-start | bytes 589832 | tf_op jit(solution)/shard_map/ppermute | solution.py:464
  22.5 3.2 %collective-permute-start.4 = (bf16[384,128]{1,0:T(8,128)(2,1)}, bf16[384,128]{1,0:T(8,128)(2,1)S(1)}, u32[]{:S(2)}, u32[]{:S(2)}) collective-permute-start(bf16[384,128]{1,0:T(8,128)(2,1)} %get-tuple-element.75), channel_id=1, source_target_pairs={{0,8},{1,9},{2,10},{3,11},{4,12},{5,13},{6,14},{7,15},{8,0},{9,1},... | collective-permute-start | bytes 294920 | tf_op jit(solution)/shard_map/ppermute | solution.py:464
  25.7 2.7 %collective-permute-done.4 = bf16[384,128]{1,0:T(8,128)(2,1)S(1)} collective-permute-done((bf16[384,128]{1,0:T(8,128)(2,1)}, bf16[384,128]{1,0:T(8,128)(2,1)S(1)}, u32[]{:S(2)}, u32[]{:S(2)}) %collective-permute-start.4) | collective-permute-done | bytes 98336 | tf_op jit(solution)/shard_map/ppermute | solution.py:464
  29.3 2.8 %collective-permute-start.8 = (bf16[384,128]{1,0:T(8,128)(2,1)S(1)}, bf16[384,128]{1,0:T(8,128)(2,1)S(1)}, u32[]{:S(2)}, u32[]{:S(2)}) collective-permute-start(bf16[384,128]{1,0:T(8,128)(2,1)S(1)} %copy-done.4), channel_id=1, source_target_pairs={{0,12},{1,13},{2,14},{3,15},{4,8},{5,9},{6,10},{7,11},{8,4},{9,5},... | collective-permute-start | bytes 294920 | tf_op jit(solution)/shard_map/ppermute | solution.py:464
  32.6 4.2 %collective-permute-done.8 = bf16[384,128]{1,0:T(8,128)(2,1)S(1)} collective-permute-done((bf16[384,128]{1,0:T(8,128)(2,1)S(1)}, bf16[384,128]{1,0:T(8,128)(2,1)S(1)}, u32[]{:S(2)}, u32[]{:S(2)}) %collective-permute-start.8) | collective-permute-done | bytes 98336 | tf_op jit(solution)/shard_map/ppermute | solution.py:464
  36.8 1.4 %collective-permute-done.7 = bf16[384,128]{1,0:T(8,128)(2,1)S(1)} collective-permute-done((bf16[384,128]{1,0:T(8,128)(2,1)S(1)}, bf16[384,128]{1,0:T(8,128)(2,1)S(1)}, u32[]{:S(2)}, u32[]{:S(2)}) %collective-permute-start.7) | collective-permute-done | bytes 98336 | tf_op jit(solution)/shard_map/ppermute | solution.py:464
  39.0 1.3 %collective-permute-start.12 = (bf16[4,384,128]{2,1,0:T(8,128)(2,1)S(1)}, bf16[4,384,128]{2,1,0:T(8,128)(2,1)S(1)}, u32[]{:S(2)}, u32[]{:S(2)}) collective-permute-start(bf16[4,384,128]{2,1,0:T(8,128)(2,1)S(1)} %pad_maximum_fusion.mine), channel_id=1, source_target_pairs={{0,2},{1,3},{2,0},{3,1},{4,6},{5,7},{6,4},{7,5},{8,10},{9,11},{10,... | collective-permute-start | bytes 1179656 | tf_op jit(solution)/shard_map/ppermute | solution.py:464
  40.2 22.9 %forward.1 = (bf16[4,4,384,128]{3,2,1,0:T(8,128)(2,1)}, bf16[1472,128]{1,0:T(8,128)(2,1)S(1)}, f32[1472,128]{1,0:T(8,128)S(1)}, f32[1472,128]{1,0:T(8,128)S(1)},...) custom-call(bf16[3,2,384,256]{3,2,1,0:T(8,128)(2,1)S(1)} %bitcast.56, ...), custom_call_target="tpu_custom_call" | custom-call | flops 13891534848 | bytes 54263808 | tf_op jit(solution)/shard_map/forward/pallas_call | solution.py:33
  63.7 2.3 %collective-permute-done.15.other_odd = bf16[4,384,128]{2,1,0:T(8,128)(2,1)S(1)} collective-permute-done((bf16[4,384,128]{2,1,0:T(8,128)(2,1)S(1)}, bf16[4,384,128]{2,1,0:T(8,128)(2,1)S(1)}, u32[]{:S(2)}, u32[]{:S(2)}) %collective-permute-start.15) | collective-permute-done | bytes 393248 | tf_op jit(solution)/shard_map/ppermute | solution.py:464
  67.4 19.3 %backward.1 = (bf16[4,4,384,128]{3,2,1,0:T(8,128)(2,1)S(1)}, bf16[1472,128]{1,0:T(8,128)(2,1)S(1)}, bf16[1472,128]{1,0:T(8,128)(2,1)S(1)}, f32[4,128,384]{2,1,0:...) custom-call(bf16[4,384,128]{2,1,0:T(8,128)(2,1)S(1)} %pad_maximum_fu, ...), custom_call_target="tpu_custom_call" | custom-call | flops 6945767424 | bytes 54263808 | tf_op jit(solution)/shard_map/backward/pallas_call | solution.py:33
  88.3 1.4 %collective-permute-start.19 = (bf16[256,384]{1,0:T(8,128)(2,1)S(1)}, bf16[256,384]{1,0:T(8,128)(2,1)S(1)}, u32[]{:S(2)}, u32[]{:S(2)}) collective-permute-start(bf16[256,384]{1,0:T(8,128)(2,1)S(1)} %get-tuple-element.126), channel_id=1, source_target_pairs={{0,4},{1,5},{2,6},{3,7},{4,0},{5,1},{6,2},{7,3},{8,12},{9,13},{10,... | collective-permute-start | bytes 589832 | tf_op jit(solution)/shard_map/ppermute | solution.py:464
  90.7 7.8 %down_grad.1 = bf16[1472,6144]{1,0:T(8,128)(2,1)} custom-call(bf16[1472,128]{1,0:T(8,128)(2,1)S(1)} %get-tuple-element.99.hid_ref, bf16[4,1536,128]{2,1,0:T(8,128)(2,1)S(1)} %bitcast.57), custom_call_target="tpu_custom_call" | custom-call | flops 2315255808 | bytes 18087936 | tf_op jit(solution)/shard_map/down_grad/pallas_call | solution.py:33
  100.7 1.4 %collective-permute-start.24 = (bf16[256,384]{1,0:T(8,128)(2,1)S(1)}, bf16[256,384]{1,0:T(8,128)(2,1)S(1)}, u32[]{:S(2)}, u32[]{:S(2)}) collective-permute-start(bf16[256,384]{1,0:T(8,128)(2,1)S(1)} %fusion), channel_id=1, source_target_pairs={{0,8},{1,9},{2,10},{3,11},{4,12},{5,13},{6,14},{7,15},{8,0},{9,1},... | collective-permute-start | bytes 589832 | tf_op jit(solution)/shard_map/ppermute | solution.py:464
  102.2 7.8 %gate_grad.1 = bf16[1472,6144]{1,0:T(8,128)(2,1)} custom-call(bf16[1472,128]{1,0:T(8,128)(2,1)S(1)} %get-tuple-element.105.hid_ref, bf16[4,1536,128]{2,1,0:T(8,128)(2,1)S(1)} %bitcast.53), custom_call_target="tpu_custom_call" | custom-call | flops 2315255808 | bytes 18087936 | tf_op jit(solution)/shard_map/gate_grad/pallas_call | solution.py:33
  110.0 2.2 %collective-permute-done.24.refs_2_ = bf16[256,384]{1,0:T(8,128)(2,1)S(1)} collective-permute-done((bf16[256,384]{1,0:T(8,128)(2,1)S(1)}, bf16[256,384]{1,0:T(8,128)(2,1)S(1)}, u32[]{:S(2)}, u32[]{:S(2)}) %collective-permute-start.24) | collective-permute-done | bytes 196640 | tf_op jit(solution)/shard_map/ppermute | solution.py:464
  112.4 2.4 %collective-permute-start.26 = (bf16[128,384]{1,0:T(8,128)(2,1)S(1)}, bf16[128,384]{1,0:T(8,128)(2,1)S(1)}, u32[]{:S(2)}, u32[]{:S(2)}) collective-permute-start(bf16[128,384]{1,0:T(8,128)(2,1)S(1)} %fusion.5), channel_id=1, source_target_pairs={{0,8},{1,9},{2,10},{3,11},{4,12},{5,13},{6,14},{7,15},{8,0},{9,1},... | collective-permute-start | bytes 294920 | tf_op jit(solution)/shard_map/ppermute | solution.py:464
  114.8 7.8 %up_grad.1 = bf16[1472,6144]{1,0:T(8,128)(2,1)} custom-call(bf16[1472,128]{1,0:T(8,128)(2,1)S(1)} %get-tuple-element.116.hid_ref, bf16[4,1536,128]{2,1,0:T(8,128)(2,1)S(1)} %bitcast.54), custom_call_target="tpu_custom_call" | custom-call | flops 2315255808 | bytes 18087936 | tf_op jit(solution)/shard_map/up_grad/pallas_call | solution.py:33
  (66 shorter events, 10.8 us)
Async XLA Ops:
  2.8 12.3 %collective-permute-start = (bf16[384,256]{1,0:T(8,128)(2,1)}, bf16[384,256]{1,0:T(8,128)(2,1)S(1)}, u32[]{:S(2)}, u32[]{:S(2)}) collective-permute-start(bf16[384,256]{1,0:T(8,128)(2,1)} %get-tuple-element.66), channel_id=1, source_target_pairs={{0,4},{1,5},{2,6},{3,7},{4,0},{5,1},{6,2},{7,3},{8,12},{9,13},{10,... | collective-permute-start | bytes 589832 | tf_op jit(solution)/shard_map/ppermute | solution.py:464
  5.9 11.8 %collective-permute-start.3 = (bf16[384,256]{1,0:T(8,128)(2,1)}, bf16[384,256]{1,0:T(8,128)(2,1)S(1)}, u32[]{:S(2)}, u32[]{:S(2)}) collective-permute-start(bf16[384,256]{1,0:T(8,128)(2,1)} %get-tuple-element.66), channel_id=1, source_target_pairs={{0,8},{1,9},{2,10},{3,11},{4,12},{5,13},{6,14},{7,15},{8,0},{9,1},... | collective-permute-start | bytes 589832 | tf_op jit(solution)/shard_map/ppermute | solution.py:464
  8.5 9.2 %collective-permute-start.2 = (bf16[384,256]{1,0:T(8,128)(2,1)}, bf16[384,256]{1,0:T(8,128)(2,1)S(1)}, u32[]{:S(2)}, u32[]{:S(2)}) collective-permute-start(bf16[384,256]{1,0:T(8,128)(2,1)} %get-tuple-element.66), channel_id=1, source_target_pairs={{0,2},{1,3},{2,0},{3,1},{4,6},{5,7},{6,4},{7,5},{8,10},{9,11},{10,... | collective-permute-start | bytes 589832 | tf_op jit(solution)/shard_map/ppermute | solution.py:464
  15.1 5.8 %collective-permute-start.1 = (bf16[384,256]{1,0:T(8,128)(2,1)S(1)}, bf16[384,256]{1,0:T(8,128)(2,1)S(1)}, u32[]{:S(2)}, u32[]{:S(2)}) collective-permute-start(bf16[384,256]{1,0:T(8,128)(2,1)S(1)} %collective-permute-done), channel_id=1, source_target_pairs={{0,2},{1,3},{2,0},{3,1},{4,6},{5,7},{6,4},{7,5},{8,10},{9,11},{10,... | collective-permute-start | bytes 589832 | tf_op jit(solution)/shard_map/ppermute | solution.py:464
  20.9 7.5 %collective-permute-start.6 = (bf16[384,256]{1,0:T(8,128)(2,1)S(1)}, bf16[384,256]{1,0:T(8,128)(2,1)S(1)}, u32[]{:S(2)}, u32[]{:S(2)}) collective-permute-start(bf16[384,256]{1,0:T(8,128)(2,1)S(1)} %collective-permute-done.3), channel_id=1, source_target_pairs={{0,4},{1,5},{2,6},{3,7},{4,0},{5,1},{6,2},{7,3},{8,12},{9,13},{10,... | collective-permute-start | bytes 589832 | tf_op jit(solution)/shard_map/ppermute | solution.py:464
  20.9 7.5 %collective-permute-start.5 = (bf16[384,256]{1,0:T(8,128)(2,1)S(1)}, bf16[384,256]{1,0:T(8,128)(2,1)S(1)}, u32[]{:S(2)}, u32[]{:S(2)}) collective-permute-start(bf16[384,256]{1,0:T(8,128)(2,1)S(1)} %collective-permute-done.3), channel_id=1, source_target_pairs={{0,2},{1,3},{2,0},{3,1},{4,6},{5,7},{6,4},{7,5},{8,10},{9,11},{10,... | collective-permute-start | bytes 589832 | tf_op jit(solution)/shard_map/ppermute | solution.py:464
  22.5 6.0 %collective-permute-start.4 = (bf16[384,128]{1,0:T(8,128)(2,1)}, bf16[384,128]{1,0:T(8,128)(2,1)S(1)}, u32[]{:S(2)}, u32[]{:S(2)}) collective-permute-start(bf16[384,128]{1,0:T(8,128)(2,1)} %get-tuple-element.75), channel_id=1, source_target_pairs={{0,8},{1,9},{2,10},{3,11},{4,12},{5,13},{6,14},{7,15},{8,0},{9,1},... | collective-permute-start | bytes 294920 | tf_op jit(solution)/shard_map/ppermute | solution.py:464
  28.4 9.8 %collective-permute-start.9 = (bf16[3,2,384,256]{3,2,1,0:T(8,128)(2,1)S(1)}, bf16[3,2,384,256]{3,2,1,0:T(8,128)(2,1)S(1)}, u32[]{:S(2)}, u32[]{:S(2)}) collective-permute-start(bf16[3,2,384,256]{3,2,1,0:T(8,128)(2,1)S(1)} %bitcast.55), channel_id=1, source_target_pairs={{0,1},{1,0},{2,3},{3,2},{4,5},{5,4},{6,7},{7,6},{8,9},{9,8},{10,11... | collective-permute-start | bytes 3538952 | tf_op jit(solution)/shard_map/ppermute | solution.py:464
  28.5 9.7 %collective-permute-start.10 = (bf16[384,256]{1,0:T(8,128)(2,1)S(1)}, bf16[384,256]{1,0:T(8,128)(2,1)S(1)}, u32[]{:S(2)}, u32[]{:S(2)}) collective-permute-start(bf16[384,256]{1,0:T(8,128)(2,1)S(1)} %collective-permute-done.6), channel_id=1, source_target_pairs={{0,2},{1,3},{2,0},{3,1},{4,6},{5,7},{6,4},{7,5},{8,10},{9,11},{10,... | collective-permute-start | bytes 589832 | tf_op jit(solution)/shard_map/ppermute | solution.py:464
  29.3 7.5 %collective-permute-start.8 = (bf16[384,128]{1,0:T(8,128)(2,1)S(1)}, bf16[384,128]{1,0:T(8,128)(2,1)S(1)}, u32[]{:S(2)}, u32[]{:S(2)}) collective-permute-start(bf16[384,128]{1,0:T(8,128)(2,1)S(1)} %copy-done.4), channel_id=1, source_target_pairs={{0,12},{1,13},{2,14},{3,15},{4,8},{5,9},{6,10},{7,11},{8,4},{9,5},... | collective-permute-start | bytes 294920 | tf_op jit(solution)/shard_map/ppermute | solution.py:464
  32.2 6.0 %collective-permute-start.7 = (bf16[384,128]{1,0:T(8,128)(2,1)S(1)}, bf16[384,128]{1,0:T(8,128)(2,1)S(1)}, u32[]{:S(2)}, u32[]{:S(2)}) collective-permute-start(bf16[384,128]{1,0:T(8,128)(2,1)S(1)} %copy-done.4), channel_id=1, source_target_pairs={{0,4},{1,5},{2,6},{3,7},{4,0},{5,1},{6,2},{7,3},{8,12},{9,13},{10,... | collective-permute-start | bytes 294920 | tf_op jit(solution)/shard_map/ppermute | solution.py:464
  38.4 24.7 %collective-permute-start.13 = (bf16[4,384,128]{2,1,0:T(8,128)(2,1)S(1)}, bf16[4,384,128]{2,1,0:T(8,128)(2,1)S(1)}, u32[]{:S(2)}, u32[]{:S(2)}) collective-permute-start(bf16[4,384,128]{2,1,0:T(8,128)(2,1)S(1)} %pad_maximum_fusion.mine), channel_id=1, source_target_pairs={{0,1},{1,0},{2,3},{3,2},{4,5},{5,4},{6,7},{7,6},{8,9},{9,8},{10,11... | collective-permute-start | bytes 1179656 | tf_op jit(solution)/shard_map/ppermute | solution.py:464
  39.0 24.2 %collective-permute-start.12 = (bf16[4,384,128]{2,1,0:T(8,128)(2,1)S(1)}, bf16[4,384,128]{2,1,0:T(8,128)(2,1)S(1)}, u32[]{:S(2)}, u32[]{:S(2)}) collective-permute-start(bf16[4,384,128]{2,1,0:T(8,128)(2,1)S(1)} %pad_maximum_fusion.mine), channel_id=1, source_target_pairs={{0,2},{1,3},{2,0},{3,1},{4,6},{5,7},{6,4},{7,5},{8,10},{9,11},{10,... | collective-permute-start | bytes 1179656 | tf_op jit(solution)/shard_map/ppermute | solution.py:464
  66.3 20.5 %collective-permute-start.16 = (bf16[4,256,384]{2,1,0:T(8,128)(2,1)S(1)}, bf16[4,256,384]{2,1,0:T(8,128)(2,1)S(1)}, u32[]{:S(2)}, u32[]{:S(2)}) collective-permute-start(bf16[4,256,384]{2,1,0:T(8,128)(2,1)S(1)} %add_convert_fusion), channel_id=1, source_target_pairs={{0,2},{1,3},{2,0},{3,1},{4,6},{5,7},{6,4},{7,5},{8,10},{9,11},{10,... | collective-permute-start | bytes 2359304 | tf_op jit(solution)/shard_map/ppermute | solution.py:464
  67.4 19.4 %collective-permute-start.17 = (bf16[4,256,384]{2,1,0:T(8,128)(2,1)S(1)}, bf16[4,256,384]{2,1,0:T(8,128)(2,1)S(1)}, u32[]{:S(2)}, u32[]{:S(2)}) collective-permute-start(bf16[4,256,384]{2,1,0:T(8,128)(2,1)S(1)} %get-tuple-element.93), channel_id=1, source_target_pairs={{0,1},{1,0},{2,3},{3,2},{4,5},{5,4},{6,7},{7,6},{8,9},{9,8},{10,11... | collective-permute-start | bytes 2359304 | tf_op jit(solution)/shard_map/ppermute | solution.py:464
  87.6 22.4 %collective-permute-start.25 = (bf16[256,384]{1,0:T(8,128)(2,1)S(1)}, bf16[256,384]{1,0:T(8,128)(2,1)S(1)}, u32[]{:S(2)}, u32[]{:S(2)}) collective-permute-start(bf16[256,384]{1,0:T(8,128)(2,1)S(1)} %get-tuple-element.125), channel_id=1, source_target_pairs={{0,4},{1,5},{2,6},{3,7},{4,0},{5,1},{6,2},{7,3},{8,12},{9,13},{10,... | collective-permute-start | bytes 589832 | tf_op jit(solution)/shard_map/ppermute | solution.py:464
  88.3 10.4 %collective-permute-start.19 = (bf16[256,384]{1,0:T(8,128)(2,1)S(1)}, bf16[256,384]{1,0:T(8,128)(2,1)S(1)}, u32[]{:S(2)}, u32[]{:S(2)}) collective-permute-start(bf16[256,384]{1,0:T(8,128)(2,1)S(1)} %get-tuple-element.126), channel_id=1, source_target_pairs={{0,4},{1,5},{2,6},{3,7},{4,0},{5,1},{6,2},{7,3},{8,12},{9,13},{10,... | collective-permute-start | bytes 589832 | tf_op jit(solution)/shard_map/ppermute | solution.py:464
  89.7 9.0 %collective-permute-start.21 = (bf16[4,128,384]{2,1,0:T(8,128)(2,1)S(1)}, bf16[4,128,384]{2,1,0:T(8,128)(2,1)S(1)}, u32[]{:S(2)}, u32[]{:S(2)}) collective-permute-start(bf16[4,128,384]{2,1,0:T(8,128)(2,1)S(1)} %get-tuple-element.103), channel_id=1, source_target_pairs={{0,1},{1,0},{2,3},{3,2},{4,5},{5,4},{6,7},{7,6},{8,9},{9,8},{10,11... | collective-permute-start | bytes 1179656 | tf_op jit(solution)/shard_map/ppermute | solution.py:464
  89.7 8.9 %collective-permute-start.20 = (bf16[2,128,384]{2,1,0:T(8,128)(2,1)S(1)}, bf16[2,128,384]{2,1,0:T(8,128)(2,1)S(1)}, u32[]{:S(2)}, u32[]{:S(2)}) collective-permute-start(bf16[2,128,384]{2,1,0:T(8,128)(2,1)S(1)} %add_convert_fusion.3), channel_id=1, source_target_pairs={{0,2},{1,3},{2,0},{3,1},{4,6},{5,7},{6,4},{7,5},{8,10},{9,11},{10,... | collective-permute-start | bytes 589832 | tf_op jit(solution)/shard_map/ppermute | solution.py:464
  98.9 11.0 %collective-permute-start.22 = (bf16[128,384]{1,0:T(8,128)(2,1)S(1)}, bf16[128,384]{1,0:T(8,128)(2,1)S(1)}, u32[]{:S(2)}, u32[]{:S(2)}) collective-permute-start(bf16[128,384]{1,0:T(8,128)(2,1)S(1)} %fusion.8), channel_id=1, source_target_pairs={{0,4},{1,5},{2,6},{3,7},{4,0},{5,1},{6,2},{7,3},{8,12},{9,13},{10,... | collective-permute-start | bytes 294920 | tf_op jit(solution)/shard_map/ppermute | solution.py:464
  99.7 10.3 %collective-permute-start.23 = (bf16[2,128,384]{2,1,0:T(8,128)(2,1)S(1)}, bf16[2,128,384]{2,1,0:T(8,128)(2,1)S(1)}, u32[]{:S(2)}, u32[]{:S(2)}) collective-permute-start(bf16[2,128,384]{2,1,0:T(8,128)(2,1)S(1)} %add_convert_fusion.2), channel_id=1, source_target_pairs={{0,2},{1,3},{2,0},{3,1},{4,6},{5,7},{6,4},{7,5},{8,10},{9,11},{10,... | collective-permute-start | bytes 589832 | tf_op jit(solution)/shard_map/ppermute | solution.py:464
  100.7 11.4 %collective-permute-start.24 = (bf16[256,384]{1,0:T(8,128)(2,1)S(1)}, bf16[256,384]{1,0:T(8,128)(2,1)S(1)}, u32[]{:S(2)}, u32[]{:S(2)}) collective-permute-start(bf16[256,384]{1,0:T(8,128)(2,1)S(1)} %fusion), channel_id=1, source_target_pairs={{0,8},{1,9},{2,10},{3,11},{4,12},{5,13},{6,14},{7,15},{8,0},{9,1},... | collective-permute-start | bytes 589832 | tf_op jit(solution)/shard_map/ppermute | solution.py:464
  112.3 10.3 %collective-permute-start.27 = (bf16[128,384]{1,0:T(8,128)(2,1)S(1)}, bf16[128,384]{1,0:T(8,128)(2,1)S(1)}, u32[]{:S(2)}, u32[]{:S(2)}) collective-permute-start(bf16[128,384]{1,0:T(8,128)(2,1)S(1)} %get-tuple-element.128), channel_id=1, source_target_pairs={{0,4},{1,5},{2,6},{3,7},{4,0},{5,1},{6,2},{7,3},{8,12},{9,13},{10,... | collective-permute-start | bytes 294920 | tf_op jit(solution)/shard_map/ppermute | solution.py:464
  112.4 10.2 %collective-permute-start.26 = (bf16[128,384]{1,0:T(8,128)(2,1)S(1)}, bf16[128,384]{1,0:T(8,128)(2,1)S(1)}, u32[]{:S(2)}, u32[]{:S(2)}) collective-permute-start(bf16[128,384]{1,0:T(8,128)(2,1)S(1)} %fusion.5), channel_id=1, source_target_pairs={{0,8},{1,9},{2,10},{3,11},{4,12},{5,13},{6,14},{7,15},{8,0},{9,1},... | collective-permute-start | bytes 294920 | tf_op jit(solution)/shard_map/ppermute | solution.py:464
  (9 other events, 72.8 us)

commit v6 on v5

--- a/solution.py
+++ b/solution.py
@@ -478,15 +478,16 @@
     gate_w, up_w = gate_weight.T, up_weight.T
     one_hot, x, g = order_tokens(tokens, upstream, loss_mask)
     z2, z1, y = flip(x, 8), flip(x, 4), flip(x, 2)
+    z1, g = join(z1, g)
     yz1 = flip(z1, 2)
-    yz1, y, z1, z2, g = join(yz1, y, z1, z2, g)
-    z3, yz2, gz2 = flip(z2, 4), flip(z2, 2), flip(g, 8)
-    gz2, yz2, z3, g = join(gz2, yz2, z3, g)
+    y, z2, g = join(y, z2, g)
+    z3, yz2, gz2, gz1 = flip(z2, 4), flip(z2, 2), flip(g, 8), flip(g, 4)
+    gz1, gz2, yz1, yz2, z3, g = join(gz1, gz2, yz1, yz2, z3, g)
     yz3 = flip(z3, 2)
     most = jnp.stack([x, y, z1, yz1, z2, yz2]).reshape(3, 2, width, tok)
     most_other = flip(most, 1)
-    gz3, gz1 = flip(g, 12), flip(g, 4)
-    gz1, gz3, most_other, yz3 = join(gz1, gz3, most_other, yz3)
+    gz3 = flip(g, 12)
+    gz3, most_other, yz3 = join(gz3, most_other, yz3)
     g_even = jnp.stack([g, gz1, gz2, gz3])
     g_odd, g_even_other = flip(g_even, 2), flip(g_even, 1)
     last = jnp.stack([z3, yz3]).reshape(1, 2, width, tok)

time: 124 us -> 123 us (level)
  starting transfers between devices: 30.7 us -> 29 us
    ppermute x28, starting transfers between devices: 30.7 us -> 29 us  [flip(): return lax.ppermute(x, 'hid', [(i, i ^ bits) for i in range(16)])]
  transfers between devices with their start and end apart: 28 -> 28, of which waited for: 8 -> 9; matrix products, arithmetic and copies ran while one was open for 1% -> 1% of each run, Pallas kernels for 53% -> 53%
where the time goes in v6:
time: 123 us
  Pallas kernels  68.8 us (56%)
  starting transfers between devices  29 us (24%)
  waiting for transfers between devices  22.4 us (18%)
    pallas_call x6, Pallas kernels, call(): pl.pallas_call(kernel, in_specs=[pl.BlockSpec(memory_space=pl.ANY)] * len...  67.8 us
    ppermute x28, starting transfers between devices, flip(): return lax.ppermute(x, 'hid', [(i, i ^ bits) for i in range(16)])  29 us
    ppermute x28, waiting for transfers between devices, flip(): return lax.ppermute(x, 'hid', [(i, i ^ bits) for i in range(16)])  22.4 us
  transfers between devices with their start and end apart: 28, of which 9 were waited for; matrix products, arithmetic and copies ran while one was open for 1% of the time, Pallas kernels for 53%

profile of v6, /device:TPU:0, one launch (start us, length us, event | category | flops | bytes accessed | tf_op | source)
XLA Modules:
  0.0 123.0 jit_solution(4529759947247682327)
XLA Ops:
  0.6 2.2 %order_tokens.1 = (bf16[256,256]{1,0:T(8,128)(2,1)}, bf16[384,256]{1,0:T(8,128)(2,1)}, bf16[384,128]{1,0:T(8,128)(2,1)}) custom-call(s32[1,256]{1,0:T(1,128)} %bitcast.70, bf16[256,384]{1,0:T(8,128)(2,1)} %tokens_ref.1, bf16[256,384]{1,0:T(8,128)(2,1)} %upstream_ref.1), custom_call_target="tpu_custom_call" | custom-call | flops 75497472 | bytes 786432 | tf_op jit(solution)/shard_map/order_tokens/pallas_call | solution.py:33
  2.8 3.1 %collective-permute-start.2 = (bf16[384,256]{1,0:T(8,128)(2,1)}, bf16[384,256]{1,0:T(8,128)(2,1)S(1)}, u32[]{:S(2)}, u32[]{:S(2)}) collective-permute-start(bf16[384,256]{1,0:T(8,128)(2,1)} %get-tuple-element.67), channel_id=1, source_target_pairs={{0,4},{1,5},{2,6},{3,7},{4,0},{5,1},{6,2},{7,3},{8,12},{9,13},{10,... | collective-permute-start | bytes 589832 | tf_op jit(solution)/shard_map/ppermute | solution.py:464
  5.9 2.6 %collective-permute-start.1 = (bf16[384,256]{1,0:T(8,128)(2,1)}, bf16[384,256]{1,0:T(8,128)(2,1)S(1)}, u32[]{:S(2)}, u32[]{:S(2)}) collective-permute-start(bf16[384,256]{1,0:T(8,128)(2,1)} %get-tuple-element.67), channel_id=1, source_target_pairs={{0,8},{1,9},{2,10},{3,11},{4,12},{5,13},{6,14},{7,15},{8,0},{9,1},... | collective-permute-start | bytes 589832 | tf_op jit(solution)/shard_map/ppermute | solution.py:464
  8.5 1.5 %collective-permute-start = (bf16[384,256]{1,0:T(8,128)(2,1)}, bf16[384,256]{1,0:T(8,128)(2,1)S(1)}, u32[]{:S(2)}, u32[]{:S(2)}) collective-permute-start(bf16[384,256]{1,0:T(8,128)(2,1)} %get-tuple-element.67), channel_id=1, source_target_pairs={{0,2},{1,3},{2,0},{3,1},{4,6},{5,7},{6,4},{7,5},{8,10},{9,11},{10,... | collective-permute-start | bytes 589832 | tf_op jit(solution)/shard_map/ppermute | solution.py:464
  11.0 4.1 %collective-permute-done.2 = bf16[384,256]{1,0:T(8,128)(2,1)S(1)} collective-permute-done((bf16[384,256]{1,0:T(8,128)(2,1)}, bf16[384,256]{1,0:T(8,128)(2,1)S(1)}, u32[]{:S(2)}, u32[]{:S(2)}) %collective-permute-start.2) | collective-permute-done | bytes 196640 | tf_op jit(solution)/shard_map/ppermute | solution.py:464
  15.1 2.6 %collective-permute-done.1 = bf16[384,256]{1,0:T(8,128)(2,1)S(1)} collective-permute-done((bf16[384,256]{1,0:T(8,128)(2,1)}, bf16[384,256]{1,0:T(8,128)(2,1)S(1)}, u32[]{:S(2)}, u32[]{:S(2)}) %collective-permute-start.1) | collective-permute-done | bytes 196640 | tf_op jit(solution)/shard_map/ppermute | solution.py:464
  18.0 2.7 %collective-permute-start.3 = (bf16[384,128]{1,0:T(8,128)(2,1)}, bf16[384,128]{1,0:T(8,128)(2,1)S(1)}, u32[]{:S(2)}, u32[]{:S(2)}) collective-permute-start(bf16[384,128]{1,0:T(8,128)(2,1)} %get-tuple-element.77), channel_id=1, source_target_pairs={{0,4},{1,5},{2,6},{3,7},{4,0},{5,1},{6,2},{7,3},{8,12},{9,13},{10,... | collective-permute-start | bytes 294920 | tf_op jit(solution)/shard_map/ppermute | solution.py:464
  20.7 1.5 %collective-permute-start.6 = (bf16[384,256]{1,0:T(8,128)(2,1)S(1)}, bf16[384,256]{1,0:T(8,128)(2,1)S(1)}, u32[]{:S(2)}, u32[]{:S(2)}) collective-permute-start(bf16[384,256]{1,0:T(8,128)(2,1)S(1)} %collective-permute-done.1), channel_id=1, source_target_pairs={{0,2},{1,3},{2,0},{3,1},{4,6},{5,7},{6,4},{7,5},{8,10},{9,11},{10,... | collective-permute-start | bytes 589832 | tf_op jit(solution)/shard_map/ppermute | solution.py:464
  22.8 1.7 %collective-permute-done.4 = bf16[384,128]{1,0:T(8,128)(2,1)S(1)} collective-permute-done((bf16[384,128]{1,0:T(8,128)(2,1)}, bf16[384,128]{1,0:T(8,128)(2,1)S(1)}, u32[]{:S(2)}, u32[]{:S(2)}) %collective-permute-start.4) | collective-permute-done | bytes 98336 | tf_op jit(solution)/shard_map/ppermute | solution.py:464
  24.7 4.4 %collective-permute-done.5 = bf16[384,256]{1,0:T(8,128)(2,1)S(1)} collective-permute-done((bf16[384,256]{1,0:T(8,128)(2,1)S(1)}, bf16[384,256]{1,0:T(8,128)(2,1)S(1)}, u32[]{:S(2)}, u32[]{:S(2)}) %collective-permute-start.5) | collective-permute-done | bytes 196640 | tf_op jit(solution)/shard_map/ppermute | solution.py:464
  29.2 1.6 %collective-permute-start.10 = (bf16[384,256]{1,0:T(8,128)(2,1)S(1)}, bf16[384,256]{1,0:T(8,128)(2,1)S(1)}, u32[]{:S(2)}, u32[]{:S(2)}) collective-permute-start(bf16[384,256]{1,0:T(8,128)(2,1)S(1)} %collective-permute-done.7), channel_id=1, source_target_pairs={{0,2},{1,3},{2,0},{3,1},{4,6},{5,7},{6,4},{7,5},{8,10},{9,11},{10,... | collective-permute-start | bytes 589832 | tf_op jit(solution)/shard_map/ppermute | solution.py:464
  30.8 2.5 %collective-permute-start.8 = (bf16[384,128]{1,0:T(8,128)(2,1)S(1)}, bf16[384,128]{1,0:T(8,128)(2,1)S(1)}, u32[]{:S(2)}, u32[]{:S(2)}) collective-permute-start(bf16[384,128]{1,0:T(8,128)(2,1)S(1)} %copy-done.4), channel_id=1, source_target_pairs={{0,12},{1,13},{2,14},{3,15},{4,8},{5,9},{6,10},{7,11},{8,4},{9,5},... | collective-permute-start | bytes 294920 | tf_op jit(solution)/shard_map/ppermute | solution.py:464
  33.3 4.3 %collective-permute-done.8 = bf16[384,128]{1,0:T(8,128)(2,1)S(1)} collective-permute-done((bf16[384,128]{1,0:T(8,128)(2,1)S(1)}, bf16[384,128]{1,0:T(8,128)(2,1)S(1)}, u32[]{:S(2)}, u32[]{:S(2)}) %collective-permute-start.8) | collective-permute-done | bytes 98336 | tf_op jit(solution)/shard_map/ppermute | solution.py:464
  39.4 22.9 %forward.1 = (bf16[4,4,384,128]{3,2,1,0:T(8,128)(2,1)}, bf16[1472,128]{1,0:T(8,128)(2,1)S(1)}, f32[1472,128]{1,0:T(8,128)S(1)}, f32[1472,128]{1,0:T(8,128)S(1)},...) custom-call(bf16[3,2,384,256]{3,2,1,0:T(8,128)(2,1)S(1)} %bitcast.56, ...), custom_call_target="tpu_custom_call" | custom-call | flops 13891534848 | bytes 54263808 | tf_op jit(solution)/shard_map/forward/pallas_call | solution.py:33
  62.9 2.3 %collective-permute-done.15.other_odd = bf16[4,384,128]{2,1,0:T(8,128)(2,1)S(1)} collective-permute-done((bf16[4,384,128]{2,1,0:T(8,128)(2,1)S(1)}, bf16[4,384,128]{2,1,0:T(8,128)(2,1)S(1)}, u32[]{:S(2)}, u32[]{:S(2)}) %collective-permute-start.15) | collective-permute-done | bytes 393248 | tf_op jit(solution)/shard_map/ppermute | solution.py:464
  66.5 19.3 %backward.1 = (bf16[4,4,384,128]{3,2,1,0:T(8,128)(2,1)S(1)}, bf16[1472,128]{1,0:T(8,128)(2,1)S(1)}, bf16[1472,128]{1,0:T(8,128)(2,1)S(1)}, f32[4,128,384]{2,1,0:...) custom-call(bf16[4,384,128]{2,1,0:T(8,128)(2,1)S(1)} %pad_maximum_fu, ...), custom_call_target="tpu_custom_call" | custom-call | flops 6945767424 | bytes 54263808 | tf_op jit(solution)/shard_map/backward/pallas_call | solution.py:33
  86.6 1.7 %collective-permute-start.25 = (bf16[256,384]{1,0:T(8,128)(2,1)S(1)}, bf16[256,384]{1,0:T(8,128)(2,1)S(1)}, u32[]{:S(2)}, u32[]{:S(2)}) collective-permute-start(bf16[256,384]{1,0:T(8,128)(2,1)S(1)} %get-tuple-element.127), channel_id=1, source_target_pairs={{0,4},{1,5},{2,6},{3,7},{4,0},{5,1},{6,2},{7,3},{8,12},{9,13},{10,... | collective-permute-start | bytes 589832 | tf_op jit(solution)/shard_map/ppermute | solution.py:464
  89.9 7.8 %down_grad.1 = bf16[1472,6144]{1,0:T(8,128)(2,1)} custom-call(bf16[1472,128]{1,0:T(8,128)(2,1)S(1)} %get-tuple-element.101.hid_ref, bf16[4,1536,128]{2,1,0:T(8,128)(2,1)S(1)} %bitcast.57), custom_call_target="tpu_custom_call" | custom-call | flops 2315255808 | bytes 18087936 | tf_op jit(solution)/shard_map/down_grad/pallas_call | solution.py:33
  98.0 1.7 %collective-permute-start.22 = (bf16[128,384]{1,0:T(8,128)(2,1)S(1)}, bf16[128,384]{1,0:T(8,128)(2,1)S(1)}, u32[]{:S(2)}, u32[]{:S(2)}) collective-permute-start(bf16[128,384]{1,0:T(8,128)(2,1)S(1)} %fusion.8), channel_id=1, source_target_pairs={{0,4},{1,5},{2,6},{3,7},{4,0},{5,1},{6,2},{7,3},{8,12},{9,13},{10,... | collective-permute-start | bytes 294920 | tf_op jit(solution)/shard_map/ppermute | solution.py:464
  100.7 1.4 %collective-permute-start.24 = (bf16[256,384]{1,0:T(8,128)(2,1)S(1)}, bf16[256,384]{1,0:T(8,128)(2,1)S(1)}, u32[]{:S(2)}, u32[]{:S(2)}) collective-permute-start(bf16[256,384]{1,0:T(8,128)(2,1)S(1)} %fusion), channel_id=1, source_target_pairs={{0,8},{1,9},{2,10},{3,11},{4,12},{5,13},{6,14},{7,15},{8,0},{9,1},... | collective-permute-start | bytes 589832 | tf_op jit(solution)/shard_map/ppermute | solution.py:464
  102.1 7.8 %gate_grad.1 = bf16[1472,6144]{1,0:T(8,128)(2,1)} custom-call(bf16[1472,128]{1,0:T(8,128)(2,1)S(1)} %get-tuple-element.107.hid_ref, bf16[4,1536,128]{2,1,0:T(8,128)(2,1)S(1)} %bitcast.53), custom_call_target="tpu_custom_call" | custom-call | flops 2315255808 | bytes 18087936 | tf_op jit(solution)/shard_map/gate_grad/pallas_call | solution.py:33
  110.0 2.1 %collective-permute-done.24.refs_2_ = bf16[256,384]{1,0:T(8,128)(2,1)S(1)} collective-permute-done((bf16[256,384]{1,0:T(8,128)(2,1)S(1)}, bf16[256,384]{1,0:T(8,128)(2,1)S(1)}, u32[]{:S(2)}, u32[]{:S(2)}) %collective-permute-start.24) | collective-permute-done | bytes 196640 | tf_op jit(solution)/shard_map/ppermute | solution.py:464
  112.3 1.9 %collective-permute-start.26 = (bf16[128,384]{1,0:T(8,128)(2,1)S(1)}, bf16[128,384]{1,0:T(8,128)(2,1)S(1)}, u32[]{:S(2)}, u32[]{:S(2)}) collective-permute-start(bf16[128,384]{1,0:T(8,128)(2,1)S(1)} %fusion.5), channel_id=1, source_target_pairs={{0,8},{1,9},{2,10},{3,11},{4,12},{5,13},{6,14},{7,15},{8,0},{9,1},... | collective-permute-start | bytes 294920 | tf_op jit(solution)/shard_map/ppermute | solution.py:464
  114.2 7.8 %up_grad.1 = bf16[1472,6144]{1,0:T(8,128)(2,1)} custom-call(bf16[1472,128]{1,0:T(8,128)(2,1)S(1)} %get-tuple-element.118.hid_ref, bf16[4,1536,128]{2,1,0:T(8,128)(2,1)S(1)} %bitcast.54), custom_call_target="tpu_custom_call" | custom-call | flops 2315255808 | bytes 18087936 | tf_op jit(solution)/shard_map/up_grad/pallas_call | solution.py:33
  (66 shorter events, 10.6 us)
Async XLA Ops:
  2.8 12.3 %collective-permute-start.2 = (bf16[384,256]{1,0:T(8,128)(2,1)}, bf16[384,256]{1,0:T(8,128)(2,1)S(1)}, u32[]{:S(2)}, u32[]{:S(2)}) collective-permute-start(bf16[384,256]{1,0:T(8,128)(2,1)} %get-tuple-element.67), channel_id=1, source_target_pairs={{0,4},{1,5},{2,6},{3,7},{4,0},{5,1},{6,2},{7,3},{8,12},{9,13},{10,... | collective-permute-start | bytes 589832 | tf_op jit(solution)/shard_map/ppermute | solution.py:464
  5.9 11.7 %collective-permute-start.1 = (bf16[384,256]{1,0:T(8,128)(2,1)}, bf16[384,256]{1,0:T(8,128)(2,1)S(1)}, u32[]{:S(2)}, u32[]{:S(2)}) collective-permute-start(bf16[384,256]{1,0:T(8,128)(2,1)} %get-tuple-element.67), channel_id=1, source_target_pairs={{0,8},{1,9},{2,10},{3,11},{4,12},{5,13},{6,14},{7,15},{8,0},{9,1},... | collective-permute-start | bytes 589832 | tf_op jit(solution)/shard_map/ppermute | solution.py:464
  8.5 9.2 %collective-permute-start = (bf16[384,256]{1,0:T(8,128)(2,1)}, bf16[384,256]{1,0:T(8,128)(2,1)S(1)}, u32[]{:S(2)}, u32[]{:S(2)}) collective-permute-start(bf16[384,256]{1,0:T(8,128)(2,1)} %get-tuple-element.67), channel_id=1, source_target_pairs={{0,2},{1,3},{2,0},{3,1},{4,6},{5,7},{6,4},{7,5},{8,10},{9,11},{10,... | collective-permute-start | bytes 589832 | tf_op jit(solution)/shard_map/ppermute | solution.py:464
  17.7 6.8 %collective-permute-start.4 = (bf16[384,128]{1,0:T(8,128)(2,1)}, bf16[384,128]{1,0:T(8,128)(2,1)S(1)}, u32[]{:S(2)}, u32[]{:S(2)}) collective-permute-start(bf16[384,128]{1,0:T(8,128)(2,1)} %get-tuple-element.77), channel_id=1, source_target_pairs={{0,8},{1,9},{2,10},{3,11},{4,12},{5,13},{6,14},{7,15},{8,0},{9,1},... | collective-permute-start | bytes 294920 | tf_op jit(solution)/shard_map/ppermute | solution.py:464
  18.0 6.7 %collective-permute-start.3 = (bf16[384,128]{1,0:T(8,128)(2,1)}, bf16[384,128]{1,0:T(8,128)(2,1)S(1)}, u32[]{:S(2)}, u32[]{:S(2)}) collective-permute-start(bf16[384,128]{1,0:T(8,128)(2,1)} %get-tuple-element.77), channel_id=1, source_target_pairs={{0,4},{1,5},{2,6},{3,7},{4,0},{5,1},{6,2},{7,3},{8,12},{9,13},{10,... | collective-permute-start | bytes 294920 | tf_op jit(solution)/shard_map/ppermute | solution.py:464
  20.7 8.4 %collective-permute-start.7 = (bf16[384,256]{1,0:T(8,128)(2,1)S(1)}, bf16[384,256]{1,0:T(8,128)(2,1)S(1)}, u32[]{:S(2)}, u32[]{:S(2)}) collective-permute-start(bf16[384,256]{1,0:T(8,128)(2,1)S(1)} %collective-permute-done.1), channel_id=1, source_target_pairs={{0,4},{1,5},{2,6},{3,7},{4,0},{5,1},{6,2},{7,3},{8,12},{9,13},{10,... | collective-permute-start | bytes 589832 | tf_op jit(solution)/shard_map/ppermute | solution.py:464
  20.7 8.4 %collective-permute-start.6 = (bf16[384,256]{1,0:T(8,128)(2,1)S(1)}, bf16[384,256]{1,0:T(8,128)(2,1)S(1)}, u32[]{:S(2)}, u32[]{:S(2)}) collective-permute-start(bf16[384,256]{1,0:T(8,128)(2,1)S(1)} %collective-permute-done.1), channel_id=1, source_target_pairs={{0,2},{1,3},{2,0},{3,1},{4,6},{5,7},{6,4},{7,5},{8,10},{9,11},{10,... | collective-permute-start | bytes 589832 | tf_op jit(solution)/shard_map/ppermute | solution.py:464
  22.2 6.9 %collective-permute-start.5 = (bf16[384,256]{1,0:T(8,128)(2,1)S(1)}, bf16[384,256]{1,0:T(8,128)(2,1)S(1)}, u32[]{:S(2)}, u32[]{:S(2)}) collective-permute-start(bf16[384,256]{1,0:T(8,128)(2,1)S(1)} %collective-permute-done.2), channel_id=1, source_target_pairs={{0,2},{1,3},{2,0},{3,1},{4,6},{5,7},{6,4},{7,5},{8,10},{9,11},{10,... | collective-permute-start | bytes 589832 | tf_op jit(solution)/shard_map/ppermute | solution.py:464
  29.2 8.4 %collective-permute-start.9 = (bf16[3,2,384,256]{3,2,1,0:T(8,128)(2,1)S(1)}, bf16[3,2,384,256]{3,2,1,0:T(8,128)(2,1)S(1)}, u32[]{:S(2)}, u32[]{:S(2)}) collective-permute-start(bf16[3,2,384,256]{3,2,1,0:T(8,128)(2,1)S(1)} %bitcast.55), channel_id=1, source_target_pairs={{0,1},{1,0},{2,3},{3,2},{4,5},{5,4},{6,7},{7,6},{8,9},{9,8},{10,11... | collective-permute-start | bytes 3538952 | tf_op jit(solution)/shard_map/ppermute | solution.py:464
  29.2 8.4 %collective-permute-start.10 = (bf16[384,256]{1,0:T(8,128)(2,1)S(1)}, bf16[384,256]{1,0:T(8,128)(2,1)S(1)}, u32[]{:S(2)}, u32[]{:S(2)}) collective-permute-start(bf16[384,256]{1,0:T(8,128)(2,1)S(1)} %collective-permute-done.7), channel_id=1, source_target_pairs={{0,2},{1,3},{2,0},{3,1},{4,6},{5,7},{6,4},{7,5},{8,10},{9,11},{10,... | collective-permute-start | bytes 589832 | tf_op jit(solution)/shard_map/ppermute | solution.py:464
  30.8 6.8 %collective-permute-start.8 = (bf16[384,128]{1,0:T(8,128)(2,1)S(1)}, bf16[384,128]{1,0:T(8,128)(2,1)S(1)}, u32[]{:S(2)}, u32[]{:S(2)}) collective-permute-start(bf16[384,128]{1,0:T(8,128)(2,1)S(1)} %copy-done.4), channel_id=1, source_target_pairs={{0,12},{1,13},{2,14},{3,15},{4,8},{5,9},{6,10},{7,11},{8,4},{9,5},... | collective-permute-start | bytes 294920 | tf_op jit(solution)/shard_map/ppermute | solution.py:464
  37.8 24.5 %collective-permute-start.13 = (bf16[4,384,128]{2,1,0:T(8,128)(2,1)S(1)}, bf16[4,384,128]{2,1,0:T(8,128)(2,1)S(1)}, u32[]{:S(2)}, u32[]{:S(2)}) collective-permute-start(bf16[4,384,128]{2,1,0:T(8,128)(2,1)S(1)} %pad_maximum_fusion.mine), channel_id=1, source_target_pairs={{0,1},{1,0},{2,3},{3,2},{4,5},{5,4},{6,7},{7,6},{8,9},{9,8},{10,11... | collective-permute-start | bytes 1179656 | tf_op jit(solution)/shard_map/ppermute | solution.py:464
  38.3 24.0 %collective-permute-start.12 = (bf16[4,384,128]{2,1,0:T(8,128)(2,1)S(1)}, bf16[4,384,128]{2,1,0:T(8,128)(2,1)S(1)}, u32[]{:S(2)}, u32[]{:S(2)}) collective-permute-start(bf16[4,384,128]{2,1,0:T(8,128)(2,1)S(1)} %pad_maximum_fusion.mine), channel_id=1, source_target_pairs={{0,2},{1,3},{2,0},{3,1},{4,6},{5,7},{6,4},{7,5},{8,10},{9,11},{10,... | collective-permute-start | bytes 1179656 | tf_op jit(solution)/shard_map/ppermute | solution.py:464
  65.5 20.4 %collective-permute-start.16 = (bf16[4,256,384]{2,1,0:T(8,128)(2,1)S(1)}, bf16[4,256,384]{2,1,0:T(8,128)(2,1)S(1)}, u32[]{:S(2)}, u32[]{:S(2)}) collective-permute-start(bf16[4,256,384]{2,1,0:T(8,128)(2,1)S(1)} %add_convert_fusion), channel_id=1, source_target_pairs={{0,2},{1,3},{2,0},{3,1},{4,6},{5,7},{6,4},{7,5},{8,10},{9,11},{10,... | collective-permute-start | bytes 2359304 | tf_op jit(solution)/shard_map/ppermute | solution.py:464
  66.5 19.4 %collective-permute-start.17 = (bf16[4,256,384]{2,1,0:T(8,128)(2,1)S(1)}, bf16[4,256,384]{2,1,0:T(8,128)(2,1)S(1)}, u32[]{:S(2)}, u32[]{:S(2)}) collective-permute-start(bf16[4,256,384]{2,1,0:T(8,128)(2,1)S(1)} %get-tuple-element.95), channel_id=1, source_target_pairs={{0,1},{1,0},{2,3},{3,2},{4,5},{5,4},{6,7},{7,6},{8,9},{9,8},{10,11... | collective-permute-start | bytes 2359304 | tf_op jit(solution)/shard_map/ppermute | solution.py:464
  86.6 23.3 %collective-permute-start.25 = (bf16[256,384]{1,0:T(8,128)(2,1)S(1)}, bf16[256,384]{1,0:T(8,128)(2,1)S(1)}, u32[]{:S(2)}, u32[]{:S(2)}) collective-permute-start(bf16[256,384]{1,0:T(8,128)(2,1)S(1)} %get-tuple-element.127), channel_id=1, source_target_pairs={{0,4},{1,5},{2,6},{3,7},{4,0},{5,1},{6,2},{7,3},{8,12},{9,13},{10,... | collective-permute-start | bytes 589832 | tf_op jit(solution)/shard_map/ppermute | solution.py:464
  88.3 9.5 %collective-permute-start.19 = (bf16[256,384]{1,0:T(8,128)(2,1)S(1)}, bf16[256,384]{1,0:T(8,128)(2,1)S(1)}, u32[]{:S(2)}, u32[]{:S(2)}) collective-permute-start(bf16[256,384]{1,0:T(8,128)(2,1)S(1)} %get-tuple-element.128), channel_id=1, source_target_pairs={{0,4},{1,5},{2,6},{3,7},{4,0},{5,1},{6,2},{7,3},{8,12},{9,13},{10,... | collective-permute-start | bytes 589832 | tf_op jit(solution)/shard_map/ppermute | solution.py:464
  88.7 9.0 %collective-permute-start.21 = (bf16[4,128,384]{2,1,0:T(8,128)(2,1)S(1)}, bf16[4,128,384]{2,1,0:T(8,128)(2,1)S(1)}, u32[]{:S(2)}, u32[]{:S(2)}) collective-permute-start(bf16[4,128,384]{2,1,0:T(8,128)(2,1)S(1)} %get-tuple-element.105), channel_id=1, source_target_pairs={{0,1},{1,0},{2,3},{3,2},{4,5},{5,4},{6,7},{7,6},{8,9},{9,8},{10,11... | collective-permute-start | bytes 1179656 | tf_op jit(solution)/shard_map/ppermute | solution.py:464
  88.7 9.0 %collective-permute-start.20 = (bf16[2,128,384]{2,1,0:T(8,128)(2,1)S(1)}, bf16[2,128,384]{2,1,0:T(8,128)(2,1)S(1)}, u32[]{:S(2)}, u32[]{:S(2)}) collective-permute-start(bf16[2,128,384]{2,1,0:T(8,128)(2,1)S(1)} %add_convert_fusion.3), channel_id=1, source_target_pairs={{0,2},{1,3},{2,0},{3,1},{4,6},{5,7},{6,4},{7,5},{8,10},{9,11},{10,... | collective-permute-start | bytes 589832 | tf_op jit(solution)/shard_map/ppermute | solution.py:464
  98.0 11.9 %collective-permute-start.22 = (bf16[128,384]{1,0:T(8,128)(2,1)S(1)}, bf16[128,384]{1,0:T(8,128)(2,1)S(1)}, u32[]{:S(2)}, u32[]{:S(2)}) collective-permute-start(bf16[128,384]{1,0:T(8,128)(2,1)S(1)} %fusion.8), channel_id=1, source_target_pairs={{0,4},{1,5},{2,6},{3,7},{4,0},{5,1},{6,2},{7,3},{8,12},{9,13},{10,... | collective-permute-start | bytes 294920 | tf_op jit(solution)/shard_map/ppermute | solution.py:464
  99.7 10.3 %collective-permute-start.23 = (bf16[2,128,384]{2,1,0:T(8,128)(2,1)S(1)}, bf16[2,128,384]{2,1,0:T(8,128)(2,1)S(1)}, u32[]{:S(2)}, u32[]{:S(2)}) collective-permute-start(bf16[2,128,384]{2,1,0:T(8,128)(2,1)S(1)} %add_convert_fusion.2), channel_id=1, source_target_pairs={{0,2},{1,3},{2,0},{3,1},{4,6},{5,7},{6,4},{7,5},{8,10},{9,11},{10,... | collective-permute-start | bytes 589832 | tf_op jit(solution)/shard_map/ppermute | solution.py:464
  100.7 11.4 %collective-permute-start.24 = (bf16[256,384]{1,0:T(8,128)(2,1)S(1)}, bf16[256,384]{1,0:T(8,128)(2,1)S(1)}, u32[]{:S(2)}, u32[]{:S(2)}) collective-permute-start(bf16[256,384]{1,0:T(8,128)(2,1)S(1)} %fusion), channel_id=1, source_target_pairs={{0,8},{1,9},{2,10},{3,11},{4,12},{5,13},{6,14},{7,15},{8,0},{9,1},... | collective-permute-start | bytes 589832 | tf_op jit(solution)/shard_map/ppermute | solution.py:464
  112.2 9.8 %collective-permute-start.27 = (bf16[128,384]{1,0:T(8,128)(2,1)S(1)}, bf16[128,384]{1,0:T(8,128)(2,1)S(1)}, u32[]{:S(2)}, u32[]{:S(2)}) collective-permute-start(bf16[128,384]{1,0:T(8,128)(2,1)S(1)} %get-tuple-element.130), channel_id=1, source_target_pairs={{0,4},{1,5},{2,6},{3,7},{4,0},{5,1},{6,2},{7,3},{8,12},{9,13},{10,... | collective-permute-start | bytes 294920 | tf_op jit(solution)/shard_map/ppermute | solution.py:464
  112.3 9.7 %collective-permute-start.26 = (bf16[128,384]{1,0:T(8,128)(2,1)S(1)}, bf16[128,384]{1,0:T(8,128)(2,1)S(1)}, u32[]{:S(2)}, u32[]{:S(2)}) collective-permute-start(bf16[128,384]{1,0:T(8,128)(2,1)S(1)} %fusion.5), channel_id=1, source_target_pairs={{0,8},{1,9},{2,10},{3,11},{4,12},{5,13},{6,14},{7,15},{8,0},{9,1},... | collective-permute-start | bytes 294920 | tf_op jit(solution)/shard_map/ppermute | solution.py:464
  (9 other events, 74.1 us)
